TPU v7x, 128 devices: a whole 4x4x4 slice. The times are simulated.
128 devices in a mesh: dp: 32 (over z, y, core), proto: 4 (over x).
Axes of the slice: x: 4, y: 4, z: 4, core: 2. Of those that a mesh axis runs over, the one named last changes fastest.
Arguments:
- teacher_feat: bfloat16 [65536, 256], P('dp'), may hold values from -100 to 100
- student_feat: bfloat16 [65536, 256], P('dp'), may hold values from -100 to 100
- teacher_proto: bfloat16 [256, 65536], P('dp', 'proto'), may hold values from -1.6 to 1.6
- student_proto: bfloat16 [256, 65536], P('dp', 'proto'), may hold values from -1.6 to 1.6
- mask_index: int32 [12288], P('dp'), may hold values from 0 to 2047, as said below
- mask_count: int32 [32], P('dp'), may hold values from 192 to 384, as said below
Outputs:
- token_loss: float32 [12288], P('dp')
- proto_grad: float32 [256, 65536], P('dp', 'proto')
Inputs may be any that keep to these rules, and one draw needn't show every extreme that they name: `mask_index`: within one index of dp the 384 slots name distinct patch tokens of its 2048; slots at or past its count hold indices too and are ignored. `mask_count`: some index of dp has all 384 slots live in every draw.
All inputs are finite; a program needn't handle non-finite values.
Results may differ from a plain program's by a relative error of at most 0.003.
Values may be sent and summed in bfloat16 or wider, within the bound.
No kernel may reach another device: no remote copies, remote signals or barrier semaphores. Data moves between devices by JAX's collectives and lax.ppermute only.
A program may use at most 192 MiB of HBM per device.

v0:
```python
import jax
import jax.numpy as jnp
from jax import lax
from jax.sharding import PartitionSpec as P

PATCH = 256
SWEEPS = 3
IMG_DEV = 8


teacher_temp = 0.07
student_temp = 0.1
loss_scale = 65536.0
precise = lax.Precision.HIGHEST


def unit_rows(features):
    wide = features.astype(jnp.float32)
    return (wide * lax.rsqrt(jnp.sum(wide * wide, axis=1, keepdims=True) + 1e-06)).astype(
        jnp.bfloat16
    )


def head_core(
    teacher_raw,
    student_raw,
    teacher_sq,
    student_sq,
    live_rows,
    token_weight,
    column_total,
    row_total,
    closing_total,
):
    inv_t = lax.rsqrt(teacher_sq + 1e-06)
    inv_s = lax.rsqrt(student_sq + 1e-06)
    energy = jnp.exp(teacher_raw * inv_t / teacher_temp)
    scale_r = live_rows
    scale_c = jnp.zeros((energy.shape[1],), jnp.float32)
    for sweep_no in range(SWEEPS):
        scale_c = 1.0 / column_total(jnp.dot(scale_r, energy, precision=precise))
        if sweep_no + 1 < SWEEPS:
            scale_r = live_rows / row_total(jnp.dot(energy, scale_c, precision=precise))
    cosine = student_raw * inv_s
    logits = cosine / student_temp
    exp_terms = jnp.exp(logits)
    weighted = energy * scale_c
    row_mass, cross_mass, softmax_sum = closing_total(
        (
            jnp.dot(energy, scale_c, precision=precise),
            jnp.sum(weighted * logits, axis=1),
            jnp.sum(exp_terms, axis=1),
        )
    )
    token_loss = live_rows * (jnp.log(softmax_sum) - cross_mass / row_mass)
    target = weighted / row_mass[:, None]
    grad_bf = (
        loss_scale
        * token_weight[:, None]
        * (exp_terms / softmax_sum[:, None] - target)
        / student_temp
    ).astype(jnp.bfloat16)
    dot_part = jnp.sum(grad_bf.astype(jnp.float32) * cosine, axis=0)
    return (token_loss, grad_bf, dot_part, inv_s)


def contract_rows(left, right):
    return lax.dot_general(
        left, right, (((0,), (0,)), ((), ())), preferred_element_type=jnp.float32
    )


def local(teacher_feat, student_feat, teacher_proto, student_proto, mask_index, mask_count):
    masked = mask_index.shape[0]
    slot_ids = jnp.arange(masked, dtype=jnp.int32)
    live_rows = (slot_ids < mask_count[0]).astype(jnp.float32)
    image_of = mask_index // PATCH
    onehot = (image_of[:, None] == jnp.arange(IMG_DEV, dtype=jnp.int32)[None, :]).astype(
        jnp.float32
    )
    per_image = jnp.sum(onehot * live_rows[:, None], axis=0)
    own_count = jnp.sum(onehot * per_image[None, :], axis=1)
    images_all = IMG_DEV * lax.axis_size("dp")
    token_weight = live_rows / (jnp.maximum(own_count, 1.0) * images_all)
    teacher_unit = unit_rows(teacher_feat[mask_index])
    student_unit = unit_rows(student_feat[mask_index])
    teacher_piece = lax.all_gather(teacher_proto, "dp", axis=0, tiled=True)
    student_piece = lax.all_gather(student_proto, "dp", axis=0, tiled=True)
    teacher_wide = teacher_piece.astype(jnp.float32)
    student_wide = student_piece.astype(jnp.float32)
    teacher_raw = jnp.dot(teacher_unit, teacher_piece, preferred_element_type=jnp.float32)
    student_raw = jnp.dot(student_unit, student_piece, preferred_element_type=jnp.float32)
    teacher_sq = jnp.sum(teacher_wide * teacher_wide, axis=0)
    student_sq = jnp.sum(student_wide * student_wide, axis=0)
    token_loss, grad_bf, dot_part, inv_s = head_core(
        teacher_raw,
        student_raw,
        teacher_sq,
        student_sq,
        live_rows,
        token_weight,
        lambda values: lax.psum(values, "dp"),
        lambda values: lax.psum(values, "proto"),
        lambda parts: lax.psum((parts[0], parts[1], parts[2]), "proto"),
    )
    dot_all = lax.psum(dot_part, "dp")
    grad_own = lax.psum_scatter(
        contract_rows(student_unit, grad_bf), "dp", scatter_dimension=0, tiled=True
    )
    proto_grad = inv_s * (grad_own - student_proto.astype(jnp.float32) * inv_s * dot_all)
    return (token_loss, proto_grad)


def solution(mesh):
    return jax.shard_map(
        local,
        mesh=mesh,
        in_specs=(
            P("dp", None),
            P("dp", None),
            P("dp", "proto"),
            P("dp", "proto"),
            P("dp"),
            P("dp"),
        ),
        out_specs=(P("dp"), P("dp", "proto")),
        check_vma=False,
    )
```

profile of v0, /device:TPU:1, one launch (start us, length us, event | category | flops | bytes accessed | tf_op | source)
XLA Modules:
  0.0 786.6 jit_solution(15077215755832458670)
XLA Ops:
  7.2 0.0 all-gather.5.cloned.1.call-start
  7.2 0.7 all-gather.5.cloned.1.call-update
  7.9 0.0 all-gather.3.cloned.1.call-start
  8.0 0.7 all-gather.3.cloned.1.call-update
  8.7 0.0 all-reduce.6.cloned.1.call-start
  9.4 0.7 add_select_fusion
  10.1 2.1 gather_fusion
  12.2 3.0 gather_fusion.1
  15.2 0.1 select_reduce_fusion.1
  15.3 0.1 select_reduce_fusion
  15.4 0.1 fusion
  15.6 0.2 fusion.2
  15.7 51.2 %all-gather.5.cloned.1.call-done = bf16[256,16384]{1,0:T(8,128)(2,1)} async-done(((bf16[8,16384]{1,0:T(8,128)(2,1)}), bf16[256,16384]{1,0:T(8,128)(2,1)}) %all-gather.5.cloned.1.call-update) | async-done | bytes 8388624 | tf_op jit(solution)/shard_map/all_gather | solution.py:87
  67.0 5.1 multiply_reduce_fusion.2
  72.1 14.8 %multiply_exponential_fusion = f32[384,16384]{1,0:T(8,128)} fusion(bf16[256,16384]{1,0:T(8,128)(2,1)} %all-gather.5.cloned.1.call-done, f32[16384]{0:T(1024)S(1)} %add_rsqrt_fusion, bf16[384,256]{1,0:T(8,128)(2,1)S(1)} %gather_fusion.1, f32[384]{0:T(512)S(1)} %add_rsqrt_fusion.2), kind=kOutput, calls=%fused_computation.5 | convolution fusion | flops 3234103296 | bytes 33818112 | tf_op jit(solution)/shard_map/dot_general | solution.py:91
  86.9 12.8 %fusion.13 = f32[1,16384]{1,0:T(1,128)} fusion(pred[384,1]{0,1:T(4,128)(4,1)S(1)} %reshape.62, f32[384,16384]{1,0:T(8,128)} %multiply_exponential_fusion), kind=kOutput, calls=%fused_computation.50 | convolution fusion | flops 75497472 | bytes 25231744 | tf_op jit(solution)/shard_map/dot_general | solution.py:41
  99.7 0.0 all-reduce.6.cloned.1.call-update
  99.7 0.5 all-reduce.8.cloned.1.call-start
  100.2 21.6 %all-gather.3.cloned.1.call-done = bf16[256,16384]{1,0:T(8,128)(2,1)} async-done(((bf16[8,16384]{1,0:T(8,128)(2,1)}), bf16[256,16384]{1,0:T(8,128)(2,1)}) %all-gather.3.cloned.1.call-update) | async-done | bytes 8388624 | tf_op jit(solution)/shard_map/all_gather | solution.py:88
  121.8 5.1 multiply_reduce_fusion.3
  126.9 93.5 %all-reduce.6.cloned.1.call-done = f32[16384]{0:T(1024)} async-done(((f32[16384]{0:T(1024)}), f32[16384]{0:T(1024)}) %all-reduce.6.cloned.1.call-update) | async-done | bytes 65552 | tf_op jit(solution)/shard_map/psum | solution.py:102
  220.5 0.9 broadcast_divide_fusion.2
  221.3 23.7 %convolution_reduce_fusion.2 = f32[384]{0:T(512)S(1)} fusion(f32[384,16384]{1,0:T(8,128)} %multiply_exponential_fusion, f32[16384,1]{0,1:T(1,128)S(1)} %bitcast.32), kind=kOutput, calls=%fused_computation.12 | convolution fusion | flops 75497472 | bytes 25232896 | tf_op jit(solution)/shard_map/dot_general | solution.py:43
  245.0 8.5 %psum.65 = f32[384]{0:T(512)S(1)} all-reduce(f32[384]{0:T(512)S(1)} %convolution_reduce_fusion.2), channel_id=1, replica_groups=mesh['dp'=32,'proto'=4] {'proto'}, use_global_device_ids=true, to_apply=%region_7.8 | all-reduce | flops 384 | bytes 3072 | tf_op jit(solution)/shard_map/psum | solution.py:103
  253.5 16.2 %fusion.14 = f32[1,16384]{1,0:T(1,128)} fusion(f32[384,1]{0,1:T(1,128)S(1)} %reshape.66, f32[384,16384]{1,0:T(8,128)} %multiply_exponential_fusion), kind=kOutput, calls=%fused_computation.51 | convolution fusion | flops 75497472 | bytes 25232896 | tf_op jit(solution)/shard_map/dot_general | solution.py:41
  269.7 0.0 all-reduce.8.cloned.1.call-update
  269.8 0.2 all-reduce.10.cloned.1.call-start
  270.0 93.9 %all-reduce.8.cloned.1.call-done = f32[16384]{0:T(1024)} async-done(((f32[16384]{0:T(1024)}), f32[16384]{0:T(1024)}) %all-reduce.8.cloned.1.call-update) | async-done | bytes 65552 | tf_op jit(solution)/shard_map/psum | solution.py:102
  363.9 0.9 broadcast_divide_fusion.1
  364.7 23.7 %convolution_reduce_fusion.1 = f32[384]{0:T(512)S(1)} fusion(f32[384,16384]{1,0:T(8,128)} %multiply_exponential_fusion, f32[16384,1]{0,1:T(1,128)S(1)} %bitcast.33), kind=kOutput, calls=%fused_computation.11 | convolution fusion | flops 75497472 | bytes 25232896 | tf_op jit(solution)/shard_map/dot_general | solution.py:43
  388.5 8.5 %psum.67 = f32[384]{0:T(512)S(1)} all-reduce(f32[384]{0:T(512)S(1)} %convolution_reduce_fusion.1), channel_id=1, replica_groups=mesh['dp'=32,'proto'=4] {'proto'}, use_global_device_ids=true, to_apply=%region_9.10 | all-reduce | flops 384 | bytes 3072 | tf_op jit(solution)/shard_map/psum | solution.py:103
  396.9 16.2 %fusion.15 = f32[1,16384]{1,0:T(1,128)} fusion(f32[384,1]{0,1:T(1,128)S(1)} %reshape.70, f32[384,16384]{1,0:T(8,128)} %multiply_exponential_fusion), kind=kOutput, calls=%fused_computation.52 | convolution fusion | flops 75497472 | bytes 25232896 | tf_op jit(solution)/shard_map/dot_general | solution.py:41
  413.2 0.0 all-reduce.10.cloned.1.call-update
  413.2 0.3 all-reduce.12.cloned.1.call-start
  413.4 15.1 %exponential_reduce_fusion = (f32[384]{0:T(512)S(1)}, f32[384,16384]{1,0:T(8,128)}) fusion(f32[16384]{0:T(1024)S(1)} %add_rsqrt_fusion.1, bf16[256,16384]{1,0:T(8,128)(2,1)} %all-gather.3.cloned.1.call-done, bf16[384,256]{1,0:T(8,128)(2,1)S(1)} %gather_fusion, f32[384]{0:T(512)S(1)} %add_rsqrt_fusion.3), kind=kOutput, calls=%fused_computation.7 | convolution fusion | flops 3240394240 | bytes 33819648 | tf_op jit(solution)/shard_map/dot_general | solution.py:92
  428.5 78.8 %all-reduce.10.cloned.1.call-done = f32[16384]{0:T(1024)} async-done(((f32[16384]{0:T(1024)}), f32[16384]{0:T(1024)}) %all-reduce.10.cloned.1.call-update) | async-done | bytes 65552 | tf_op jit(solution)/shard_map/psum | solution.py:102
  507.3 0.9 broadcast_divide_fusion
  508.2 23.7 %convolution_reduce_fusion = f32[384]{0:T(512)S(1)} fusion(f32[384,16384]{1,0:T(8,128)} %multiply_exponential_fusion, f32[16384,1]{0,1:T(1,128)S(1)} %bitcast.28), kind=kOutput, calls=%fused_computation.10 | convolution fusion | flops 75497472 | bytes 25232896 | tf_op jit(solution)/shard_map/dot_general | solution.py:50
  531.9 8.5 %all-reduce = (f32[384]{0:T(512)S(1)}, f32[384]{0:T(512)S(1)}) all-reduce(f32[384]{0:T(512)S(1)} %convolution_reduce_fusion, f32[384]{0:T(512)S(1)} %get-tuple-element.9), channel_id=1, replica_groups=mesh['dp'=32,'proto'=4] {'proto'}, use_global_device_ids=true, to_apply=%region_13.14 | all-reduce | flops 768 | bytes 6144 | tf_op jit(solution)/shard_map/psum | solution.py:104
  540.3 26.6 %multiply_reduce_fusion = (f32[16384]{0:T(1024)}, f32[384]{0:T(512)S(1)}, bf16[384,16384]{1,0:T(8,128)(2,1)}) fusion(f32[384,16384]{1,0:T(8,128)} %get-tuple-element.10, f32[384,16384]{1,0:T(8,128)} %multiply_exponential_fusion, f32[16384]{0:T(1024)S(1)} %broadcast_divide_fusion, f32[384]{0:T(512)S(1)} %get-tuple-element.4, f32[384]{0:T(512)S(1)} %get-tuple-element.5, ...), kind=kLoop, calls=%fused_computation.2 | loop fusion | flops 81772160 | bytes 63051776 | tf_op jit(solution)/shard_map/reduce_sum | solution.py:63
  566.9 0.0 all-reduce.12.cloned.1.call-update
  567.0 0.0 reduce-scatter.2.cloned.1.call-start
  567.0 12.9 %fusion.6 = f32[256,16384]{1,0:T(8,128)} fusion(bf16[384,16384]{1,0:T(8,128)(2,1)} %get-tuple-element.6, bf16[384,256]{1,0:T(8,128)(2,1)S(1)} %gather_fusion, f32[384]{0:T(512)S(1)} %add_rsqrt_fusion.3), kind=kOutput, calls=%fused_computation.23 | convolution fusion | flops 3221520384 | bytes 29558272 | tf_op jit(solution)/shard_map/dot_general | solution.py:68
  580.0 6.5 psum.69
  586.5 0.6 subtract_select_fusion
  587.1 74.0 %all-reduce.12.cloned.1.call-done = f32[16384]{0:T(1024)} async-done(((f32[16384]{0:T(1024)}), f32[16384]{0:T(1024)}) %all-reduce.12.cloned.1.call-update) | async-done | bytes 65552 | tf_op jit(solution)/shard_map/psum | solution.py:106
  661.1 116.5 %reduce-scatter.2.cloned.1.call-done = f32[8,16384]{1,0:T(8,128)} async-done(((f32[256,16384]{1,0:T(8,128)}), f32[8,16384]{1,0:T(8,128)}) %reduce-scatter.2.cloned.1.call-update) | async-done | bytes 524304 | tf_op jit(solution)/shard_map/reduce_scatter | solution.py:107
  777.6 1.9 subtract_multiply_fusion
  (20 shorter events, 0.1 us)
Async XLA Ops:
  7.2 2.9 copy-start
  7.2 59.8 %all-gather.5.cloned.1.call-start = ((), (), s32[]{:S(2)}) async-start(), calls=%async_computation.2 | async-start | bytes 8650752 | tf_op jit(solution)/shard_map/all_gather | solution.py:87
  7.9 113.9 %all-gather.3.cloned.1.call-start = ((), (), s32[]{:S(2)}) async-start(), calls=%async_computation.1 | async-start | bytes 8650752 | tf_op jit(solution)/shard_map/all_gather | solution.py:88
  8.7 211.8 %all-reduce.6.cloned.1.call-start = ((), (), s32[]{:S(2)}) async-start(), calls=%async_computation.3 | async-start | bytes 131072 | tf_op jit(solution)/shard_map/psum | solution.py:102
  99.7 264.2 %all-reduce.8.cloned.1.call-start = ((), (), s32[]{:S(2)}) async-start(), calls=%async_computation.4 | async-start | bytes 131072 | tf_op jit(solution)/shard_map/psum | solution.py:102
  269.8 237.5 %all-reduce.10.cloned.1.call-start = ((), (), s32[]{:S(2)}) async-start(), calls=%async_computation.5 | async-start | bytes 131072 | tf_op jit(solution)/shard_map/psum | solution.py:102
  413.2 247.9 %all-reduce.12.cloned.1.call-start = ((), (), s32[]{:S(2)}) async-start(), calls=%async_computation.7 | async-start | bytes 131072 | tf_op jit(solution)/shard_map/psum | solution.py:106
  567.0 210.6 %reduce-scatter.2.cloned.1.call-start = ((), (), s32[]{:S(2)}) async-start(), calls=%async_computation.6 | async-start | bytes 17301504 | tf_op jit(solution)/shard_map/reduce_scatter | solution.py:107
  567.0 212.5 %copy-start.1 = (bf16[2048,256]{1,0:T(8,128)(2,1)S(1)}, bf16[2048,256]{1,0:T(8,128)(2,1)}, u32[]{:S(2)}) copy-start(bf16[2048,256]{1,0:T(8,128)(2,1)} %param.7) | copy-start | bytes 3145732
  567.0 210.5 %copy-start.2 = (bf16[8,16384]{1,0:T(8,128)(2,1)S(1)}, bf16[8,16384]{1,0:T(8,128)(2,1)}, u32[]{:S(2)}) copy-start(bf16[8,16384]{1,0:T(8,128)(2,1)} %param.9) | copy-start | bytes 786436
Sparse Core Ops, SparseCore 0:
  10.3 56.6 all-gather.4
  69.2 52.5 all-gather.2
  125.6 94.7 all-reduce.5
  269.9 93.9 all-reduce.7
  413.3 93.9 all-reduce.9
  567.1 93.9 all-reduce.11
  665.0 112.5 reduce-scatter.1
where the time goes:
time: 794 us; the launch traced here: 787 us
  waiting for transfers between devices  531 us (67%)
  matrix products  159 us (20%)
  other arithmetic  43.2 us (5%)
  blocking collectives  31.9 us (4%)
  between operations  15.2 us (2%)
    psum x3, waiting for transfers between devices, local(): lax.psum(values, 'dp')  266 us
    reduce_scatter x1, waiting for transfers between devices, local(): lax.psum_scatter(contract_rows(student_unit, grad_bf), 'dp', scatter_dime...  116 us
    psum x1, waiting for transfers between devices, local(): dot_all = lax.psum(dot_part, 'dp')  74 us
    all_gather x1, waiting for transfers between devices, local(): teacher_piece = lax.all_gather(teacher_proto, 'dp', axis=0, tiled=True)  51.2 us
    dot_general x2, matrix products, head_core(): scale_r = live_rows / row_total(jnp.dot(energy, scale_c, precision=precise))  47.4 us
    dot_general x3, matrix products, head_core(): scale_c = 1.0 / column_total(jnp.dot(scale_r, energy, precision=precise))  45.2 us
    reduce_sum x1, other arithmetic, head_core(): dot_part = jnp.sum(grad_bf.astype(jnp.float32) * cosine, axis=0)  26.6 us
    dot_general x1, matrix products, head_core(): jnp.dot(energy, scale_c, precision=precise)  23.7 us
  transfers between devices with their start and end apart: 7, of which 7 were waited for; matrix products, arithmetic and copies ran while one was open for 9% of the time, Pallas kernels for 0%

commit v1 on v0

v1 whole, which is shorter than its diff:
```python
import functools

import jax
import jax.numpy as jnp
from jax import lax
from jax.experimental import pallas as pl
from jax.experimental.pallas import tpu as pltpu
from jax.sharding import PartitionSpec as P

PATCH = 256
EXTRA = 16
LOG2E = 1.4426950408889634

teacher_temp = 0.07
student_temp = 0.1
loss_scale = 65536.0

f32 = jnp.float32
bf16 = jnp.bfloat16


def params(mib):
    return pltpu.CompilerParams(vmem_limit_bytes=mib * 1024 * 1024)


def nn(a, b):
    return lax.dot_general(a, b, (((1,), (0,)), ((), ())), preferred_element_type=f32)


def nt(a, b):
    return lax.dot_general(a, b, (((1,), (1,)), ((), ())), preferred_element_type=f32)


def tokens_kernel(count_ref, index_ref, teacher_ref, student_ref, t_out, s_out):
    slots = index_ref.shape[1]
    source = teacher_ref.shape[0]
    index_row = index_ref[...]
    index_col = jnp.transpose(jnp.broadcast_to(index_row, (8, slots)))[:, 0:1]
    count = count_ref[0]
    live_row = lax.broadcasted_iota(jnp.int32, (1, slots), 1) < count
    live_col = lax.broadcasted_iota(jnp.int32, (slots, 1), 0) < count
    same = ((index_col >> 8) == (index_row >> 8)) & live_col
    own = jnp.sum(jnp.where(same, 1.0, 0.0), axis=0, keepdims=True)
    own = jnp.where(live_row, own, 0.0)
    pick = jnp.where(
        lax.broadcasted_iota(jnp.int32, (slots, source), 1) == index_col, 1.0, 0.0
    ).astype(bf16)
    for src, dst in ((teacher_ref, t_out), (student_ref, s_out)):
        rows = nn(pick, src[...])
        unit = rows * lax.rsqrt(jnp.sum(rows * rows, axis=1, keepdims=True) + 1e-06)
        dst[0 : unit.shape[1], :] = jnp.transpose(unit).astype(bf16)
    d = teacher_ref.shape[1]
    t_out[d : d + EXTRA, :] = jnp.broadcast_to(own, (EXTRA, slots)).astype(bf16)


def tokens(count, index, teacher_feat, student_feat):
    slots, d = index.shape[0], teacher_feat.shape[1]
    vm = pl.BlockSpec(memory_space=pltpu.VMEM)
    return pl.pallas_call(
        tokens_kernel,
        out_shape=(
            jax.ShapeDtypeStruct((d + EXTRA, slots), bf16),
            jax.ShapeDtypeStruct((d, slots), bf16),
        ),
        in_specs=[pl.BlockSpec(memory_space=pltpu.SMEM), vm, vm, vm],
        out_specs=(vm, vm),
        compiler_params=params(32),
        name="token_rows",
    )(count, index.reshape(1, slots), teacher_feat, student_feat)


def column_scale(wide_t):
    return lax.rsqrt(jnp.sum(wide_t * wide_t, axis=1, keepdims=True) + 1e-06)


def pair(ref):
    return jnp.concatenate([ref[0], ref[1]], axis=1)


def fold(m):
    total = m[:, 0:128]
    for k in range(1, m.shape[1] // 128):
        total = total + m[:, 128 * k : 128 * (k + 1)]
    return total


def energy_kernel(u_ref, w_ref, e_ref, row_ref, own_ref, wt, scale, acc, e_all, own_all):
    step, steps = pl.program_id(0), pl.num_programs(0)
    d = w_ref.shape[0]

    @pl.when(step == 0)
    def _():
        wide = jnp.transpose(w_ref[...].astype(f32))
        wt[...] = wide.astype(bf16)
        scale[...] = column_scale(wide) * (LOG2E / teacher_temp)
        acc[...] = jnp.zeros_like(acc)

    block = pair(u_ref)
    own = block[d : d + 8, :].astype(f32)[0:1, :]
    own_ref[0] = own
    live = jnp.where(own > 0.0, 1.0, 0.0)
    width = block.shape[1]
    for k in range(0, width, 256):
        raw = nn(wt[...], block[0:d, k : k + 256])
        energy = jnp.exp2(raw * scale[...])
        acc[...] += fold(energy * live[:, k : k + 256])
        low = energy.astype(bf16)
        e_ref[0, :, k : k + 256] = low
        e_all[step, :, k : k + 256] = low

    @pl.when(step == steps - 1)
    def _():
        c = 1.0 / jnp.sum(acc[...], axis=1, keepdims=True)

        def rows(i, _):
            row_ref[i] = jnp.sum(e_all[i].astype(f32) * c, axis=0, keepdims=True)
            return 0

        lax.fori_loop(0, e_all.shape[0], rows, 0)


def energy_pass(blocks, w):
    groups, rows, slots = blocks.shape
    d, cols = w.shape
    steps, width = groups // 2, 2 * slots
    return pl.pallas_call(
        energy_kernel,
        grid=(steps,),
        out_shape=(
            jax.ShapeDtypeStruct((steps, cols, width), bf16),
            jax.ShapeDtypeStruct((steps, 1, width), f32),
            jax.ShapeDtypeStruct((steps, 1, width), f32),
        ),
        in_specs=[
            pl.BlockSpec((2, rows, slots), lambda i: (i, 0, 0)),
            pl.BlockSpec((d, cols), lambda i: (0, 0)),
        ],
        out_specs=(
            pl.BlockSpec((1, cols, width), lambda i: (i, 0, 0)),
            pl.BlockSpec((steps, 1, width), lambda i: (0, 0, 0)),
            pl.BlockSpec((1, 1, width), lambda i: (i, 0, 0)),
        ),
        scratch_shapes=[
            pltpu.VMEM((cols, d), bf16),
            pltpu.VMEM((cols, 1), f32),
            pltpu.VMEM((cols, 128), f32),
            pltpu.VMEM((steps, cols, width), bf16),
            pltpu.VMEM((steps, 1, width), f32),
        ],
        compiler_params=params(48),
        name="energy_pass",
    )(blocks, w)


def load_all(hbm, vmem, sems):
    copies = [
        pltpu.make_async_copy(hbm.at[i], vmem.at[i], sems.at[i]) for i in range(vmem.shape[0])
    ]
    return copies


def column_pass(e_all, own_ref, total_ref, acc):
    acc[...] = jnp.zeros_like(acc)

    def cols(i, _):
        r = jnp.where(own_ref[i] > 0.0, 1.0, 0.0) / total_ref[i]
        acc[...] += fold(e_all[i].astype(f32) * r)
        return 0

    return cols


def sweep_kernel(own_ref, total_ref, e_ref, row_ref, acc, e_all, sems):
    steps = e_all.shape[0]

    def copy(i):
        return pltpu.make_async_copy(e_ref.at[i], e_all.at[i], sems.at[i])

    lax.fori_loop(0, steps, lambda i, _: (copy(i).start(), 0)[1], 0)
    body = column_pass(e_all, own_ref, total_ref, acc)

    def cols(i, _):
        copy(i).wait()
        return body(i, 0)

    lax.fori_loop(0, steps, cols, 0)
    c = 1.0 / jnp.sum(acc[...], axis=1, keepdims=True)

    def rows(i, _):
        row_ref[i] = jnp.sum(e_all[i].astype(f32) * c, axis=0, keepdims=True)
        return 0

    lax.fori_loop(0, steps, rows, 0)


def sweep_pass(own, total, energy):
    steps, cols, width = energy.shape
    vm = pl.BlockSpec(memory_space=pltpu.VMEM)
    return pl.pallas_call(
        sweep_kernel,
        out_shape=jax.ShapeDtypeStruct((steps, 1, width), f32),
        in_specs=[vm, vm, pl.BlockSpec(memory_space=pl.ANY)],
        out_specs=vm,
        scratch_shapes=[
            pltpu.VMEM((cols, 128), f32),
            pltpu.VMEM((steps, cols, width), bf16),
            pltpu.SemaphoreType.DMA((steps,)),
        ],
        compiler_params=params(48),
        name="sweep_pass",
    )(own, total, energy)


def softmax_kernel(u_ref, w_ref, sum_ref, wt, scale):
    @pl.when(pl.program_id(0) == 0)
    def _():
        wide = jnp.transpose(w_ref[...].astype(f32))
        wt[...] = wide.astype(bf16)
        scale[...] = column_scale(wide) * (LOG2E / student_temp)

    block = pair(u_ref)
    for k in range(0, block.shape[1], 256):
        raw = nn(wt[...], block[:, k : k + 256])
        sum_ref[0, :, k : k + 256] = jnp.sum(
            jnp.exp2(raw * scale[...]), axis=0, keepdims=True
        )


def softmax_pass(blocks, w):
    groups, d, slots = blocks.shape
    cols = w.shape[1]
    steps, width = groups // 2, 2 * slots
    return pl.pallas_call(
        softmax_kernel,
        grid=(steps,),
        out_shape=jax.ShapeDtypeStruct((steps, 1, width), f32),
        in_specs=[
            pl.BlockSpec((2, d, slots), lambda i: (i, 0, 0)),
            pl.BlockSpec((d, cols), lambda i: (0, 0)),
        ],
        out_specs=pl.BlockSpec((1, 1, width), lambda i: (i, 0, 0)),
        scratch_shapes=[pltpu.VMEM((cols, d), bf16), pltpu.VMEM((cols, 1), f32)],
        compiler_params=params(32),
        name="softmax_pass",
    )(blocks, w)


def closing_kernel(own_ref, total_ref, e_ref, u_ref, w_ref, c_ref, mass_ref, cross_ref,
                   acc, e_all, u_all, wt, sems, u_sems):
    steps = e_all.shape[0]

    def copy(i):
        return pltpu.make_async_copy(e_ref.at[i], e_all.at[i], sems.at[i])

    def copy_u(i):
        return pltpu.make_async_copy(
            u_ref.at[pl.ds(2 * i, 2)], u_all.at[pl.ds(2 * i, 2)], u_sems.at[i]
        )

    lax.fori_loop(0, steps, lambda i, _: (copy(i).start(), 0)[1], 0)
    lax.fori_loop(0, steps, lambda i, _: (copy_u(i).start(), 0)[1], 0)
    wide = jnp.transpose(w_ref[...].astype(f32))
    wt[...] = wide.astype(bf16)
    body = column_pass(e_all, own_ref, total_ref, acc)

    def cols(i, _):
        copy(i).wait()
        return body(i, 0)

    lax.fori_loop(0, steps, cols, 0)
    c = 1.0 / jnp.sum(acc[...], axis=1, keepdims=True)
    c_ref[...] = c
    cs = c * (column_scale(wide) * (1.0 / student_temp))

    def rows(i, _):
        copy_u(i).wait()
        block = pair(u_all.at[pl.ds(2 * i, 2)])
        for k in range(0, block.shape[1], 256):
            raw = nn(wt[...], block[:, k : k + 256])
            energy = e_all[i, :, k : k + 256].astype(f32)
            mass_ref[i, :, k : k + 256] = jnp.sum(energy * c, axis=0, keepdims=True)
            cross_ref[i, :, k : k + 256] = jnp.sum(
                energy * cs * raw, axis=0, keepdims=True
            )
        return 0

    lax.fori_loop(0, steps, rows, 0)


def closing_pass(own, total, energy, blocks, w):
    steps, cols, width = energy.shape
    d = w.shape[0]
    vm = pl.BlockSpec(memory_space=pltpu.VMEM)
    hbm = pl.BlockSpec(memory_space=pl.ANY)
    return pl.pallas_call(
        closing_kernel,
        out_shape=(
            jax.ShapeDtypeStruct((cols, 1), f32),
            jax.ShapeDtypeStruct((steps, 1, width), f32),
            jax.ShapeDtypeStruct((steps, 1, width), f32),
        ),
        in_specs=[vm, vm, hbm, hbm, vm],
        out_specs=(vm, vm, vm),
        scratch_shapes=[
            pltpu.VMEM((cols, 128), f32),
            pltpu.VMEM((steps, cols, width), bf16),
            pltpu.VMEM(blocks.shape, bf16),
            pltpu.VMEM((cols, d), bf16),
            pltpu.SemaphoreType.DMA((steps,)),
            pltpu.SemaphoreType.DMA((steps,)),
        ],
        compiler_params=params(48),
        name="closing_pass",
    )(own, total, energy, blocks, w)


def grad_kernel(images, own_ref, mass_ref, soft_ref, e_ref, u_ref, w_ref, c_ref, g_ref,
                wt, scale, acc):
    step = pl.program_id(0)

    @pl.when(step == 0)
    def _():
        wide = jnp.transpose(w_ref[...].astype(f32))
        wt[...] = wide.astype(bf16)
        scale[...] = column_scale(wide) * (LOG2E / student_temp)
        acc[...] = jnp.zeros_like(acc)

    block = pair(u_ref)
    own = own_ref[0]
    weight = jnp.where(own > 0.0, 1.0, 0.0) / (jnp.maximum(own, 1.0) * images)
    weight = weight * (loss_scale / student_temp)
    soft_w = weight / soft_ref[0]
    mass_w = weight / mass_ref[0]
    for k in range(0, block.shape[1], 256):
        part = block[:, k : k + 256]
        raw = nn(wt[...], part)
        soft = jnp.exp2(raw * scale[...]) * soft_w[:, k : k + 256]
        target = e_ref[0, :, k : k + 256].astype(f32) * c_ref[...] * mass_w[:, k : k + 256]
        acc[...] += nt((soft - target).astype(bf16), part)

    @pl.when(step == pl.num_programs(0) - 1)
    def _():
        wide = jnp.transpose(w_ref[...].astype(f32))
        inv = column_scale(wide)
        grad = acc[...]
        unit = wide * inv
        dot = jnp.sum(grad * unit, axis=1, keepdims=True)
        g_ref[...] = jnp.transpose(inv * (grad - unit * dot))


def grad_pass(images, own, mass, soft, energy, blocks, w, c):
    steps, cols, width = energy.shape
    d, slots = blocks.shape[1:]
    vec = pl.BlockSpec((1, 1, width), lambda i: (i, 0, 0))
    return pl.pallas_call(
        functools.partial(grad_kernel, float(images)),
        grid=(steps,),
        out_shape=jax.ShapeDtypeStruct((d, cols), f32),
        in_specs=[
            vec,
            vec,
            vec,
            pl.BlockSpec((1, cols, width), lambda i: (i, 0, 0)),
            pl.BlockSpec((2, d, slots), lambda i: (i, 0, 0)),
            pl.BlockSpec((d, cols), lambda i: (0, 0)),
            pl.BlockSpec((cols, 1), lambda i: (0, 0)),
        ],
        out_specs=pl.BlockSpec((d, cols), lambda i: (0, 0)),
        scratch_shapes=[
            pltpu.VMEM((cols, d), bf16),
            pltpu.VMEM((cols, 1), f32),
            pltpu.VMEM((cols, d), f32),
        ],
        compiler_params=params(32),
        name="grad_pass",
    )(own, mass, soft, energy, blocks, w, c)


def dp_shift(value, part, k):
    size, stride = {"z": (4, 8), "y": (4, 2), "core": (2, 1)}[part]
    perm = []
    for i in range(32):
        at = (i // stride) % size
        perm.append((i, i + (((at + k) % size) - at) * stride))
    return lax.ppermute(value, "dp", perm)


def x_shift(value, k):
    return lax.ppermute(value, "proto", [(i, (i + k) % 4) for i in range(4)])


def total_of(value):
    value = value + dp_shift(value, "core", 1)
    value = value + x_shift(value, 1) + x_shift(value, 3) + x_shift(value, 2)
    for part in ("y", "z"):
        value = (
            value
            + dp_shift(value, part, 1)
            + dp_shift(value, part, 3)
            + dp_shift(value, part, 2)
        )
    return value


def local(teacher_feat, student_feat, teacher_proto, student_proto, mask_index, mask_count):
    slots = mask_index.shape[0]
    groups = lax.axis_size("dp")
    images = groups * (teacher_feat.shape[0] // PATCH)
    t_block, s_block = tokens(mask_count, mask_index, teacher_feat, student_feat)
    t_blocks = lax.all_gather(t_block, "dp", axis=0)
    s_blocks = lax.all_gather(s_block, "dp", axis=0)
    t_w = lax.all_to_all(teacher_proto, "dp", 1, 0, tiled=True)
    s_w = lax.all_to_all(student_proto, "dp", 1, 0, tiled=True)
    energy, row, own = energy_pass(t_blocks, t_w)
    total = total_of(row)
    soft_part = softmax_pass(s_blocks, s_w)
    row = sweep_pass(own, total, energy)
    both = total_of(jnp.concatenate([row, soft_part], axis=1))
    total, soft = both[:, 0:1], both[:, 1:2]
    c, mass_part, cross_part = closing_pass(own, total, energy, s_blocks, s_w)
    mass = total_of(mass_part)
    cross = total_of(cross_part)
    grad = grad_pass(images, own, mass, soft, energy, s_blocks, s_w, c)
    proto_grad = lax.all_to_all(grad, "dp", 0, 1, tiled=True)
    start = lax.axis_index("dp") * slots

    def mine(v):
        return lax.dynamic_slice_in_dim(v.reshape(-1), start, slots, 0)

    live = (jnp.arange(slots, dtype=jnp.int32) < mask_count[0]).astype(f32)
    token_loss = live * (jnp.log(mine(soft)) - mine(cross) / mine(mass))
    return (token_loss, proto_grad)


def solution(mesh):
    return jax.shard_map(
        local,
        mesh=mesh,
        in_specs=(
            P("dp", None),
            P("dp", None),
            P("dp", "proto"),
            P("dp", "proto"),
            P("dp"),
            P("dp"),
        ),
        out_specs=(P("dp"), P("dp", "proto")),
        check_vma=False,
    )
```

time: 794 us -> 251 us (0.32)
  waiting for transfers between devices: 531 us -> 79.9 us
  matrix products: 159 us -> 0 us
  Pallas kernels: 0 us -> 64.1 us
  starting transfers between devices: 1.13 us -> 61.5 us
  other arithmetic: 43.2 us -> 1.37 us
  blocking collectives: 31.9 us -> 18.5 us
    psum x4 -> x0, waiting for transfers between devices: 340 us -> none  [the longest x3 266 us: local(): lax.psum(values, 'dp')]
    dot_general x9 -> x0, matrix products: 159 us -> none  [the longest x2 47.4 us: head_core(): scale_r = live_rows / row_total(jnp.dot(energy, scale_c, precision=precise))]
    reduce_scatter x1 -> x0, waiting for transfers between devices: 116 us -> none  [local(): lax.psum_scatter(contract_rows(student_unit, grad_bf), 'dp', scatter_dime...]
    pallas_call x0 -> x6, Pallas kernels: none -> 64.1 us  [the longest x1 19.9 us: energy_pass(): pl.pallas_call(energy_kernel, grid=(steps,), out_shape=(jax.ShapeDtypeStr...]
    ppermute x0 -> x40, starting transfers between devices: none -> 44.2 us  [the longest x28 31.7 us: dp_shift(): return lax.ppermute(value, 'dp', perm)]
    reduce_sum x7 -> x0, other arithmetic: 37.3 us -> none  [the longest x1 26.6 us: head_core(): dot_part = jnp.sum(grad_bf.astype(jnp.float32) * cosine, axis=0)]
    all_gather x2, waiting for transfers between devices: 72.8 us -> 38.4 us  [the longest x1 34.5 us: local(): t_blocks = lax.all_gather(t_block, 'dp', axis=0)]
    ppermute x0 -> x40, waiting for transfers between devices: none -> 33.9 us  [the longest x28 22.9 us: dp_shift(): return lax.ppermute(value, 'dp', perm)]
  transfers between devices with their start and end apart: 7 -> 44, of which waited for: 7 -> 27; matrix products, arithmetic and copies ran while one was open for 9% -> 0% of each run, Pallas kernels for 0% -> 16%
where the time goes in v1:
time: 251 us; the launch traced here: 250 us
  waiting for transfers between devices  79.9 us (32%)
  Pallas kernels  64.1 us (26%)
  starting transfers between devices  61.5 us (25%)
  blocking collectives  18.5 us (7%)
  between operations  15 us (6%)
  local copies, waits for them, and re-layouts  9.58 us (4%)
    all_gather x1, waiting for transfers between devices, local(): t_blocks = lax.all_gather(t_block, 'dp', axis=0)  34.5 us
    ppermute x28, starting transfers between devices, dp_shift(): return lax.ppermute(value, 'dp', perm)  31.7 us
    ppermute x28, waiting for transfers between devices, dp_shift(): return lax.ppermute(value, 'dp', perm)  22.9 us
    pallas_call x1, Pallas kernels, energy_pass(): pl.pallas_call(energy_kernel, grid=(steps,), out_shape=(jax.ShapeDtypeStr...  19.9 us
    all_to_all x1, blocking collectives, local(): t_w = lax.all_to_all(teacher_proto, 'dp', 1, 0, tiled=True)  18.5 us
    pallas_call x1, Pallas kernels, grad_pass(): pl.pallas_call(functools.partial(grad_kernel, float(images)), grid=(steps...  12.9 us
    pallas_call x1, Pallas kernels, closing_pass(): pl.pallas_call(closing_kernel, out_shape=(jax.ShapeDtypeStruct((cols, 1),...  12.7 us
    ppermute x12, starting transfers between devices, x_shift(): return lax.ppermute(value, 'proto', [(i, (i + k) % 4) for i in range(4)])  12.5 us
  transfers between devices with their start and end apart: 44, of which 27 were waited for; matrix products, arithmetic and copies ran while one was open for 0% of the time, Pallas kernels for 16%

profile of v1, /device:TPU:1, one launch (start us, length us, event | category | flops | bytes accessed | tf_op | source)
XLA Modules:
  0.0 250.0 jit_solution(9188261110053208043)
XLA Ops:
  8.5 1.2 copy-done.2
  9.8 1.2 copy-done.3
  11.0 2.2 token_rows.1
  14.0 18.5 %all_to_all.57 = bf16[8,32,512]{2,0,1:T(8,128)(2,1)S(1)} all-to-all(bf16[8,32,512]{2,0,1:T(8,128)(2,1)} %bitcast.94), channel_id=1, replica_groups=mesh['dp'=32,'proto'=4] {'dp'}, dimensions={1} | all-to-all | bytes 524288 | tf_op jit(solution)/shard_map/all_to_all | solution.py:412
  32.5 34.5 %all-gather.5.cloned.1.call-done = bf16[8704,384]{1,0:T(8,128)(2,1)} async-done(((bf16[272,384]{1,0:T(8,128)(2,1)}), bf16[8704,384]{1,0:T(8,128)(2,1)}) %all-gather.5.cloned.1.call-update) | async-done | bytes 6684688 | tf_op jit(solution)/shard_map/all_gather | solution.py:410
  67.0 19.9 %energy_pass.1 = (bf16[16,512,768]{2,1,0:T(8,128)(2,1)}, f32[16,1,768]{2,1,0:T(1,128)S(1)}, f32[16,1,768]{2,1,0:T(1,128)S(1)}) custom-call(bf16[32,272,384]{2,1,0:T(8,128)(2,1)} %bitcast.87, bf16[256,512]{1,0:T(8,128)(2,1)S(1)} %bitcast.82), custom_call_target="tpu_custom_call" | custom-call | tf_op jit(solution)/shard_map/energy_pass/pallas_call | solution.py:126
  87.1 1.0 collective-permute-done
  88.2 2.8 %collective-permute-start.3 = (f32[16,1,768]{2,1,0:T(1,128)S(1)}, f32[16,1,768]{2,1,0:T(1,128)S(1)}, u32[]{:S(2)}, u32[]{:S(2)}) collective-permute-start(f32[16,1,768]{2,1,0:T(1,128)S(1)} %add.125), channel_id=1, source_target_pairs={{0,2},{1,3},{2,0},{3,1},{4,6},{5,7},{6,4},{7,5},{8,10},{9,11},{10,... | collective-permute-start | bytes 147464 | tf_op jit(solution)/shard_map/ppermute | solution.py:389
  92.7 1.3 collective-permute-done.2
  94.0 2.0 collective-permute-done.1
  96.0 2.0 collective-permute-start.6
  99.5 7.6 %all-to-all-start.1 = ((bf16[8,32,512]{2,0,1:T(8,128)(2,1)}), bf16[8,32,512]{2,0,1:T(8,128)(2,1)S(1)}, u32[]{:S(2)}, u32[]{:S(2)}) async-start(bf16[8,32,512]{2,0,1:T(8,128)(2,1)} %bitcast.6), calls=%async_computation.1 | async-start | bytes 524288 | tf_op jit(solution)/shard_map/all_to_all | solution.py:413
  107.1 3.0 %collective-permute-start.9 = (f32[16,1,768]{2,1,0:T(1,128)S(1)}, f32[16,1,768]{2,1,0:T(1,128)S(1)}, u32[]{:S(2)}, u32[]{:S(2)}) collective-permute-start(f32[16,1,768]{2,1,0:T(1,128)S(1)} %bitcast.110), channel_id=1, source_target_pairs={{0,64},{4,68},{8,72},{12,76},{16,80},{20,84},{24,88},{28,92},{32,9... | collective-permute-start | bytes 147464 | tf_op jit(solution)/shard_map/ppermute | solution.py:385
  111.6 6.9 %all-to-all-done.1 = bf16[8,32,512]{2,0,1:T(8,128)(2,1)S(1)} async-done(((bf16[8,32,512]{2,0,1:T(8,128)(2,1)}), bf16[8,32,512]{2,0,1:T(8,128)(2,1)S(1)}, u32[]{:S(2)}, u32[]{:S(2)}) %all-to-all-start.1) | async-done | bytes 262176 | tf_op jit(solution)/shard_map/all_to_all | solution.py:413
  118.5 3.9 %all-gather.7.cloned.1.call-done = bf16[8192,384]{1,0:T(8,128)(2,1)} async-done(((bf16[256,384]{1,0:T(8,128)(2,1)}), bf16[8192,384]{1,0:T(8,128)(2,1)}) %all-gather.7.cloned.1.call-update) | async-done | bytes 6291472 | tf_op jit(solution)/shard_map/all_gather | solution.py:411
  122.4 2.8 %copy-done = bf16[8192,384]{1,0:T(8,128)(2,1)S(1)} copy-done((bf16[8192,384]{1,0:T(8,128)(2,1)S(1)}, bf16[8192,384]{1,0:T(8,128)(2,1)}, u32[]{:S(2)}) %copy-start) | copy-done | bytes 6291480
  125.2 7.3 %softmax_pass.1 = f32[16,1,768]{2,1,0:T(1,128)S(1)} custom-call(bf16[32,256,384]{2,1,0:T(8,128)(2,1)S(1)} %bitcast.77, bf16[256,512]{1,0:T(8,128)(2,1)S(1)} %bitcast.79), custom_call_target="tpu_custom_call" | custom-call | tf_op jit(solution)/shard_map/softmax_pass/pallas_call | solution.py:233
  132.5 9.1 %sweep_pass.1 = f32[16,1,768]{2,1,0:T(1,128)S(1)} custom-call(f32[16,1,768]{2,1,0:T(1,128)S(1)} %get-tuple-element.11.own_ref, f32[16,1,768]{2,1,0:T(1,128)S(1)} %bitcast.86, bf16[16,512,768]{2,1,0:T(8,128)(2,1)} %get-tuple-element.13.e_ref), custom_call_target="tpu_custom_call" | custom-call | tf_op jit(solution)/shard_map/sweep_pass/pallas_call | solution.py:199
  142.1 1.1 collective-permute-done.10
  143.3 2.0 collective-permute-start.13
  145.2 1.1 collective-permute-start.12
  146.7 2.3 collective-permute-done.13
  149.0 1.3 collective-permute-done.12
  151.2 2.1 collective-permute-start.16
  154.8 1.5 collective-permute-done.16
  156.8 3.0 %collective-permute-done.14 = f32[16,2,768]{2,1,0:T(2,128)S(1)} collective-permute-done((f32[16,2,768]{2,1,0:T(2,128)S(1)}, f32[16,2,768]{2,1,0:T(2,128)S(1)}, u32[]{:S(2)}, u32[]{:S(2)}) %collective-permute-start.14) | collective-permute-done | bytes 98336 | tf_op jit(solution)/shard_map/ppermute | solution.py:385
  159.8 1.2 collective-permute-start.19
  161.0 1.4 collective-permute-start.18
  162.5 2.4 collective-permute-done.19
  164.9 3.4 %collective-permute-done.17 = f32[16,2,768]{2,1,0:T(2,128)S(1)} collective-permute-done((f32[16,2,768]{2,1,0:T(2,128)S(1)}, f32[16,2,768]{2,1,0:T(2,128)S(1)}, u32[]{:S(2)}, u32[]{:S(2)}) %collective-permute-start.17) | collective-permute-done | bytes 98336 | tf_op jit(solution)/shard_map/ppermute | solution.py:385
  168.5 12.7 %closing_pass.1 = (f32[512,1]{1,0:T(8,128)S(1)}, f32[16,1,768]{2,1,0:T(1,128)S(1)}, f32[16,1,768]{2,1,0:T(1,128)S(1)}) custom-call(f32[16,1,768]{2,1,0:T(1,128)S(1)} %get-tuple-element.11.own_ref, f32[16,1,768]{2,1,0:T(1,128)S(1)} %get-tuple-element.19.total_ref, bf16[16,512,768]{2,1,0:T(8,128)(2,1)} %get-tuple-element.13.e_ref, ...), custom_call_target="tpu_custom_call" | custom-call | tf_op jit(solution)/shard_map/closing_pass/pallas_call | solution.py:295
  181.2 3.2 %collective-permute-start.30 = (f32[16,1,768]{2,1,0:T(1,128)S(1)}, f32[16,1,768]{2,1,0:T(1,128)S(1)}, u32[]{:S(2)}, u32[]{:S(2)}) collective-permute-start(f32[16,1,768]{2,1,0:T(1,128)S(1)} %get-tuple-element.16), channel_id=1, source_target_pairs={{0,4},{4,0},{8,12},{12,8},{16,20},{20,16},{24,28},{28,24},{32,36},... | collective-permute-start | bytes 147464 | tf_op jit(solution)/shard_map/ppermute | solution.py:385
  185.4 1.4 collective-permute-start.33
  186.8 0.9 collective-permute-start.32
  188.2 1.2 collective-permute-start.20
  190.2 1.7 collective-permute-done.31
  191.9 1.1 collective-permute-start.36
  194.9 1.5 collective-permute-start.22
  196.4 1.6 collective-permute-done.34
  198.8 1.1 collective-permute-start.38
  200.9 1.9 collective-permute-start.26
  204.4 2.8 %copy-done.1 = bf16[8192,384]{1,0:T(8,128)(2,1)S(1)} copy-done((bf16[8192,384]{1,0:T(8,128)(2,1)S(1)}, bf16[8192,384]{1,0:T(8,128)(2,1)}, u32[]{:S(2)}) %copy-start.1) | copy-done | bytes 6291480
  207.2 12.9 %grad_pass.1 = f32[256,512]{1,0:T(8,128)} custom-call(f32[16,1,768]{2,1,0:T(1,128)S(1)} %get-tuple-element.11.own_ref, f32[16,1,768]{2,1,0:T(1,128)S(1)} %bitcast.84, f32[16,1,768]{2,1,0:T(1,128)S(1)} %get-tuple-element.18.soft_ref, bf16[16,512,768]{2,1,0:T(8,128)(2,1)S(1)} %bitcast.75, bf16[32,256,384]{2,1,0:T(8,128)(2,1)S(1)} %bitcast.78, ...), custom_call_target="tpu_custom_call" | custom-call | tf_op jit(solution)/shard_map/grad_pass/pallas_call | solution.py:355
  220.1 9.7 %all-to-all-start.2 = ((f32[32,8,512]{2,1,0:T(8,128)}), f32[32,8,512]{2,1,0:T(8,128)S(1)}, u32[]{:S(2)}, u32[]{:S(2)}) async-start(f32[32,8,512]{2,1,0:T(8,128)} %bitcast.13), calls=%async_computation.2 | async-start | bytes 1048576 | tf_op jit(solution)/shard_map/all_to_all | solution.py:424
  229.9 3.0 %collective-permute-start.29 = (f32[16,1,768]{2,1,0:T(1,128)S(1)}, f32[16,1,768]{2,1,0:T(1,128)S(1)}, u32[]{:S(2)}, u32[]{:S(2)}) collective-permute-start(f32[16,1,768]{2,1,0:T(1,128)S(1)} %bitcast.104), channel_id=1, source_target_pairs={{0,64},{4,68},{8,72},{12,76},{16,80},{20,84},{24,88},{28,92},{32,9... | collective-permute-start | bytes 147464 | tf_op jit(solution)/shard_map/ppermute | solution.py:385
  234.3 3.0 %collective-permute-done.29 = f32[16,1,768]{2,1,0:T(1,128)S(1)} collective-permute-done((f32[16,1,768]{2,1,0:T(1,128)S(1)}, f32[16,1,768]{2,1,0:T(1,128)S(1)}, u32[]{:S(2)}, u32[]{:S(2)}) %collective-permute-start.29) | collective-permute-done | bytes 49184 | tf_op jit(solution)/shard_map/ppermute | solution.py:385
  237.4 3.1 %collective-permute-done.28 = f32[16,1,768]{2,1,0:T(1,128)S(1)} collective-permute-done((f32[16,1,768]{2,1,0:T(1,128)S(1)}, f32[16,1,768]{2,1,0:T(1,128)S(1)}, u32[]{:S(2)}, u32[]{:S(2)}) %collective-permute-start.28) | collective-permute-done | bytes 49184 | tf_op jit(solution)/shard_map/ppermute | solution.py:385
  240.5 1.2 collective-permute-done.27
  (85 shorter events, 21.0 us)
Async XLA Ops:
  7.2 59.8 %all-gather.5.cloned.1.call-start = ((), (), s32[]{:S(2)}) async-start(), calls=%async_computation.3 | async-start | bytes 6893568 | tf_op jit(solution)/shard_map/all_gather | solution.py:410
  13.2 109.2 %all-gather.7.cloned.1.call-start = ((), (), s32[]{:S(2)}) async-start(), calls=%async_computation.4 | async-start | bytes 6488064 | tf_op jit(solution)/shard_map/all_gather | solution.py:411
  86.9 1.2 collective-permute-start
  88.2 4.5 %collective-permute-start.3 = (f32[16,1,768]{2,1,0:T(1,128)S(1)}, f32[16,1,768]{2,1,0:T(1,128)S(1)}, u32[]{:S(2)}, u32[]{:S(2)}) collective-permute-start(f32[16,1,768]{2,1,0:T(1,128)S(1)} %add.125), channel_id=1, source_target_pairs={{0,2},{1,3},{2,0},{3,1},{4,6},{5,7},{6,4},{7,5},{8,10},{9,11},{10,... | collective-permute-start | bytes 147464 | tf_op jit(solution)/shard_map/ppermute | solution.py:389
  91.0 3.0 %collective-permute-start.2 = (f32[16,1,768]{2,1,0:T(1,128)S(1)}, f32[16,1,768]{2,1,0:T(1,128)S(1)}, u32[]{:S(2)}, u32[]{:S(2)}) collective-permute-start(f32[16,1,768]{2,1,0:T(1,128)S(1)} %add.125), channel_id=1, source_target_pairs={{0,3},{1,0},{2,1},{3,2},{4,7},{5,4},{6,5},{7,6},{8,11},{9,8},{10,9... | collective-permute-start | bytes 147464 | tf_op jit(solution)/shard_map/ppermute | solution.py:389
  91.8 4.2 %collective-permute-start.1 = (f32[16,1,768]{2,1,0:T(1,128)S(1)}, f32[16,1,768]{2,1,0:T(1,128)S(1)}, u32[]{:S(2)}, u32[]{:S(2)}) collective-permute-start(f32[16,1,768]{2,1,0:T(1,128)S(1)} %add.125), channel_id=1, source_target_pairs={{0,1},{1,2},{2,3},{3,0},{4,5},{5,6},{6,7},{7,4},{8,9},{9,10},{10,1... | collective-permute-start | bytes 147464 | tf_op jit(solution)/shard_map/ppermute | solution.py:389
  96.0 11.1 %collective-permute-start.6 = (f32[16,1,768]{2,1,0:T(1,128)S(1)}, f32[16,1,768]{2,1,0:T(1,128)S(1)}, u32[]{:S(2)}, u32[]{:S(2)}) collective-permute-start(f32[16,1,768]{2,1,0:T(1,128)S(1)} %bitcast.113), channel_id=1, source_target_pairs={{0,16},{4,20},{8,24},{12,28},{16,0},{20,4},{24,8},{28,12},{32,48},... | collective-permute-start | bytes 147464 | tf_op jit(solution)/shard_map/ppermute | solution.py:385
  98.0 9.1 %collective-permute-start.5 = (f32[16,1,768]{2,1,0:T(1,128)S(1)}, f32[16,1,768]{2,1,0:T(1,128)S(1)}, u32[]{:S(2)}, u32[]{:S(2)}) collective-permute-start(f32[16,1,768]{2,1,0:T(1,128)S(1)} %bitcast.114), channel_id=1, source_target_pairs={{0,24},{4,28},{8,0},{12,4},{16,8},{20,12},{24,16},{28,20},{32,56},... | collective-permute-start | bytes 147464 | tf_op jit(solution)/shard_map/ppermute | solution.py:385
  98.9 8.2 %collective-permute-start.4 = (f32[16,1,768]{2,1,0:T(1,128)S(1)}, f32[16,1,768]{2,1,0:T(1,128)S(1)}, u32[]{:S(2)}, u32[]{:S(2)}) collective-permute-start(f32[16,1,768]{2,1,0:T(1,128)S(1)} %bitcast.115), channel_id=1, source_target_pairs={{0,8},{4,12},{8,16},{12,20},{16,24},{20,28},{24,0},{28,4},{32,40},... | collective-permute-start | bytes 147464 | tf_op jit(solution)/shard_map/ppermute | solution.py:385
  99.5 19.0 %all-to-all-start.1 = ((bf16[8,32,512]{2,0,1:T(8,128)(2,1)}), bf16[8,32,512]{2,0,1:T(8,128)(2,1)S(1)}, u32[]{:S(2)}, u32[]{:S(2)}) async-start(bf16[8,32,512]{2,0,1:T(8,128)(2,1)} %bitcast.6), calls=%async_computation.1 | async-start | bytes 524288 | tf_op jit(solution)/shard_map/all_to_all | solution.py:413
  107.1 25.4 %collective-permute-start.9 = (f32[16,1,768]{2,1,0:T(1,128)S(1)}, f32[16,1,768]{2,1,0:T(1,128)S(1)}, u32[]{:S(2)}, u32[]{:S(2)}) collective-permute-start(f32[16,1,768]{2,1,0:T(1,128)S(1)} %bitcast.110), channel_id=1, source_target_pairs={{0,64},{4,68},{8,72},{12,76},{16,80},{20,84},{24,88},{28,92},{32,9... | collective-permute-start | bytes 147464 | tf_op jit(solution)/shard_map/ppermute | solution.py:385
  110.1 22.4 %collective-permute-start.8 = (f32[16,1,768]{2,1,0:T(1,128)S(1)}, f32[16,1,768]{2,1,0:T(1,128)S(1)}, u32[]{:S(2)}, u32[]{:S(2)}) collective-permute-start(f32[16,1,768]{2,1,0:T(1,128)S(1)} %bitcast.111), channel_id=1, source_target_pairs={{0,96},{4,100},{8,104},{12,108},{16,112},{20,116},{24,120},{28,124... | collective-permute-start | bytes 147464 | tf_op jit(solution)/shard_map/ppermute | solution.py:385
  111.0 21.5 %collective-permute-start.7 = (f32[16,1,768]{2,1,0:T(1,128)S(1)}, f32[16,1,768]{2,1,0:T(1,128)S(1)}, u32[]{:S(2)}, u32[]{:S(2)}) collective-permute-start(f32[16,1,768]{2,1,0:T(1,128)S(1)} %bitcast.112), channel_id=1, source_target_pairs={{0,32},{4,36},{8,40},{12,44},{16,48},{20,52},{24,56},{28,60},{32,6... | collective-permute-start | bytes 147464 | tf_op jit(solution)/shard_map/ppermute | solution.py:385
  141.7 62.7 %slice-start = ((s8[12582912]{0:T(1024)(128)(4,1)}), s8[4194304]{0:T(1024)(128)(4,1)S(1)}, s32[]{:S(2)}) async-start(s8[12582912]{0:T(1024)(128)(4,1)} %bitcast.74), calls=%async_computation.5 | async-start | bytes 8388608
  141.8 1.4 collective-permute-start.10
  143.3 5.7 %collective-permute-start.13 = (f32[16,2,768]{2,1,0:T(2,128)S(1)}, f32[16,2,768]{2,1,0:T(2,128)S(1)}, u32[]{:S(2)}, u32[]{:S(2)}) collective-permute-start(f32[16,2,768]{2,1,0:T(2,128)S(1)} %fusion), channel_id=1, source_target_pairs={{0,2},{1,3},{2,0},{3,1},{4,6},{5,7},{6,4},{7,5},{8,10},{9,11},{10,... | collective-permute-start | bytes 294920 | tf_op jit(solution)/shard_map/ppermute | solution.py:389
  145.2 5.1 %collective-permute-start.12 = (f32[16,2,768]{2,1,0:T(2,128)S(1)}, f32[16,2,768]{2,1,0:T(2,128)S(1)}, u32[]{:S(2)}, u32[]{:S(2)}) collective-permute-start(f32[16,2,768]{2,1,0:T(2,128)S(1)} %fusion), channel_id=1, source_target_pairs={{0,3},{1,0},{2,1},{3,2},{4,7},{5,4},{6,5},{7,6},{8,11},{9,8},{10,9... | collective-permute-start | bytes 294920 | tf_op jit(solution)/shard_map/ppermute | solution.py:389
  146.3 4.7 %collective-permute-start.11 = (f32[16,2,768]{2,1,0:T(2,128)S(1)}, f32[16,2,768]{2,1,0:T(2,128)S(1)}, u32[]{:S(2)}, u32[]{:S(2)}) collective-permute-start(f32[16,2,768]{2,1,0:T(2,128)S(1)} %fusion), channel_id=1, source_target_pairs={{0,1},{1,2},{2,3},{3,0},{4,5},{5,6},{6,7},{7,4},{8,9},{9,10},{10,1... | collective-permute-start | bytes 294920 | tf_op jit(solution)/shard_map/ppermute | solution.py:389
  151.2 5.1 %collective-permute-start.16 = (f32[16,2,768]{2,1,0:T(2,128)S(1)}, f32[16,2,768]{2,1,0:T(2,128)S(1)}, u32[]{:S(2)}, u32[]{:S(2)}) collective-permute-start(f32[16,2,768]{2,1,0:T(2,128)S(1)} %add_add_fusion.2), channel_id=1, source_target_pairs={{0,16},{4,20},{8,24},{12,28},{16,0},{20,4},{24,8},{28,12},{32,48},... | collective-permute-start | bytes 294920 | tf_op jit(solution)/shard_map/ppermute | solution.py:385
  153.3 3.5 %collective-permute-start.15 = (f32[16,2,768]{2,1,0:T(2,128)S(1)}, f32[16,2,768]{2,1,0:T(2,128)S(1)}, u32[]{:S(2)}, u32[]{:S(2)}) collective-permute-start(f32[16,2,768]{2,1,0:T(2,128)S(1)} %add_add_fusion.2), channel_id=1, source_target_pairs={{0,24},{4,28},{8,0},{12,4},{16,8},{20,12},{24,16},{28,20},{32,56},... | collective-permute-start | bytes 294920 | tf_op jit(solution)/shard_map/ppermute | solution.py:385
  154.2 5.6 %collective-permute-start.14 = (f32[16,2,768]{2,1,0:T(2,128)S(1)}, f32[16,2,768]{2,1,0:T(2,128)S(1)}, u32[]{:S(2)}, u32[]{:S(2)}) collective-permute-start(f32[16,2,768]{2,1,0:T(2,128)S(1)} %add_add_fusion.2), channel_id=1, source_target_pairs={{0,8},{4,12},{8,16},{12,20},{16,24},{20,28},{24,0},{28,4},{32,40},... | collective-permute-start | bytes 294920 | tf_op jit(solution)/shard_map/ppermute | solution.py:385
  159.8 5.1 %collective-permute-start.19 = (f32[16,2,768]{2,1,0:T(2,128)S(1)}, f32[16,2,768]{2,1,0:T(2,128)S(1)}, u32[]{:S(2)}, u32[]{:S(2)}) collective-permute-start(f32[16,2,768]{2,1,0:T(2,128)S(1)} %bitcast.91), channel_id=1, source_target_pairs={{0,64},{4,68},{8,72},{12,76},{16,80},{20,84},{24,88},{28,92},{32,9... | collective-permute-start | bytes 294920 | tf_op jit(solution)/shard_map/ppermute | solution.py:385
  161.0 3.9 %collective-permute-start.18 = (f32[16,2,768]{2,1,0:T(2,128)S(1)}, f32[16,2,768]{2,1,0:T(2,128)S(1)}, u32[]{:S(2)}, u32[]{:S(2)}) collective-permute-start(f32[16,2,768]{2,1,0:T(2,128)S(1)} %bitcast.92), channel_id=1, source_target_pairs={{0,96},{4,100},{8,104},{12,108},{16,112},{20,116},{24,120},{28,124... | collective-permute-start | bytes 294920 | tf_op jit(solution)/shard_map/ppermute | solution.py:385
  162.5 5.9 %collective-permute-start.17 = (f32[16,2,768]{2,1,0:T(2,128)S(1)}, f32[16,2,768]{2,1,0:T(2,128)S(1)}, u32[]{:S(2)}, u32[]{:S(2)}) collective-permute-start(f32[16,2,768]{2,1,0:T(2,128)S(1)} %bitcast.93), channel_id=1, source_target_pairs={{0,32},{4,36},{8,40},{12,44},{16,48},{20,52},{24,56},{28,60},{32,6... | collective-permute-start | bytes 294920 | tf_op jit(solution)/shard_map/ppermute | solution.py:385
  168.5 35.9 %slice-start.1 = ((s8[12582912]{0:T(1024)(128)(4,1)}), s8[4194304]{0:T(1024)(128)(4,1)S(1)}, s32[]{:S(2)}) async-start(s8[12582912]{0:T(1024)(128)(4,1)} %bitcast.74), calls=%async_computation.6 | async-start | bytes 8388608
  168.5 35.9 %slice-start.2 = ((s8[12582912]{0:T(1024)(128)(4,1)}), s8[4194304]{0:T(1024)(128)(4,1)S(1)}, s32[]{:S(2)}) async-start(s8[12582912]{0:T(1024)(128)(4,1)} %bitcast.74), calls=%async_computation.7 | async-start | bytes 8388608
  181.2 4.1 %collective-permute-start.30 = (f32[16,1,768]{2,1,0:T(1,128)S(1)}, f32[16,1,768]{2,1,0:T(1,128)S(1)}, u32[]{:S(2)}, u32[]{:S(2)}) collective-permute-start(f32[16,1,768]{2,1,0:T(1,128)S(1)} %get-tuple-element.16), channel_id=1, source_target_pairs={{0,4},{4,0},{8,12},{12,8},{16,20},{20,16},{24,28},{28,24},{32,36},... | collective-permute-start | bytes 147464 | tf_op jit(solution)/shard_map/ppermute | solution.py:385
  185.4 4.5 %collective-permute-start.33 = (f32[16,1,768]{2,1,0:T(1,128)S(1)}, f32[16,1,768]{2,1,0:T(1,128)S(1)}, u32[]{:S(2)}, u32[]{:S(2)}) collective-permute-start(f32[16,1,768]{2,1,0:T(1,128)S(1)} %add.156), channel_id=1, source_target_pairs={{0,2},{1,3},{2,0},{3,1},{4,6},{5,7},{6,4},{7,5},{8,10},{9,11},{10,... | collective-permute-start | bytes 147464 | tf_op jit(solution)/shard_map/ppermute | solution.py:389
  186.8 3.4 %collective-permute-start.32 = (f32[16,1,768]{2,1,0:T(1,128)S(1)}, f32[16,1,768]{2,1,0:T(1,128)S(1)}, u32[]{:S(2)}, u32[]{:S(2)}) collective-permute-start(f32[16,1,768]{2,1,0:T(1,128)S(1)} %add.156), channel_id=1, source_target_pairs={{0,3},{1,0},{2,1},{3,2},{4,7},{5,4},{6,5},{7,6},{8,11},{9,8},{10,9... | collective-permute-start | bytes 147464 | tf_op jit(solution)/shard_map/ppermute | solution.py:389
  187.7 4.2 %collective-permute-start.31 = (f32[16,1,768]{2,1,0:T(1,128)S(1)}, f32[16,1,768]{2,1,0:T(1,128)S(1)}, u32[]{:S(2)}, u32[]{:S(2)}) collective-permute-start(f32[16,1,768]{2,1,0:T(1,128)S(1)} %add.156), channel_id=1, source_target_pairs={{0,1},{1,2},{2,3},{3,0},{4,5},{5,6},{6,7},{7,4},{8,9},{9,10},{10,1... | collective-permute-start | bytes 147464 | tf_op jit(solution)/shard_map/ppermute | solution.py:389
  188.2 6.2 %collective-permute-start.20 = (f32[16,1,768]{2,1,0:T(1,128)S(1)}, f32[16,1,768]{2,1,0:T(1,128)S(1)}, u32[]{:S(2)}, u32[]{:S(2)}) collective-permute-start(f32[16,1,768]{2,1,0:T(1,128)S(1)} %get-tuple-element.15), channel_id=1, source_target_pairs={{0,4},{4,0},{8,12},{12,8},{16,20},{20,16},{24,28},{28,24},{32,36},... | collective-permute-start | bytes 147464 | tf_op jit(solution)/shard_map/ppermute | solution.py:385
  191.9 4.6 %collective-permute-start.36 = (f32[16,1,768]{2,1,0:T(1,128)S(1)}, f32[16,1,768]{2,1,0:T(1,128)S(1)}, u32[]{:S(2)}, u32[]{:S(2)}) collective-permute-start(f32[16,1,768]{2,1,0:T(1,128)S(1)} %bitcast.107), channel_id=1, source_target_pairs={{0,16},{4,20},{8,24},{12,28},{16,0},{20,4},{24,8},{28,12},{32,48},... | collective-permute-start | bytes 147464 | tf_op jit(solution)/shard_map/ppermute | solution.py:385
  193.0 3.5 %collective-permute-start.35 = (f32[16,1,768]{2,1,0:T(1,128)S(1)}, f32[16,1,768]{2,1,0:T(1,128)S(1)}, u32[]{:S(2)}, u32[]{:S(2)}) collective-permute-start(f32[16,1,768]{2,1,0:T(1,128)S(1)} %bitcast.108), channel_id=1, source_target_pairs={{0,24},{4,28},{8,0},{12,4},{16,8},{20,12},{24,16},{28,20},{32,56},... | collective-permute-start | bytes 147464 | tf_op jit(solution)/shard_map/ppermute | solution.py:385
  193.8 4.2 %collective-permute-start.34 = (f32[16,1,768]{2,1,0:T(1,128)S(1)}, f32[16,1,768]{2,1,0:T(1,128)S(1)}, u32[]{:S(2)}, u32[]{:S(2)}) collective-permute-start(f32[16,1,768]{2,1,0:T(1,128)S(1)} %bitcast.109), channel_id=1, source_target_pairs={{0,8},{4,12},{8,16},{12,20},{16,24},{20,28},{24,0},{28,4},{32,40},... | collective-permute-start | bytes 147464 | tf_op jit(solution)/shard_map/ppermute | solution.py:385
  194.5 5.4 %collective-permute-start.23 = (f32[16,1,768]{2,1,0:T(1,128)S(1)}, f32[16,1,768]{2,1,0:T(1,128)S(1)}, u32[]{:S(2)}, u32[]{:S(2)}) collective-permute-start(f32[16,1,768]{2,1,0:T(1,128)S(1)} %add.146), channel_id=1, source_target_pairs={{0,2},{1,3},{2,0},{3,1},{4,6},{5,7},{6,4},{7,5},{8,10},{9,11},{10,... | collective-permute-start | bytes 147464 | tf_op jit(solution)/shard_map/ppermute | solution.py:389
  194.9 5.3 %collective-permute-start.22 = (f32[16,1,768]{2,1,0:T(1,128)S(1)}, f32[16,1,768]{2,1,0:T(1,128)S(1)}, u32[]{:S(2)}, u32[]{:S(2)}) collective-permute-start(f32[16,1,768]{2,1,0:T(1,128)S(1)} %add.146), channel_id=1, source_target_pairs={{0,3},{1,0},{2,1},{3,2},{4,7},{5,4},{6,5},{7,6},{8,11},{9,8},{10,9... | collective-permute-start | bytes 147464 | tf_op jit(solution)/shard_map/ppermute | solution.py:389
  196.4 4.4 %collective-permute-start.21 = (f32[16,1,768]{2,1,0:T(1,128)S(1)}, f32[16,1,768]{2,1,0:T(1,128)S(1)}, u32[]{:S(2)}, u32[]{:S(2)}) collective-permute-start(f32[16,1,768]{2,1,0:T(1,128)S(1)} %add.146), channel_id=1, source_target_pairs={{0,1},{1,2},{2,3},{3,0},{4,5},{5,6},{6,7},{7,4},{8,9},{9,10},{10,1... | collective-permute-start | bytes 147464 | tf_op jit(solution)/shard_map/ppermute | solution.py:389
  198.0 5.4 %collective-permute-start.39 = (f32[16,1,768]{2,1,0:T(1,128)S(1)}, f32[16,1,768]{2,1,0:T(1,128)S(1)}, u32[]{:S(2)}, u32[]{:S(2)}) collective-permute-start(f32[16,1,768]{2,1,0:T(1,128)S(1)} %bitcast.101), channel_id=1, source_target_pairs={{0,64},{4,68},{8,72},{12,76},{16,80},{20,84},{24,88},{28,92},{32,9... | collective-permute-start | bytes 147464 | tf_op jit(solution)/shard_map/ppermute | solution.py:385
  198.8 5.5 %collective-permute-start.38 = (f32[16,1,768]{2,1,0:T(1,128)S(1)}, f32[16,1,768]{2,1,0:T(1,128)S(1)}, u32[]{:S(2)}, u32[]{:S(2)}) collective-permute-start(f32[16,1,768]{2,1,0:T(1,128)S(1)} %bitcast.102), channel_id=1, source_target_pairs={{0,96},{4,100},{8,104},{12,108},{16,112},{20,116},{24,120},{28,124... | collective-permute-start | bytes 147464 | tf_op jit(solution)/shard_map/ppermute | solution.py:385
  199.9 4.4 %collective-permute-start.37 = (f32[16,1,768]{2,1,0:T(1,128)S(1)}, f32[16,1,768]{2,1,0:T(1,128)S(1)}, u32[]{:S(2)}, u32[]{:S(2)}) collective-permute-start(f32[16,1,768]{2,1,0:T(1,128)S(1)} %bitcast.103), channel_id=1, source_target_pairs={{0,32},{4,36},{8,40},{12,44},{16,48},{20,52},{24,56},{28,60},{32,6... | collective-permute-start | bytes 147464 | tf_op jit(solution)/shard_map/ppermute | solution.py:385
  200.9 28.9 %collective-permute-start.26 = (f32[16,1,768]{2,1,0:T(1,128)S(1)}, f32[16,1,768]{2,1,0:T(1,128)S(1)}, u32[]{:S(2)}, u32[]{:S(2)}) collective-permute-start(f32[16,1,768]{2,1,0:T(1,128)S(1)} %bitcast.98), channel_id=1, source_target_pairs={{0,16},{4,20},{8,24},{12,28},{16,0},{20,4},{24,8},{28,12},{32,48},... | collective-permute-start | bytes 147464 | tf_op jit(solution)/shard_map/ppermute | solution.py:385
  202.8 27.0 %collective-permute-start.25 = (f32[16,1,768]{2,1,0:T(1,128)S(1)}, f32[16,1,768]{2,1,0:T(1,128)S(1)}, u32[]{:S(2)}, u32[]{:S(2)}) collective-permute-start(f32[16,1,768]{2,1,0:T(1,128)S(1)} %bitcast.99), channel_id=1, source_target_pairs={{0,24},{4,28},{8,0},{12,4},{16,8},{20,12},{24,16},{28,20},{32,56},... | collective-permute-start | bytes 147464 | tf_op jit(solution)/shard_map/ppermute | solution.py:385
  203.4 26.4 %collective-permute-start.24 = (f32[16,1,768]{2,1,0:T(1,128)S(1)}, f32[16,1,768]{2,1,0:T(1,128)S(1)}, u32[]{:S(2)}, u32[]{:S(2)}) collective-permute-start(f32[16,1,768]{2,1,0:T(1,128)S(1)} %bitcast.100), channel_id=1, source_target_pairs={{0,8},{4,12},{8,16},{12,20},{16,24},{20,28},{24,0},{28,4},{32,40},... | collective-permute-start | bytes 147464 | tf_op jit(solution)/shard_map/ppermute | solution.py:385
  204.4 2.8 %copy-start.1 = (bf16[8192,384]{1,0:T(8,128)(2,1)S(1)}, bf16[8192,384]{1,0:T(8,128)(2,1)}, u32[]{:S(2)}) copy-start(bf16[8192,384]{1,0:T(8,128)(2,1)} %all-gather.7.cloned.1.call-done) | copy-start | bytes 18874372
  220.1 22.3 %all-to-all-start.2 = ((f32[32,8,512]{2,1,0:T(8,128)}), f32[32,8,512]{2,1,0:T(8,128)S(1)}, u32[]{:S(2)}, u32[]{:S(2)}) async-start(f32[32,8,512]{2,1,0:T(8,128)} %bitcast.13), calls=%async_computation.2 | async-start | bytes 1048576 | tf_op jit(solution)/shard_map/all_to_all | solution.py:424
  229.9 7.5 %collective-permute-start.29 = (f32[16,1,768]{2,1,0:T(1,128)S(1)}, f32[16,1,768]{2,1,0:T(1,128)S(1)}, u32[]{:S(2)}, u32[]{:S(2)}) collective-permute-start(f32[16,1,768]{2,1,0:T(1,128)S(1)} %bitcast.104), channel_id=1, source_target_pairs={{0,64},{4,68},{8,72},{12,76},{16,80},{20,84},{24,88},{28,92},{32,9... | collective-permute-start | bytes 147464 | tf_op jit(solution)/shard_map/ppermute | solution.py:385
  232.8 7.7 %collective-permute-start.28 = (f32[16,1,768]{2,1,0:T(1,128)S(1)}, f32[16,1,768]{2,1,0:T(1,128)S(1)}, u32[]{:S(2)}, u32[]{:S(2)}) collective-permute-start(f32[16,1,768]{2,1,0:T(1,128)S(1)} %bitcast.105), channel_id=1, source_target_pairs={{0,96},{4,100},{8,104},{12,108},{16,112},{20,116},{24,120},{28,124... | collective-permute-start | bytes 147464 | tf_op jit(solution)/shard_map/ppermute | solution.py:385
  233.7 8.0 %collective-permute-start.27 = (f32[16,1,768]{2,1,0:T(1,128)S(1)}, f32[16,1,768]{2,1,0:T(1,128)S(1)}, u32[]{:S(2)}, u32[]{:S(2)}) collective-permute-start(f32[16,1,768]{2,1,0:T(1,128)S(1)} %bitcast.106), channel_id=1, source_target_pairs={{0,32},{4,36},{8,40},{12,44},{16,48},{20,52},{24,56},{28,60},{32,6... | collective-permute-start | bytes 147464 | tf_op jit(solution)/shard_map/ppermute | solution.py:385
  (3 other events, 5.2 us)
Sparse Core Ops, SparseCore 0:
  13.3 53.5 all-gather.4
  69.2 53.1 all-gather.6

commit v2 on v0

v2 whole, which is shorter than its diff:
```python
import functools

import jax
import jax.numpy as jnp
from jax import lax
from jax.experimental import pallas as pl
from jax.experimental.pallas import tpu as pltpu
from jax.sharding import Mesh
from jax.sharding import PartitionSpec as P

PATCH = 256
SWEEPS = 3
EXTRA = 16
LOG2E = 1.4426950408889634
ROWS = 64
SURE = 192
WIDE = 256
PER = 3
TALL = 32
LANES = 128
SHIFTS = (1, 3, 2)
SIDE = 4
GROUP = ("z", "c", "x")

teacher_temp = 0.07
student_temp = 0.1
loss_scale = 65536.0

f32 = jnp.float32
bf16 = jnp.bfloat16

VM = pl.BlockSpec(memory_space=pltpu.VMEM)
SM = pl.BlockSpec(memory_space=pltpu.SMEM)
ANY = pl.BlockSpec(memory_space=pl.ANY)


def params(mib):
    return pltpu.CompilerParams(vmem_limit_bytes=mib * 1024 * 1024)


def pinned(array):
    return pltpu.with_memory_space_constraint(array, pltpu.VMEM)


def shape(dims, dtype=f32):
    return jax.ShapeDtypeStruct(dims, dtype)


def nn(a, b):
    return lax.dot_general(a, b, (((1,), (0,)), ((), ())), preferred_element_type=f32)


def tn(a, b):
    return lax.dot_general(a, b, (((0,), (0,)), ((), ())), preferred_element_type=f32)


def tokens_kernel(me_ref, count_ref, index_ref, teacher_ref, student_ref, tp_ref, sp_ref,
                  t_out, s_out, w_out, info_out, feats, protos, sems, p_sems):
    proto_copies = [
        pltpu.make_async_copy(ref, protos.at[i], p_sems.at[i])
        for i, ref in enumerate((tp_ref, sp_ref))
    ]
    copies = [
        pltpu.make_async_copy(ref, feats.at[i], sems.at[i])
        for i, ref in enumerate((teacher_ref, student_ref))
    ]
    for c in proto_copies + copies:
        c.start()
    me = me_ref[0]
    z, y, core = me >> 3, (me >> 1) & 3, me & 1
    info_out[0] = z
    info_out[1] = core
    slots = index_ref.shape[0]
    source, d = feats.shape[1:]
    index_row = index_ref[...].reshape(1, slots)
    index_col = jnp.transpose(jnp.broadcast_to(index_row, (8, slots)))[:, 0:1]
    count = count_ref[0]
    live_row = lax.broadcasted_iota(jnp.int32, (1, slots), 1) < count
    live_col = lax.broadcasted_iota(jnp.int32, (slots, 1), 0) < count
    same = ((index_col >> 8) == (index_row >> 8)) & live_col
    own = jnp.sum(jnp.where(same, 1.0, 0.0), axis=0, keepdims=True)
    own = jnp.where(live_row, own, 0.0)
    rest = jnp.concatenate([own[:, d:], jnp.zeros((1, 2 * d - slots), f32)], axis=1)
    at = lax.broadcasted_iota(jnp.int32, (EXTRA, d), 0)
    counts = jnp.where(at == 0, own[:, 0:d], jnp.where(at == 1, rest, 0.0))
    t_out[slots : slots + EXTRA, :] = counts.astype(bf16)
    pick = jnp.where(
        lax.broadcasted_iota(jnp.int32, (slots, source), 1) == index_col, 1.0, 0.0
    ).astype(bf16)
    to = lax.broadcasted_iota(jnp.int32, (1, d), 1)
    turn = to >> 6
    shift = jnp.where(turn == 2, 3, jnp.where(turn == 3, 2, turn))
    origin = (
        ((to >> 4) & 3) * 64 + ((y + 4 - shift) & 3) * 16 + ((to >> 3) & 1) * 8 + (to & 7)
    )
    order = jnp.where(
        lax.broadcasted_iota(jnp.int32, (d, d), 0) == origin, 1.0, 0.0
    ).astype(bf16)
    for c in proto_copies:
        c.wait()
    parts, _, width = w_out.shape
    for q in range(parts):
        lanes = slice(q * width, (q + 1) * width)
        w_out[q] = jnp.concatenate(
            [protos[0, :, lanes].astype(f32), protos[1, :, lanes].astype(f32)], axis=0
        ).astype(bf16)
    for i, out in enumerate((t_out, s_out)):
        copies[i].wait()
        rows = nn(pick, feats[i])
        unit = rows * lax.rsqrt(jnp.sum(rows * rows, axis=1, keepdims=True) + 1e-06)
        out[0:slots, :] = nn(unit.astype(bf16), order).astype(bf16)


def tokens(me, count, index, teacher_feat, student_feat, teacher_proto, student_proto):
    slots, (source, d) = index.shape[0], teacher_feat.shape
    rows, cols = teacher_proto.shape
    parts = 8
    return pl.pallas_call(
        tokens_kernel,
        out_shape=(
            shape((slots + EXTRA, d), bf16),
            shape((slots, d), bf16),
            shape((parts, 2 * rows, cols // parts), bf16),
            shape((2,), jnp.int32),
        ),
        in_specs=[SM, SM, VM, ANY, ANY, ANY, ANY],
        out_specs=(VM, VM, VM, SM),
        scratch_shapes=[
            pltpu.VMEM((2, source, d), bf16),
            pltpu.VMEM((2, rows, cols), bf16),
            pltpu.SemaphoreType.DMA((2,)),
            pltpu.SemaphoreType.DMA((2,)),
        ],
        compiler_params=params(56),
        name="token_rows",
    )(me, count, index, teacher_feat, student_feat, teacher_proto, student_proto)


def split_kernel(which, w_ref, tok_ref, *refs):
    out, tok_out = refs[-2:]
    parts, rows, width = w_ref.shape
    out[...] = (
        w_ref[...].astype(f32)[:, 8 * which : 8 * which + 8]
        .reshape(parts * 8, width)
        .astype(bf16)
    )
    tok_out[...] = tok_ref[...]


def split(which, w, tok, after=()):
    parts, rows, width = w.shape
    return pl.pallas_call(
        functools.partial(split_kernel, which),
        out_shape=(shape((parts * rows // 2, width), bf16), shape(tok.shape, bf16)),
        in_specs=[VM, VM] + [ANY] * len(after),
        out_specs=(VM, VM),
        compiler_params=params(16),
        name="split_rows",
    )(w, tok, *after)


def token_copies(info_ref, refs, dst, sems):
    z, core = info_ref[0], info_ref[1]
    copies = []
    for a, ref in enumerate(refs):
        k = (0,) + SHIFTS
        at = ((z + 4 - k[a % 4]) & 3) * 2 + (core if a < 4 else 1 - core)
        copies.append(
            pltpu.make_async_copy(ref, dst.at[at], sems.at[a])
        )
    return copies


def weight_copies(refs, dst, sems):
    rows = refs[0].shape[0]
    return [
        pltpu.make_async_copy(ref, dst.at[pl.ds(i * rows, rows)], sems.at[i])
        for i, ref in enumerate(refs)
    ]


def inverse_norms(w_ref):
    wide = w_ref[...].astype(f32)
    return lax.rsqrt(jnp.sum(wide * wide, axis=0, keepdims=True) + 1e-06)


def down(rows):
    return jnp.concatenate(
        [
            jnp.transpose(jnp.broadcast_to(rows[j : j + 1, :], (LANES, LANES)))
            for j in range(rows.shape[0])
        ],
        axis=0,
    )


def across(parts_ref):
    return jnp.concatenate(
        [
            jnp.sum(jnp.transpose(parts_ref[j : j + LANES, :]), axis=0, keepdims=True)
            for j in range(0, parts_ref.shape[0], LANES)
        ],
        axis=0,
    )


def vector(ref, b, first=0):
    return ref[pl.ds(first + PER * b, PER), :]


def added(parts_ref):
    total = parts_ref[0].astype(f32)
    for i in range(1, parts_ref.shape[0]):
        total = total + parts_ref[i].astype(f32)
    return total


def live_of(own):
    return jnp.where(own > 0.0, 1.0, 0.0)


def column_factor(refs):
    total = refs[0][...]
    for ref in refs[1:]:
        total = total + ref[...]
    return 1.0 / total


def chunks(n, size):
    return [slice(at, at + size) for at in range(0, n, size)]


def energy_kernel(info_ref, *refs):
    toks, w_refs = refs[0:8], refs[8:12]
    e_ref, own_ref, sum_ref, u, w, live, acc, t_sems, w_sems = refs[-9:]
    blocks, slots, cols = e_ref.shape
    t_copies = token_copies(info_ref, toks, u, t_sems)
    w_copies = weight_copies(w_refs, w, w_sems)
    for c in t_copies + w_copies:
        c.start()
    for c in w_copies:
        c.wait()
    scale = inverse_norms(w) * (LOG2E / teacher_temp)
    acc[...] = jnp.zeros_like(acc)
    own_ref[...] = jnp.zeros_like(own_ref)
    for c in t_copies:
        c.wait()

    def step(b, _):
        counts = u[b, slots : slots + EXTRA, :].astype(f32)
        for j in range(PER):
            row, lane = divmod(j * LANES, counts.shape[1])
            own_ref[pl.ds(PER * b + j, 1), :] = counts[row : row + 1, lane : lane + LANES]
        live[...] = down(live_of(vector(own_ref, b)))
        for n in chunks(cols, WIDE):
            raw = nn(u[b, 0:slots, :], w[:, n])
            for i in range(0, WIDE, LANES):
                k = slice(n.start + i, n.start + i + LANES)
                total = acc[:, k]
                for r in chunks(slots, ROWS):
                    energy = jnp.exp2(raw[r, i : i + LANES] * scale[:, k])
                    e_ref[b, r, k] = energy.astype(bf16)
                    total = total + (energy * live[r, :] if r.stop > SURE else energy)
                acc[:, k] = total
        return 0

    lax.fori_loop(0, blocks, step, 0)
    sum_ref[...] = jnp.sum(acc[...], axis=0, keepdims=True)


def energy_pass(info, toks, w_parts, slots, after):
    d, cols = SIDE * w_parts[0].shape[0], w_parts[0].shape[1]
    blocks = len(toks)
    return pl.pallas_call(
        energy_kernel,
        out_shape=(
            pltpu.VMEM((blocks, slots, cols), bf16),
            shape((TALL, LANES)),
            shape((1, cols)),
        ),
        in_specs=[SM] + [ANY] * (blocks + len(w_parts) + len(after)),
        out_specs=(VM, VM, VM),
        scratch_shapes=[
            pltpu.VMEM((blocks, slots + EXTRA, d), bf16),
            pltpu.VMEM((d, cols), bf16),
            pltpu.VMEM((slots, LANES), f32),
            pltpu.VMEM((ROWS, cols), f32),
            pltpu.SemaphoreType.DMA((blocks,)),
            pltpu.SemaphoreType.DMA((len(w_parts),)),
        ],
        compiler_params=params(16),
        cost_estimate=pl.CostEstimate(
            flops=2 * blocks * slots * cols * d,
            transcendentals=blocks * slots * cols,
            bytes_accessed=2 * blocks * slots * cols,
        ),
        name="energy_pass",
    )(info, *toks, *w_parts, *after)


def row_kernel(*refs):
    sums, (e, *_, out_ref, part, rows) = refs[0:SIDE], refs[SIDE:]
    blocks, slots, cols = e.shape
    c = column_factor(sums)
    rows[...] = jnp.zeros_like(rows)

    def step(b, _):
        for r in chunks(slots, ROWS):
            total = jnp.zeros((ROWS, LANES), f32)
            for k in chunks(cols, LANES):
                total = total + e[b, r, k].astype(f32) * c[:, k]
            part[r, :] = total
        rows[pl.ds(PER * b, PER), :] = across(part)
        return 0

    lax.fori_loop(0, blocks, step, 0)
    low = rows[...].astype(bf16)
    for i in range(out_ref.shape[0]):
        out_ref[i] = low


def row_pass(sums, energy, peers, after=()):
    blocks, slots, cols = energy.shape
    return pl.pallas_call(
        row_kernel,
        out_shape=shape((peers, TALL, LANES), bf16),
        in_specs=[VM] * (SIDE + 1) + [ANY] * len(after),
        out_specs=VM,
        scratch_shapes=[
            pltpu.VMEM((slots, LANES), f32),
            pltpu.VMEM((TALL, LANES), f32),
        ],
        compiler_params=params(8),
        name="row_pass",
    )(*sums, pinned(energy), *after)


def column_kernel(rows_ref, own_ref, e, out_ref, weight, ratio, acc):
    blocks, slots, cols = e.shape
    acc[...] = jnp.zeros_like(acc)
    own = own_ref[...]
    ratio[...] = live_of(own) / jnp.where(own > 0.0, added(rows_ref), 1.0)

    def step(b, _):
        weight[...] = down(vector(ratio, b))
        for k in chunks(cols, LANES):
            total = acc[:, k]
            for r in chunks(slots, ROWS):
                total = total + e[b, r, k].astype(f32) * weight[r, :]
            acc[:, k] = total
        return 0

    lax.fori_loop(0, blocks, step, 0)
    out_ref[...] = jnp.sum(acc[...], axis=0, keepdims=True)


def column_pass(rows, own, energy):
    blocks, slots, cols = energy.shape
    return pl.pallas_call(
        column_kernel,
        out_shape=shape((1, cols)),
        in_specs=[VM, VM, VM],
        out_specs=VM,
        scratch_shapes=[
            pltpu.VMEM((slots, LANES), f32),
            pltpu.VMEM((TALL, LANES), f32),
            pltpu.VMEM((ROWS, cols), f32),
        ],
        compiler_params=params(8),
        name="column_pass",
    )(rows, own, pinned(energy))


def closing_kernel(info_ref, *refs):
    toks, w_refs, sums = refs[0:8], refs[8:12], refs[12 : 12 + SIDE]
    e, u, ut, w, out_ref, part, rows, crosses, t_sems, w_sems = refs[12 + SIDE :]
    blocks, slots, cols = e.shape
    t_copies = token_copies(info_ref, toks, u, t_sems)
    w_copies = weight_copies(w_refs, w, w_sems)
    for copy in w_copies + t_copies:
        copy.start()
    c = column_factor(sums)
    for copy in w_copies + t_copies:
        copy.wait()
    scale = inverse_norms(w) * (LOG2E / student_temp)
    rows[...] = jnp.zeros_like(rows)

    def step(b, _):
        ut[b] = jnp.transpose(u[b].astype(f32)).astype(bf16)
        for tall in chunks(slots, LANES):
            raw = nn(u[b, tall, :], w[...])
            for at in chunks(LANES, ROWS):
                r = slice(tall.start + at.start, tall.start + at.stop)
                mass = jnp.zeros((ROWS, LANES), f32)
                cross = jnp.zeros((ROWS, LANES), f32)
                total = jnp.zeros((ROWS, LANES), f32)
                for k in chunks(cols, LANES):
                    power = raw[at, k] * scale[:, k]
                    total = total + jnp.exp2(power)
                    energy = e[b, r, k].astype(f32) * c[:, k]
                    mass = mass + energy
                    cross = cross + energy * power
                part[0, r, :] = mass
                part[1, r, :] = total
                part[2, r, :] = cross
        rows[pl.ds(PER * b, PER), :] = across(part.at[0])
        rows[pl.ds(PER * (blocks + b), PER), :] = across(part.at[1])
        crosses[b, 0:PER, :] = across(part.at[2]) * (1.0 / LOG2E)
        return 0

    lax.fori_loop(0, blocks, step, 0)
    at = 2 * PER * blocks
    for i in range(out_ref.shape[0]):
        rows[at : at + PER, :] = crosses[i // 4, 0:PER, :]
        out_ref[i] = rows[...].astype(bf16)


def closing_pass(info, toks, w_parts, sums, energy, peers):
    blocks, slots, cols = energy.shape
    d = SIDE * w_parts[0].shape[0]
    return pl.pallas_call(
        closing_kernel,
        out_shape=(
            pltpu.VMEM((blocks, slots, d), bf16),
            pltpu.VMEM((blocks, d, slots), bf16),
            pltpu.VMEM((d, cols), bf16),
            shape((peers, 2 * TALL, LANES), bf16),
        ),
        in_specs=[SM] + [ANY] * (blocks + len(w_parts)) + [VM] * (SIDE + 1),
        out_specs=(VM, VM, VM, VM),
        scratch_shapes=[
            pltpu.VMEM((3, slots, LANES), f32),
            pltpu.VMEM((2 * TALL, LANES), f32),
            pltpu.VMEM((blocks, 8, LANES), f32),
            pltpu.SemaphoreType.DMA((blocks,)),
            pltpu.SemaphoreType.DMA((len(w_parts),)),
        ],
        compiler_params=params(16),
        name="closing_pass",
    )(info, *toks, *w_parts, *sums, pinned(energy))


def grad_kernel(images, info_ref, rows_ref, own_ref, *refs):
    sums = refs[0:SIDE]
    (u, ut, w, e, keep_ref, *sends, loss_ref, soft_w, mass_w, acc, totals, soft_all,
     mass_all) = refs[SIDE:]
    blocks, slots, cols = e.shape
    totals[...] = added(rows_ref)
    own = own_ref[...]
    n = PER * blocks
    me = info_ref[0] * 2 + info_ref[1]
    mine = jnp.log(vector(totals, me, n)) - vector(totals, 0, 2 * n) / vector(totals, me)
    loss_ref[...] = jnp.where(vector(own_ref, me) > 0.0, mine, 0.0)
    weight = live_of(own) / (jnp.maximum(own, 1.0) * images) * (loss_scale / student_temp)
    soft_all[0:n, :] = weight[0:n] / totals[n : 2 * n, :]
    mass_all[0:n, :] = weight[0:n] / totals[0:n, :]
    c = column_factor(sums)
    inv = inverse_norms(w)
    scale = inv * (LOG2E / student_temp)
    acc[...] = jnp.zeros_like(acc)

    def step(s, _):
        for half in range(2):
            at = slice(half * slots, (half + 1) * slots)
            soft_w[at, :] = down(vector(soft_all, 2 * s + half))
            mass_w[at, :] = down(vector(mass_all, 2 * s + half))
        units = jnp.concatenate([ut[2 * s], ut[2 * s + 1]], axis=1)
        for n in chunks(cols, WIDE):
            raws = [nn(u[2 * s + half], w[:, n]) for half in range(2)]
            columns = []
            for i in range(0, WIDE, LANES):
                k = slice(n.start + i, n.start + i + LANES)
                parts = []
                for half in range(2):
                    b = 2 * s + half
                    for r in chunks(slots, ROWS):
                        at = slice(half * slots + r.start, half * slots + r.stop)
                        power = raws[half][r, i : i + LANES] * scale[:, k]
                        soft = jnp.exp2(power) * soft_w[at, :]
                        target = e[b, r, k].astype(f32) * c[:, k] * mass_w[at, :]
                        parts.append((soft - target).astype(bf16))
                columns.append(jnp.concatenate(parts, axis=0))
            acc[:, n] += nn(units, jnp.concatenate(columns, axis=1))
        return 0

    lax.fori_loop(0, blocks // 2, step, 0)
    grad = acc[...]
    unit = w[...].astype(f32) * inv
    dot = jnp.sum(grad * unit, axis=0, keepdims=True)
    acc[...] = inv * (grad - unit * dot)
    rows = keep_ref.shape[0]
    keep_ref[...] = acc[0:rows, :]
    for i, ref in enumerate(sends):
        ref[...] = acc[(i + 1) * rows : (i + 2) * rows, :].astype(bf16)


def grad_pass(images, info, rows, own, sums, u, ut, w, energy):
    blocks, slots, cols = energy.shape
    d = ut.shape[1]
    part = (d // SIDE, cols)
    return pl.pallas_call(
        functools.partial(grad_kernel, float(images)),
        out_shape=(shape(part), *[shape(part, bf16)] * len(SHIFTS), shape((PER, LANES))),
        in_specs=[SM] + [VM] * (SIDE + 6),
        out_specs=(VM,) * 5,
        scratch_shapes=[
            pltpu.VMEM((2 * slots, LANES), f32),
            pltpu.VMEM((2 * slots, LANES), f32),
            pltpu.VMEM((d, cols), f32),
            pltpu.VMEM(rows.shape[1:], f32),
            pltpu.VMEM((TALL, LANES), f32),
            pltpu.VMEM((TALL, LANES), f32),
        ],
        compiler_params=params(16),
        name="grad_pass",
    )(info, rows, own, *sums, u, ut, w, pinned(energy))


def shift(value, axis, k):
    n = lax.axis_size(axis)
    return lax.ppermute(value, axis, [(i, (i + k) % n) for i in range(n)])


def exchange(value, axes):
    return lax.all_to_all(value, axes, 0, 0, tiled=True)


def ring(value, axis):
    return [value] + [shift(value, axis, k) for k in SHIFTS]


def both_cores(blocks):
    return blocks + [shift(b, "c", 1) for b in blocks]


def local(teacher_feat, student_feat, teacher_proto, student_proto, mask_index, mask_count):
    slots = mask_index.shape[0]
    images = lax.axis_size(("z", "y", "c")) * (teacher_feat.shape[0] // PATCH)
    peers = lax.axis_size(GROUP)
    me = lax.axis_index(("z", "y", "c")).reshape(1)
    t_tok, s_tok, w, info = tokens(
        me, mask_count, mask_index, teacher_feat, student_feat, teacher_proto, student_proto
    )
    w = exchange(w, ("z", "c"))
    s_toks = ring(s_tok, "z")
    t_w, t_tok = split(0, w, t_tok, s_toks)
    t_parts = ring(t_w, "y")
    t_toks = both_cores(ring(t_tok, "z"))
    s_toks = both_cores(s_toks)
    s_w, _ = split(1, w, s_tok, t_parts)
    s_parts = ring(s_w, "y")
    energy, own, sums = energy_pass(info, t_toks, t_parts, slots, [s_w, *s_toks])
    for i in range(SWEEPS - 1):
        after = s_parts if i == 0 else []
        rows = exchange(row_pass(ring(sums, "y"), energy, peers, after), GROUP)
        sums = column_pass(rows, own, energy)
    sums = ring(sums, "y")
    s_u, s_ut, s_w, rows = closing_pass(info, s_toks, s_parts, sums, energy, peers)
    rows = exchange(rows, GROUP)
    keep, *sends, loss = grad_pass(images, info, rows, own, sums, s_u, s_ut, s_w, energy)
    for k, send in zip(SHIFTS, sends):
        keep = keep + shift(send, "y", -k).astype(f32)
    proto_grad = lax.all_to_all(keep, ("z", "c"), 0, 1, tiled=True)
    return (loss.reshape(-1), proto_grad)


def solution(mesh):
    parts = Mesh(mesh.devices.reshape(4, 4, 2, 4), ("z", "y", "c", "x"))
    dp = ("z", "y", "c")
    return jax.shard_map(
        local,
        mesh=parts,
        in_specs=(P(dp, None), P(dp, None), P(dp, "x"), P(dp, "x"), P(dp), P(dp)),
        out_specs=(P(dp), P(dp, "x")),
        check_vma=False,
    )
```

time: 794 us -> 205 us (0.26)
  waiting for transfers between devices: 531 us -> 40.8 us
  matrix products: 159 us -> 0 us
  Pallas kernels: 0 us -> 55.9 us
  other arithmetic: 43.2 us -> 0.13 us
  starting transfers between devices: 1.13 us -> 40 us
  blocking collectives: 31.9 us -> 63.5 us
  between operations: 15.2 us -> 1.4 us
    psum x4 -> x0, waiting for transfers between devices: 340 us -> none  [the longest x3 266 us: local(): lax.psum(values, 'dp')]
    dot_general x9 -> x0, matrix products: 159 us -> none  [the longest x2 47.4 us: head_core(): scale_r = live_rows / row_total(jnp.dot(energy, scale_c, precision=precise))]
    reduce_scatter x1 -> x0, waiting for transfers between devices: 116 us -> none  [local(): lax.psum_scatter(contract_rows(student_unit, grad_bf), 'dp', scatter_dime...]
    all_gather x2 -> x0, waiting for transfers between devices: 72.8 us -> none  [the longest x1 51.2 us: local(): teacher_piece = lax.all_gather(teacher_proto, 'dp', axis=0, tiled=True)]
    all_to_all x0 -> x4, blocking collectives: none -> 63.5 us  [the longest x3 49.7 us: exchange(): return lax.all_to_all(value, axes, 0, 0, tiled=True)]
    pallas_call x0 -> x10, Pallas kernels: none -> 55.9 us  [the longest x1 15 us: closing_pass(): pl.pallas_call(closing_kernel, out_shape=(pltpu.VMEM((blocks, slots, d),...]
    ppermute x0 -> x32, waiting for transfers between devices: none -> 40.8 us  [shift(): return lax.ppermute(value, axis, [(i, (i + k) % n) for i in range(n)])]
    reduce_sum x7 -> x0, other arithmetic: 37.3 us -> none  [the longest x1 26.6 us: head_core(): dot_part = jnp.sum(grad_bf.astype(jnp.float32) * cosine, axis=0)]
  transfers between devices with their start and end apart: 7 -> 33, of which waited for: 7 -> 16; matrix products, arithmetic and copies ran while one was open for 9% -> 0% of each run, Pallas kernels for 0% -> 5%
where the time goes in v2:
time: 205 us; the launch traced here: 204 us
  blocking collectives  63.5 us (31%)
  Pallas kernels  55.9 us (27%)
  waiting for transfers between devices  40.8 us (20%)
  starting transfers between devices  40 us (20%)
  local copies, waits for them, and re-layouts  2.66 us (1%)
    all_to_all x3, blocking collectives, exchange(): return lax.all_to_all(value, axes, 0, 0, tiled=True)  49.7 us
    ppermute x32, waiting for transfers between devices, shift(): return lax.ppermute(value, axis, [(i, (i + k) % n) for i in range(n)])  40.8 us
    ppermute x32, starting transfers between devices, shift(): return lax.ppermute(value, axis, [(i, (i + k) % n) for i in range(n)])  33.2 us
    pallas_call x1, Pallas kernels, closing_pass(): pl.pallas_call(closing_kernel, out_shape=(pltpu.VMEM((blocks, slots, d),...  15 us
    all_to_all x1, blocking collectives, local(): proto_grad = lax.all_to_all(keep, ('z', 'c'), 0, 1, tiled=True)  13.8 us
    pallas_call x1, Pallas kernels, grad_pass(): pl.pallas_call(functools.partial(grad_kernel, float(images)), out_shape=(...  11.7 us
    pallas_call x1, Pallas kernels, energy_pass(): pl.pallas_call(energy_kernel, out_shape=(pltpu.VMEM((blocks, slots, cols)...  9.92 us
    all_to_all x1, starting transfers between devices, exchange(): return lax.all_to_all(value, axes, 0, 0, tiled=True)  6.83 us
  transfers between devices with their start and end apart: 33, of which 16 were waited for; matrix products, arithmetic and copies ran while one was open for 0% of the time, Pallas kernels for 5%

profile of v2, /device:TPU:1, one launch (start us, length us, event | category | flops | bytes accessed | tf_op | source)
XLA Modules:
  0.0 204.3 jit_solution(9761084105579167789)
XLA Ops:
  1.3 5.6 %token_rows.1 = (bf16[400,256]{1,0:T(8,128)(2,1)}, bf16[384,256]{1,0:T(8,128)(2,1)}, bf16[8,16,2048]{2,1,0:T(8,128)(2,1)}, s32[2]{0:T(128)}) custom-call(s32[1]{0:T(128)} %bitcast.me_ref, s32[1]{0:T(128)S(6)} %copy.9.count_ref, s32[384]{0:T(512)} %index_ref.1, bf16[2048,256]{1,0:T(8,128)(2,1)} %teacher_ref.1, bf16[2048,256]{1,0:T(8,128)(2,1)} %student_ref.1, ...), custom_call_target="tpu_custom_call" | custom-call | tf_op jit(solution)/shard_map/token_rows/pallas_call | solution.py:118
  6.9 6.8 %all-to-all-start = ((bf16[8,16,2048]{2,1,0:T(8,128)(2,1)}), bf16[8,16,2048]{2,1,0:T(8,128)(2,1)S(1)}, u32[]{:S(2)}, u32[]{:S(2)}) async-start(bf16[8,16,2048]{2,1,0:T(8,128)(2,1)} %get-tuple-element.23), calls=%async_computation | async-start | bytes 1048576 | tf_op jit(solution)/shard_map/all_to_all | solution.py:525
  13.7 2.9 %collective-permute-start.2 = (bf16[384,256]{1,0:T(8,128)(2,1)}, bf16[384,256]{1,0:T(8,128)(2,1)S(1)}, u32[]{:S(2)}, u32[]{:S(2)}) collective-permute-start(bf16[384,256]{1,0:T(8,128)(2,1)} %get-tuple-element.22.refs_0_.tok_ref.refs_13_), channel_id=1, source_target_pairs={{0,64},{32,96},{64,0},{96,32},{1,65},{33,97},{65,1},{97,33},{2,66}... | collective-permute-start | bytes 589832 | tf_op jit(solution)/shard_map/ppermute | solution.py:521
  16.6 0.9 collective-permute-start.1
  18.1 1.2 collective-permute-start.3
  19.3 8.2 %collective-permute-done.2.refs_3_.refs_16_ = bf16[384,256]{1,0:T(8,128)(2,1)S(1)} collective-permute-done((bf16[384,256]{1,0:T(8,128)(2,1)}, bf16[384,256]{1,0:T(8,128)(2,1)S(1)}, u32[]{:S(2)}, u32[]{:S(2)}) %collective-permute-start.2) | collective-permute-done | bytes 196640 | tf_op jit(solution)/shard_map/ppermute | solution.py:521
  27.5 1.3 collective-permute-start.6
  28.8 1.4 collective-permute-done.1.refs_2_.refs_15_
  30.2 1.7 collective-permute-done.refs_1_.refs_14_
  31.9 0.9 copy-done
  32.8 0.9 copy-done.2
  33.8 0.8 collective-permute-start.15
  34.6 1.2 collective-permute-start.5
  35.7 2.9 %collective-permute-start.9 = (bf16[64,2048]{1,0:T(8,128)(2,1)S(1)}, bf16[64,2048]{1,0:T(8,128)(2,1)S(1)}, u32[]{:S(2)}, u32[]{:S(2)}) collective-permute-start(bf16[64,2048]{1,0:T(8,128)(2,1)S(1)} %get-tuple-element.25.refs_0_.refs_8_), channel_id=1, source_target_pairs={{0,16},{8,24},{16,0},{24,8},{1,17},{9,25},{17,1},{25,9},{2,18},{10... | collective-permute-start | bytes 786440 | tf_op jit(solution)/shard_map/ppermute | solution.py:521
  38.6 0.8 collective-permute-start.8
  40.1 1.1 collective-permute-start.14
  41.6 4.3 %collective-permute-done.14.refs_2_ = bf16[400,256]{1,0:T(8,128)(2,1)S(1)} collective-permute-done((bf16[400,256]{1,0:T(8,128)(2,1)S(1)}, bf16[400,256]{1,0:T(8,128)(2,1)S(1)}, u32[]{:S(2)}, u32[]{:S(2)}) %collective-permute-start.14) | collective-permute-done | bytes 204832 | tf_op jit(solution)/shard_map/ppermute | solution.py:521
  45.9 1.7 collective-permute-start.16
  47.7 2.4 %collective-permute-start.19 = (bf16[400,256]{1,0:T(8,128)(2,1)S(1)}, bf16[400,256]{1,0:T(8,128)(2,1)S(1)}, u32[]{:S(2)}, u32[]{:S(2)}) collective-permute-start(bf16[400,256]{1,0:T(8,128)(2,1)S(1)} %collective-permute-done.15.refs_3_), channel_id=1, source_target_pairs={{0,4},{4,0},{1,5},{5,1},{2,6},{6,2},{3,7},{7,3},{8,12},{12,8},{9,1... | collective-permute-start | bytes 614408 | tf_op jit(solution)/shard_map/ppermute | solution.py:521
  50.1 1.1 collective-permute-done.8.refs_2_.refs_10_
  51.2 0.8 collective-permute-start.17
  53.4 2.2 %collective-permute-start.12 = (bf16[64,2048]{1,0:T(8,128)(2,1)S(1)}, bf16[64,2048]{1,0:T(8,128)(2,1)S(1)}, u32[]{:S(2)}, u32[]{:S(2)}) collective-permute-start(bf16[64,2048]{1,0:T(8,128)(2,1)S(1)} %get-tuple-element.26.refs_12_.refs_5_.refs_8_), channel_id=1, source_target_pairs={{0,16},{8,24},{16,0},{24,8},{1,17},{9,25},{17,1},{25,9},{2,18},{10... | collective-permute-start | bytes 786440 | tf_op jit(solution)/shard_map/ppermute | solution.py:521
  55.6 1.1 collective-permute-start.11
  57.1 9.9 %energy_pass.1 = (bf16[8,384,2048]{2,1,0:T(8,128)(2,1)S(1)}, f32[32,128]{1,0:T(8,128)S(1)}, f32[1,2048]{1,0:T(1,128)S(1)}) custom-call(s32[2]{0:T(128)S(1)} %copy-done.3, bf16[400,256]{1,0:T(8,128)(2,1)S(1)} %get-tuple-element.27.refs_0_, bf16[400,256]{1,0:T(8,128)(2,1)S(1)} %collective-permute-done.13.refs_1_, ...), custom_call_target="tpu_custom_call" | custom-call | flops 3221225472 | bytes 12582912 | tf_op jit(solution)/shard_map/energy_pass/pallas_call | solution.py:274
  67.0 1.2 collective-permute-start.22
  68.2 2.1 %collective-permute-start.21 = (f32[1,2048]{1,0:T(1,128)S(1)}, f32[1,2048]{1,0:T(1,128)S(1)}, u32[]{:S(2)}, u32[]{:S(2)}) collective-permute-start(f32[1,2048]{1,0:T(1,128)S(1)} %get-tuple-element.28.refs_0_), channel_id=1, source_target_pairs={{0,24},{8,0},{16,8},{24,16},{1,25},{9,1},{17,9},{25,17},{2,26},{10... | collective-permute-start | bytes 24584 | tf_op jit(solution)/shard_map/ppermute | solution.py:521
  70.2 0.8 collective-permute-done.22.refs_3_
  71.8 2.9 %collective-permute-done.20.refs_1_ = f32[1,2048]{1,0:T(1,128)S(1)} collective-permute-done((f32[1,2048]{1,0:T(1,128)S(1)}, f32[1,2048]{1,0:T(1,128)S(1)}, u32[]{:S(2)}, u32[]{:S(2)}) %collective-permute-start.20) | collective-permute-done | bytes 8224 | tf_op jit(solution)/shard_map/ppermute | solution.py:521
  74.8 3.1 %row_pass.2 = bf16[32,32,128]{2,1,0:T(8,128)(2,1)S(1)} custom-call(f32[1,2048]{1,0:T(1,128)S(1)} %get-tuple-element.28.refs_0_, f32[1,2048]{1,0:T(1,128)S(1)} %collective-permute-done.20.refs_1_, f32[1,2048]{1,0:T(1,128)S(1)} %collective-permute-done.21.refs_2_, f32[1,2048]{1,0:T(1,128)S(1)} %collective-permute-done.22.refs_3_, ...), custom_call_target="tpu_custom_call" | custom-call | tf_op jit(solution)/shard_map/row_pass/pallas_call | solution.py:324
  77.9 18.3 %all_to_all.39.rows_ref = bf16[32,32,128]{2,1,0:T(8,128)(2,1)S(1)} all-to-all(bf16[32,32,128]{2,1,0:T(8,128)(2,1)S(1)} %row_pass.2), channel_id=1, replica_groups=mesh['z'=4,'y'=4,'c'=2,'x'=4] {'z','c','x'}, dimensions={0} | all-to-all | bytes 524288 | tf_op jit(solution)/shard_map/all_to_all | solution.py:525
  96.2 3.3 %column_pass.2.refs_0_ = f32[1,2048]{1,0:T(1,128)S(1)} custom-call(bf16[32,32,128]{2,1,0:T(8,128)(2,1)S(1)} %all_to_all.39.rows_ref, f32[32,128]{1,0:T(8,128)S(1)} %get-tuple-element.30.own_ref, bf16[8,384,2048]{2,1,0:T(8,128)(2,1)S(1)} %get-tuple-element.29.refs_4_.e.refs_16_.refs_7_), custom_call_target="tpu_custom_call" | custom-call | tf_op jit(solution)/shard_map/column_pass/pallas_call | solution.py:359
  99.9 1.6 collective-permute-start.24
  101.5 2.1 %collective-permute-done.25.refs_3_ = f32[1,2048]{1,0:T(1,128)S(1)} collective-permute-done((f32[1,2048]{1,0:T(1,128)S(1)}, f32[1,2048]{1,0:T(1,128)S(1)}, u32[]{:S(2)}, u32[]{:S(2)}) %collective-permute-start.25) | collective-permute-done | bytes 8224 | tf_op jit(solution)/shard_map/ppermute | solution.py:521
  103.6 1.6 collective-permute-done.23.refs_1_
  105.2 3.1 %row_pass.3 = bf16[32,32,128]{2,1,0:T(8,128)(2,1)S(1)} custom-call(f32[1,2048]{1,0:T(1,128)S(1)} %column_pass.2.refs_0_, f32[1,2048]{1,0:T(1,128)S(1)} %collective-permute-done.23.refs_1_, f32[1,2048]{1,0:T(1,128)S(1)} %collective-permute-done.24.refs_2_, f32[1,2048]{1,0:T(1,128)S(1)} %collective-permute-done.25.refs_3_, ...), custom_call_target="tpu_custom_call" | custom-call | tf_op jit(solution)/shard_map/row_pass/pallas_call | solution.py:324
  108.3 14.5 %all_to_all.40.rows_ref = bf16[32,32,128]{2,1,0:T(8,128)(2,1)S(1)} all-to-all(bf16[32,32,128]{2,1,0:T(8,128)(2,1)S(1)} %row_pass.3), channel_id=1, replica_groups=mesh['z'=4,'y'=4,'c'=2,'x'=4] {'z','c','x'}, dimensions={0} | all-to-all | bytes 524288 | tf_op jit(solution)/shard_map/all_to_all | solution.py:525
  122.8 3.3 %column_pass.3.refs_12_.refs_0_ = f32[1,2048]{1,0:T(1,128)S(1)} custom-call(bf16[32,32,128]{2,1,0:T(8,128)(2,1)S(1)} %all_to_all.40.rows_ref, f32[32,128]{1,0:T(8,128)S(1)} %get-tuple-element.30.own_ref, bf16[8,384,2048]{2,1,0:T(8,128)(2,1)S(1)} %get-tuple-element.29.refs_4_.e.refs_16_.refs_7_), custom_call_target="tpu_custom_call" | custom-call | tf_op jit(solution)/shard_map/column_pass/pallas_call | solution.py:359
  127.3 0.8 collective-permute-start.26
  128.1 2.2 %collective-permute-done.28.refs_15_.refs_3_ = f32[1,2048]{1,0:T(1,128)S(1)} collective-permute-done((f32[1,2048]{1,0:T(1,128)S(1)}, f32[1,2048]{1,0:T(1,128)S(1)}, u32[]{:S(2)}, u32[]{:S(2)}) %collective-permute-start.28) | collective-permute-done | bytes 8224 | tf_op jit(solution)/shard_map/ppermute | solution.py:521
  130.3 0.9 collective-permute-done.26.refs_13_.refs_1_
  131.2 15.0 %closing_pass.1 = (bf16[8,384,256]{2,1,0:T(8,128)(2,1)S(1)}, bf16[8,256,384]{2,1,0:T(8,128)(2,1)S(1)}, bf16[256,2048]{1,0:T(8,128)(2,1)S(1)}, bf16[32,64,128]{2,1,0:T(8,128)(2,1)S(1)}) custom-call(s32[2]{0:T(128)S(1)} %copy-done.3, bf16[384,256]{1,0:T(8,128)(2,1)S(1)} %copy-done.1, bf16[384,256]{1,0:T(8,128)(2,1)S(1)} %collective-permute-done.refs_1_.refs_14_, ...), custom_call_target="tpu_custom_call" | custom-call | tf_op jit(solution)/shard_map/closing_pass/pallas_call | solution.py:421
  146.2 16.8 %all_to_all.41.rows_ref = bf16[32,64,128]{2,1,0:T(8,128)(2,1)S(1)} all-to-all(bf16[32,64,128]{2,1,0:T(8,128)(2,1)S(1)} %get-tuple-element.31), channel_id=1, replica_groups=mesh['z'=4,'y'=4,'c'=2,'x'=4] {'z','c','x'}, dimensions={0} | all-to-all | bytes 1048576 | tf_op jit(solution)/shard_map/all_to_all | solution.py:525
  163.0 11.7 %grad_pass.1 = (f32[64,2048]{1,0:T(8,128)S(1)}, bf16[64,2048]{1,0:T(8,128)(2,1)S(1)}, bf16[64,2048]{1,0:T(8,128)(2,1)S(1)}, bf16[64,2048]{1,0:T(8,128)(2,1)S(1)}, f32[3,128]{1,0:T(4,128)}) custom-call(s32[2]{0:T(128)S(1)} %copy-done.3, bf16[32,64,128]{2,1,0:T(8,128)(2,1)S(1)} %all_to_all.41.rows_ref, f32[32,128]{1,0:T(8,128)S(1)} %get-tuple-element.30.own_ref, ...), custom_call_target="tpu_custom_call" | custom-call | tf_op jit(solution)/shard_map/grad_pass/pallas_call | solution.py:501
  174.8 1.0 collective-permute-start.29
  177.0 5.1 %collective-permute-done.29 = bf16[64,2048]{1,0:T(8,128)(2,1)S(1)} collective-permute-done((bf16[64,2048]{1,0:T(8,128)(2,1)S(1)}, bf16[64,2048]{1,0:T(8,128)(2,1)S(1)}, u32[]{:S(2)}, u32[]{:S(2)}) %collective-permute-start.29) | collective-permute-done | bytes 262176 | tf_op jit(solution)/shard_map/ppermute | solution.py:521
  182.1 7.5 %collective-permute-done.30 = bf16[64,2048]{1,0:T(8,128)(2,1)S(1)} collective-permute-done((bf16[64,2048]{1,0:T(8,128)(2,1)S(1)}, bf16[64,2048]{1,0:T(8,128)(2,1)S(1)}, u32[]{:S(2)}, u32[]{:S(2)}) %collective-permute-start.30) | collective-permute-done | bytes 262176 | tf_op jit(solution)/shard_map/ppermute | solution.py:521
  189.7 13.8 %all_to_all.42 = f32[8,8,2048]{2,1,0:T(8,128)S(1)} all-to-all(f32[8,8,2048]{2,1,0:T(8,128)S(1)} %add_bitcast_fusion), channel_id=1, replica_groups=mesh['z'=4,'y'=4,'c'=2,'x'=4] {'z','c'}, dimensions={0} | all-to-all | bytes 1048576 | tf_op jit(solution)/shard_map/all_to_all | solution.py:563
  203.5 0.8 copy.10
  (42 shorter events, 7.1 us)
Async XLA Ops:
  6.9 24.9 %all-to-all-start = ((bf16[8,16,2048]{2,1,0:T(8,128)(2,1)}), bf16[8,16,2048]{2,1,0:T(8,128)(2,1)S(1)}, u32[]{:S(2)}, u32[]{:S(2)}) async-start(bf16[8,16,2048]{2,1,0:T(8,128)(2,1)} %get-tuple-element.23), calls=%async_computation | async-start | bytes 1048576 | tf_op jit(solution)/shard_map/all_to_all | solution.py:525
  13.7 13.7 %collective-permute-start.2 = (bf16[384,256]{1,0:T(8,128)(2,1)}, bf16[384,256]{1,0:T(8,128)(2,1)S(1)}, u32[]{:S(2)}, u32[]{:S(2)}) collective-permute-start(bf16[384,256]{1,0:T(8,128)(2,1)} %get-tuple-element.22.refs_0_.tok_ref.refs_13_), channel_id=1, source_target_pairs={{0,64},{32,96},{64,0},{96,32},{1,65},{33,97},{65,1},{97,33},{2,66}... | collective-permute-start | bytes 589832 | tf_op jit(solution)/shard_map/ppermute | solution.py:521
  16.6 13.6 %collective-permute-start.1 = (bf16[384,256]{1,0:T(8,128)(2,1)}, bf16[384,256]{1,0:T(8,128)(2,1)S(1)}, u32[]{:S(2)}, u32[]{:S(2)}) collective-permute-start(bf16[384,256]{1,0:T(8,128)(2,1)} %get-tuple-element.22.refs_0_.tok_ref.refs_13_), channel_id=1, source_target_pairs={{0,96},{32,0},{64,32},{96,64},{1,97},{33,1},{65,33},{97,65},{2,98}... | collective-permute-start | bytes 589832 | tf_op jit(solution)/shard_map/ppermute | solution.py:521
  17.5 14.3 %collective-permute-start = (bf16[384,256]{1,0:T(8,128)(2,1)}, bf16[384,256]{1,0:T(8,128)(2,1)S(1)}, u32[]{:S(2)}, u32[]{:S(2)}) collective-permute-start(bf16[384,256]{1,0:T(8,128)(2,1)} %get-tuple-element.22.refs_0_.tok_ref.refs_13_), channel_id=1, source_target_pairs={{0,32},{32,64},{64,96},{96,0},{1,33},{33,65},{65,97},{97,1},{2,34}... | collective-permute-start | bytes 589832 | tf_op jit(solution)/shard_map/ppermute | solution.py:521
  18.1 20.5 %collective-permute-start.3 = (bf16[384,256]{1,0:T(8,128)(2,1)}, bf16[384,256]{1,0:T(8,128)(2,1)S(1)}, u32[]{:S(2)}, u32[]{:S(2)}) collective-permute-start(bf16[384,256]{1,0:T(8,128)(2,1)} %get-tuple-element.22.refs_0_.tok_ref.refs_13_), channel_id=1, source_target_pairs={{0,4},{4,0},{1,5},{5,1},{2,6},{6,2},{3,7},{7,3},{8,12},{12,8},{9,1... | collective-permute-start | bytes 589832 | tf_op jit(solution)/shard_map/ppermute | solution.py:521
  27.5 11.9 %collective-permute-start.6 = (bf16[384,256]{1,0:T(8,128)(2,1)S(1)}, bf16[384,256]{1,0:T(8,128)(2,1)S(1)}, u32[]{:S(2)}, u32[]{:S(2)}) collective-permute-start(bf16[384,256]{1,0:T(8,128)(2,1)S(1)} %collective-permute-done.2.refs_3_.refs_16_), channel_id=1, source_target_pairs={{0,4},{4,0},{1,5},{5,1},{2,6},{6,2},{3,7},{7,3},{8,12},{12,8},{9,1... | collective-permute-start | bytes 589832 | tf_op jit(solution)/shard_map/ppermute | solution.py:521
  31.9 0.9 copy-start
  32.8 0.9 copy-start.2
  33.7 23.3 %copy-start.1 = (bf16[384,256]{1,0:T(8,128)(2,1)S(1)}, bf16[384,256]{1,0:T(8,128)(2,1)}, u32[]{:S(2)}) copy-start(bf16[384,256]{1,0:T(8,128)(2,1)} %get-tuple-element.22.refs_0_.tok_ref.refs_13_) | copy-start | bytes 589828
  33.7 23.3 %copy-start.3 = (s32[2]{0:T(128)S(1)}, s32[2]{0:T(128)}, u32[]{:S(2)}) copy-start(s32[2]{0:T(128)} %get-tuple-element.21.info_ref) | copy-start | bytes 28
  33.8 7.6 %collective-permute-start.15 = (bf16[400,256]{1,0:T(8,128)(2,1)S(1)}, bf16[400,256]{1,0:T(8,128)(2,1)S(1)}, u32[]{:S(2)}, u32[]{:S(2)}) collective-permute-start(bf16[400,256]{1,0:T(8,128)(2,1)S(1)} %get-tuple-element.27.refs_0_), channel_id=1, source_target_pairs={{0,64},{32,96},{64,0},{96,32},{1,65},{33,97},{65,1},{97,33},{2,66}... | collective-permute-start | bytes 614408 | tf_op jit(solution)/shard_map/ppermute | solution.py:521
  34.6 5.5 %collective-permute-start.5 = (bf16[384,256]{1,0:T(8,128)(2,1)S(1)}, bf16[384,256]{1,0:T(8,128)(2,1)S(1)}, u32[]{:S(2)}, u32[]{:S(2)}) collective-permute-start(bf16[384,256]{1,0:T(8,128)(2,1)S(1)} %collective-permute-done.1.refs_2_.refs_15_), channel_id=1, source_target_pairs={{0,4},{4,0},{1,5},{5,1},{2,6},{6,2},{3,7},{7,3},{8,12},{12,8},{9,1... | collective-permute-start | bytes 589832 | tf_op jit(solution)/shard_map/ppermute | solution.py:521
  35.7 14.4 %collective-permute-start.9 = (bf16[64,2048]{1,0:T(8,128)(2,1)S(1)}, bf16[64,2048]{1,0:T(8,128)(2,1)S(1)}, u32[]{:S(2)}, u32[]{:S(2)}) collective-permute-start(bf16[64,2048]{1,0:T(8,128)(2,1)S(1)} %get-tuple-element.25.refs_0_.refs_8_), channel_id=1, source_target_pairs={{0,16},{8,24},{16,0},{24,8},{1,17},{9,25},{17,1},{25,9},{2,18},{10... | collective-permute-start | bytes 786440 | tf_op jit(solution)/shard_map/ppermute | solution.py:521
  38.6 12.5 %collective-permute-start.8 = (bf16[64,2048]{1,0:T(8,128)(2,1)S(1)}, bf16[64,2048]{1,0:T(8,128)(2,1)S(1)}, u32[]{:S(2)}, u32[]{:S(2)}) collective-permute-start(bf16[64,2048]{1,0:T(8,128)(2,1)S(1)} %get-tuple-element.25.refs_0_.refs_8_), channel_id=1, source_target_pairs={{0,24},{8,0},{16,8},{24,16},{1,25},{9,1},{17,9},{25,17},{2,26},{10... | collective-permute-start | bytes 786440 | tf_op jit(solution)/shard_map/ppermute | solution.py:521
  39.4 12.5 %collective-permute-start.7 = (bf16[64,2048]{1,0:T(8,128)(2,1)S(1)}, bf16[64,2048]{1,0:T(8,128)(2,1)S(1)}, u32[]{:S(2)}, u32[]{:S(2)}) collective-permute-start(bf16[64,2048]{1,0:T(8,128)(2,1)S(1)} %get-tuple-element.25.refs_0_.refs_8_), channel_id=1, source_target_pairs={{0,8},{8,16},{16,24},{24,0},{1,9},{9,17},{17,25},{25,1},{2,10},{10... | collective-permute-start | bytes 786440 | tf_op jit(solution)/shard_map/ppermute | solution.py:521
  40.1 5.8 %collective-permute-start.14 = (bf16[400,256]{1,0:T(8,128)(2,1)S(1)}, bf16[400,256]{1,0:T(8,128)(2,1)S(1)}, u32[]{:S(2)}, u32[]{:S(2)}) collective-permute-start(bf16[400,256]{1,0:T(8,128)(2,1)S(1)} %get-tuple-element.27.refs_0_), channel_id=1, source_target_pairs={{0,96},{32,0},{64,32},{96,64},{1,97},{33,1},{65,33},{97,65},{2,98}... | collective-permute-start | bytes 614408 | tf_op jit(solution)/shard_map/ppermute | solution.py:521
  41.4 6.3 %collective-permute-start.13 = (bf16[400,256]{1,0:T(8,128)(2,1)S(1)}, bf16[400,256]{1,0:T(8,128)(2,1)S(1)}, u32[]{:S(2)}, u32[]{:S(2)}) collective-permute-start(bf16[400,256]{1,0:T(8,128)(2,1)S(1)} %get-tuple-element.27.refs_0_), channel_id=1, source_target_pairs={{0,32},{32,64},{64,96},{96,0},{1,33},{33,65},{65,97},{97,1},{2,34}... | collective-permute-start | bytes 614408 | tf_op jit(solution)/shard_map/ppermute | solution.py:521
  45.9 9.7 %collective-permute-start.16 = (bf16[400,256]{1,0:T(8,128)(2,1)S(1)}, bf16[400,256]{1,0:T(8,128)(2,1)S(1)}, u32[]{:S(2)}, u32[]{:S(2)}) collective-permute-start(bf16[400,256]{1,0:T(8,128)(2,1)S(1)} %get-tuple-element.27.refs_0_), channel_id=1, source_target_pairs={{0,4},{4,0},{1,5},{5,1},{2,6},{6,2},{3,7},{7,3},{8,12},{12,8},{9,1... | collective-permute-start | bytes 614408 | tf_op jit(solution)/shard_map/ppermute | solution.py:521
  47.7 9.0 %collective-permute-start.19 = (bf16[400,256]{1,0:T(8,128)(2,1)S(1)}, bf16[400,256]{1,0:T(8,128)(2,1)S(1)}, u32[]{:S(2)}, u32[]{:S(2)}) collective-permute-start(bf16[400,256]{1,0:T(8,128)(2,1)S(1)} %collective-permute-done.15.refs_3_), channel_id=1, source_target_pairs={{0,4},{4,0},{1,5},{5,1},{2,6},{6,2},{3,7},{7,3},{8,12},{12,8},{9,1... | collective-permute-start | bytes 614408 | tf_op jit(solution)/shard_map/ppermute | solution.py:521
  50.1 6.9 %collective-permute-start.18 = (bf16[400,256]{1,0:T(8,128)(2,1)S(1)}, bf16[400,256]{1,0:T(8,128)(2,1)S(1)}, u32[]{:S(2)}, u32[]{:S(2)}) collective-permute-start(bf16[400,256]{1,0:T(8,128)(2,1)S(1)} %collective-permute-done.14.refs_2_), channel_id=1, source_target_pairs={{0,4},{4,0},{1,5},{5,1},{2,6},{6,2},{3,7},{7,3},{8,12},{12,8},{9,1... | collective-permute-start | bytes 614408 | tf_op jit(solution)/shard_map/ppermute | solution.py:521
  51.2 5.9 %collective-permute-start.17 = (bf16[400,256]{1,0:T(8,128)(2,1)S(1)}, bf16[400,256]{1,0:T(8,128)(2,1)S(1)}, u32[]{:S(2)}, u32[]{:S(2)}) collective-permute-start(bf16[400,256]{1,0:T(8,128)(2,1)S(1)} %collective-permute-done.13.refs_1_), channel_id=1, source_target_pairs={{0,4},{4,0},{1,5},{5,1},{2,6},{6,2},{3,7},{7,3},{8,12},{12,8},{9,1... | collective-permute-start | bytes 614408 | tf_op jit(solution)/shard_map/ppermute | solution.py:521
  52.0 1.4 collective-permute-start.4
  53.4 21.4 %collective-permute-start.12 = (bf16[64,2048]{1,0:T(8,128)(2,1)S(1)}, bf16[64,2048]{1,0:T(8,128)(2,1)S(1)}, u32[]{:S(2)}, u32[]{:S(2)}) collective-permute-start(bf16[64,2048]{1,0:T(8,128)(2,1)S(1)} %get-tuple-element.26.refs_12_.refs_5_.refs_8_), channel_id=1, source_target_pairs={{0,16},{8,24},{16,0},{24,8},{1,17},{9,25},{17,1},{25,9},{2,18},{10... | collective-permute-start | bytes 786440 | tf_op jit(solution)/shard_map/ppermute | solution.py:521
  55.6 19.2 %collective-permute-start.11 = (bf16[64,2048]{1,0:T(8,128)(2,1)S(1)}, bf16[64,2048]{1,0:T(8,128)(2,1)S(1)}, u32[]{:S(2)}, u32[]{:S(2)}) collective-permute-start(bf16[64,2048]{1,0:T(8,128)(2,1)S(1)} %get-tuple-element.26.refs_12_.refs_5_.refs_8_), channel_id=1, source_target_pairs={{0,24},{8,0},{16,8},{24,16},{1,25},{9,1},{17,9},{25,17},{2,26},{10... | collective-permute-start | bytes 786440 | tf_op jit(solution)/shard_map/ppermute | solution.py:521
  56.7 18.1 %collective-permute-start.10 = (bf16[64,2048]{1,0:T(8,128)(2,1)S(1)}, bf16[64,2048]{1,0:T(8,128)(2,1)S(1)}, u32[]{:S(2)}, u32[]{:S(2)}) collective-permute-start(bf16[64,2048]{1,0:T(8,128)(2,1)S(1)} %get-tuple-element.26.refs_12_.refs_5_.refs_8_), channel_id=1, source_target_pairs={{0,8},{8,16},{16,24},{24,0},{1,9},{9,17},{17,25},{25,1},{2,10},{10... | collective-permute-start | bytes 786440 | tf_op jit(solution)/shard_map/ppermute | solution.py:521
  67.0 4.1 %collective-permute-start.22 = (f32[1,2048]{1,0:T(1,128)S(1)}, f32[1,2048]{1,0:T(1,128)S(1)}, u32[]{:S(2)}, u32[]{:S(2)}) collective-permute-start(f32[1,2048]{1,0:T(1,128)S(1)} %get-tuple-element.28.refs_0_), channel_id=1, source_target_pairs={{0,16},{8,24},{16,0},{24,8},{1,17},{9,25},{17,1},{25,9},{2,18},{10... | collective-permute-start | bytes 24584 | tf_op jit(solution)/shard_map/ppermute | solution.py:521
  68.2 3.7 %collective-permute-start.21 = (f32[1,2048]{1,0:T(1,128)S(1)}, f32[1,2048]{1,0:T(1,128)S(1)}, u32[]{:S(2)}, u32[]{:S(2)}) collective-permute-start(f32[1,2048]{1,0:T(1,128)S(1)} %get-tuple-element.28.refs_0_), channel_id=1, source_target_pairs={{0,24},{8,0},{16,8},{24,16},{1,25},{9,1},{17,9},{25,17},{2,26},{10... | collective-permute-start | bytes 24584 | tf_op jit(solution)/shard_map/ppermute | solution.py:521
  71.1 3.7 %collective-permute-start.20 = (f32[1,2048]{1,0:T(1,128)S(1)}, f32[1,2048]{1,0:T(1,128)S(1)}, u32[]{:S(2)}, u32[]{:S(2)}) collective-permute-start(f32[1,2048]{1,0:T(1,128)S(1)} %get-tuple-element.28.refs_0_), channel_id=1, source_target_pairs={{0,8},{8,16},{16,24},{24,0},{1,9},{9,17},{17,25},{25,1},{2,10},{10... | collective-permute-start | bytes 24584 | tf_op jit(solution)/shard_map/ppermute | solution.py:521
  99.6 4.1 %collective-permute-start.25 = (f32[1,2048]{1,0:T(1,128)S(1)}, f32[1,2048]{1,0:T(1,128)S(1)}, u32[]{:S(2)}, u32[]{:S(2)}) collective-permute-start(f32[1,2048]{1,0:T(1,128)S(1)} %column_pass.2.refs_0_), channel_id=1, source_target_pairs={{0,16},{8,24},{16,0},{24,8},{1,17},{9,25},{17,1},{25,9},{2,18},{10... | collective-permute-start | bytes 24584 | tf_op jit(solution)/shard_map/ppermute | solution.py:521
  99.9 3.8 %collective-permute-start.24 = (f32[1,2048]{1,0:T(1,128)S(1)}, f32[1,2048]{1,0:T(1,128)S(1)}, u32[]{:S(2)}, u32[]{:S(2)}) collective-permute-start(f32[1,2048]{1,0:T(1,128)S(1)} %column_pass.2.refs_0_), channel_id=1, source_target_pairs={{0,24},{8,0},{16,8},{24,16},{1,25},{9,1},{17,9},{25,17},{2,26},{10... | collective-permute-start | bytes 24584 | tf_op jit(solution)/shard_map/ppermute | solution.py:521
  101.5 3.7 %collective-permute-start.23 = (f32[1,2048]{1,0:T(1,128)S(1)}, f32[1,2048]{1,0:T(1,128)S(1)}, u32[]{:S(2)}, u32[]{:S(2)}) collective-permute-start(f32[1,2048]{1,0:T(1,128)S(1)} %column_pass.2.refs_0_), channel_id=1, source_target_pairs={{0,8},{8,16},{16,24},{24,0},{1,9},{9,17},{17,25},{25,1},{2,10},{10... | collective-permute-start | bytes 24584 | tf_op jit(solution)/shard_map/ppermute | solution.py:521
  126.2 4.1 %collective-permute-start.28 = (f32[1,2048]{1,0:T(1,128)S(1)}, f32[1,2048]{1,0:T(1,128)S(1)}, u32[]{:S(2)}, u32[]{:S(2)}) collective-permute-start(f32[1,2048]{1,0:T(1,128)S(1)} %column_pass.3.refs_12_.refs_0_), channel_id=1, source_target_pairs={{0,16},{8,24},{16,0},{24,8},{1,17},{9,25},{17,1},{25,9},{2,18},{10... | collective-permute-start | bytes 24584 | tf_op jit(solution)/shard_map/ppermute | solution.py:521
  126.6 3.7 %collective-permute-start.27 = (f32[1,2048]{1,0:T(1,128)S(1)}, f32[1,2048]{1,0:T(1,128)S(1)}, u32[]{:S(2)}, u32[]{:S(2)}) collective-permute-start(f32[1,2048]{1,0:T(1,128)S(1)} %column_pass.3.refs_12_.refs_0_), channel_id=1, source_target_pairs={{0,24},{8,0},{16,8},{24,16},{1,25},{9,1},{17,9},{25,17},{2,26},{10... | collective-permute-start | bytes 24584 | tf_op jit(solution)/shard_map/ppermute | solution.py:521
  127.3 3.9 %collective-permute-start.26 = (f32[1,2048]{1,0:T(1,128)S(1)}, f32[1,2048]{1,0:T(1,128)S(1)}, u32[]{:S(2)}, u32[]{:S(2)}) collective-permute-start(f32[1,2048]{1,0:T(1,128)S(1)} %column_pass.3.refs_12_.refs_0_), channel_id=1, source_target_pairs={{0,8},{8,16},{16,24},{24,0},{1,9},{9,17},{17,25},{25,1},{2,10},{10... | collective-permute-start | bytes 24584 | tf_op jit(solution)/shard_map/ppermute | solution.py:521
  174.8 7.3 %collective-permute-start.29 = (bf16[64,2048]{1,0:T(8,128)(2,1)S(1)}, bf16[64,2048]{1,0:T(8,128)(2,1)S(1)}, u32[]{:S(2)}, u32[]{:S(2)}) collective-permute-start(bf16[64,2048]{1,0:T(8,128)(2,1)S(1)} %get-tuple-element.37), channel_id=1, source_target_pairs={{0,24},{8,0},{16,8},{24,16},{1,25},{9,1},{17,9},{25,17},{2,26},{10... | collective-permute-start | bytes 786440 | tf_op jit(solution)/shard_map/ppermute | solution.py:521
  175.8 13.8 %collective-permute-start.30 = (bf16[64,2048]{1,0:T(8,128)(2,1)S(1)}, bf16[64,2048]{1,0:T(8,128)(2,1)S(1)}, u32[]{:S(2)}, u32[]{:S(2)}) collective-permute-start(bf16[64,2048]{1,0:T(8,128)(2,1)S(1)} %get-tuple-element.38), channel_id=1, source_target_pairs={{0,8},{8,16},{16,24},{24,0},{1,9},{9,17},{17,25},{25,1},{2,10},{10... | collective-permute-start | bytes 786440 | tf_op jit(solution)/shard_map/ppermute | solution.py:521
  176.2 13.4 %collective-permute-start.31 = (bf16[64,2048]{1,0:T(8,128)(2,1)S(1)}, bf16[64,2048]{1,0:T(8,128)(2,1)S(1)}, u32[]{:S(2)}, u32[]{:S(2)}) collective-permute-start(bf16[64,2048]{1,0:T(8,128)(2,1)S(1)} %get-tuple-element.39), channel_id=1, source_target_pairs={{0,16},{8,24},{16,0},{24,8},{1,17},{9,25},{17,1},{25,9},{2,18},{10... | collective-permute-start | bytes 786440 | tf_op jit(solution)/shard_map/ppermute | solution.py:521

commit v3 on v2

--- a/solution.py
+++ b/solution.py
@@ -20,6 +20,7 @@
 LANES = 128
 SHIFTS = (1, 3, 2)
 SIDE = 4
+DP = ("z", "y", "c")
 GROUP = ("z", "c", "x")
 
 teacher_temp = 0.07
@@ -55,7 +56,7 @@
 
 
 def tokens_kernel(me_ref, count_ref, index_ref, teacher_ref, student_ref, tp_ref, sp_ref,
-                  t_out, s_out, w_out, info_out, feats, protos, sems, p_sems):
+                  tok_out, w_out, info_out, feats, protos, sems, p_sems):
     proto_copies = [
         pltpu.make_async_copy(ref, protos.at[i], p_sems.at[i])
         for i, ref in enumerate((tp_ref, sp_ref))
@@ -67,9 +68,10 @@
     for c in proto_copies + copies:
         c.start()
     me = me_ref[0]
-    z, y, core = me >> 3, (me >> 1) & 3, me & 1
-    info_out[0] = z
-    info_out[1] = core
+    y = (me >> 1) & 3
+    info_out[0] = me >> 3
+    info_out[1] = me & 1
+    info_out[2] = y
     slots = index_ref.shape[0]
     source, d = feats.shape[1:]
     index_row = index_ref[...].reshape(1, slots)
@@ -83,15 +85,15 @@
     rest = jnp.concatenate([own[:, d:], jnp.zeros((1, 2 * d - slots), f32)], axis=1)
     at = lax.broadcasted_iota(jnp.int32, (EXTRA, d), 0)
     counts = jnp.where(at == 0, own[:, 0:d], jnp.where(at == 1, rest, 0.0))
-    t_out[slots : slots + EXTRA, :] = counts.astype(bf16)
+    tok_out[slots : slots + EXTRA, :] = counts.astype(bf16)
     pick = jnp.where(
         lax.broadcasted_iota(jnp.int32, (slots, source), 1) == index_col, 1.0, 0.0
     ).astype(bf16)
     to = lax.broadcasted_iota(jnp.int32, (1, d), 1)
     turn = to >> 6
-    shift = jnp.where(turn == 2, 3, jnp.where(turn == 3, 2, turn))
+    turn = jnp.where(turn == 2, 3, jnp.where(turn == 3, 2, turn))
     origin = (
-        ((to >> 4) & 3) * 64 + ((y + 4 - shift) & 3) * 16 + ((to >> 3) & 1) * 8 + (to & 7)
+        ((to >> 4) & 3) * 64 + ((y + 4 - turn) & 3) * 16 + ((to >> 3) & 1) * 8 + (to & 7)
     )
     order = jnp.where(
         lax.broadcasted_iota(jnp.int32, (d, d), 0) == origin, 1.0, 0.0
@@ -104,11 +106,11 @@
         w_out[q] = jnp.concatenate(
             [protos[0, :, lanes].astype(f32), protos[1, :, lanes].astype(f32)], axis=0
         ).astype(bf16)
-    for i, out in enumerate((t_out, s_out)):
+    for i, at in enumerate((0, slots + EXTRA)):
         copies[i].wait()
         rows = nn(pick, feats[i])
         unit = rows * lax.rsqrt(jnp.sum(rows * rows, axis=1, keepdims=True) + 1e-06)
-        out[0:slots, :] = nn(unit.astype(bf16), order).astype(bf16)
+        tok_out[at : at + slots, :] = nn(unit.astype(bf16), order).astype(bf16)
 
 
 def tokens(me, count, index, teacher_feat, student_feat, teacher_proto, student_proto):
@@ -118,13 +120,12 @@
     return pl.pallas_call(
         tokens_kernel,
         out_shape=(
-            shape((slots + EXTRA, d), bf16),
-            shape((slots, d), bf16),
+            shape((2 * slots + EXTRA, d), bf16),
             shape((parts, 2 * rows, cols // parts), bf16),
-            shape((2,), jnp.int32),
+            shape((3,), jnp.int32),
         ),
         in_specs=[SM, SM, VM, ANY, ANY, ANY, ANY],
-        out_specs=(VM, VM, VM, SM),
+        out_specs=(VM, VM, SM),
         scratch_shapes=[
             pltpu.VMEM((2, source, d), bf16),
             pltpu.VMEM((2, rows, cols), bf16),
@@ -136,39 +137,55 @@
     )(me, count, index, teacher_feat, student_feat, teacher_proto, student_proto)
 
 
-def split_kernel(which, w_ref, tok_ref, *refs):
-    out, tok_out = refs[-2:]
-    parts, rows, width = w_ref.shape
-    out[...] = (
-        w_ref[...].astype(f32)[:, 8 * which : 8 * which + 8]
-        .reshape(parts * 8, width)
-        .astype(bf16)
-    )
-    tok_out[...] = tok_ref[...]
-
-
-def split(which, w, tok, after=()):
+def stack_kernel(info_ref, *refs):
+    toks, (t_out, s_out) = refs[0:4], refs[-2:]
+    rows = t_out.shape[1]
+    for k, ref in zip((0,) + SHIFTS, toks):
+        z = (info_ref[0] + 4 - k) & 3
+        t_out[z] = ref[0:rows, :]
+        s_out[z] = ref[rows:, :]
+
+
+def stack(info, toks, slots, after):
+    n, d = len(toks), toks[0].shape[1]
+    return pl.pallas_call(
+        stack_kernel,
+        out_shape=(shape((n, slots + EXTRA, d), bf16), shape((n, slots, d), bf16)),
+        in_specs=[SM] + [VM] * n + [ANY] * len(after),
+        out_specs=(VM, VM),
+        compiler_params=params(16),
+        name="stack",
+    )(info, *toks, *after)
+
+
+def split_kernel(which, w_ref, *refs):
+    out = refs[-1]
+    parts, _, width = w_ref.shape
+    rows = w_ref[...].astype(f32)[:, 8 * which : 8 * which + 8]
+    out[...] = rows.reshape(parts * 8, width).astype(bf16)
+
+
+def split(which, w, after=()):
     parts, rows, width = w.shape
     return pl.pallas_call(
         functools.partial(split_kernel, which),
-        out_shape=(shape((parts * rows // 2, width), bf16), shape(tok.shape, bf16)),
-        in_specs=[VM, VM] + [ANY] * len(after),
-        out_specs=(VM, VM),
+        out_shape=shape((parts * rows // 2, width), bf16),
+        in_specs=[VM] + [ANY] * len(after),
+        out_specs=VM,
         compiler_params=params(16),
         name="split_rows",
-    )(w, tok, *after)
+    )(w, *after)
 
 
 def token_copies(info_ref, refs, dst, sems):
-    z, core = info_ref[0], info_ref[1]
-    copies = []
-    for a, ref in enumerate(refs):
-        k = (0,) + SHIFTS
-        at = ((z + 4 - k[a % 4]) & 3) * 2 + (core if a < 4 else 1 - core)
-        copies.append(
-            pltpu.make_async_copy(ref, dst.at[at], sems.at[a])
+    core = info_ref[1]
+    return [
+        pltpu.make_async_copy(
+            ref.at[z], dst.at[2 * z + (1 - core if i else core)], sems.at[4 * i + z]
         )
-    return copies
+        for i, ref in enumerate(refs)
+        for z in range(4)
+    ]
 
 
 def weight_copies(refs, dst, sems):
@@ -231,7 +248,7 @@
 
 
 def energy_kernel(info_ref, *refs):
-    toks, w_refs = refs[0:8], refs[8:12]
+    toks, w_refs = refs[0:2], refs[2:6]
     e_ref, own_ref, sum_ref, u, w, live, acc, t_sems, w_sems = refs[-9:]
     blocks, slots, cols = e_ref.shape
     t_copies = token_copies(info_ref, toks, u, t_sems)
@@ -270,7 +287,7 @@
 
 def energy_pass(info, toks, w_parts, slots, after):
     d, cols = SIDE * w_parts[0].shape[0], w_parts[0].shape[1]
-    blocks = len(toks)
+    blocks = 2 * toks[0].shape[0]
     return pl.pallas_call(
         energy_kernel,
         out_shape=(
@@ -278,7 +295,7 @@
             shape((TALL, LANES)),
             shape((1, cols)),
         ),
-        in_specs=[SM] + [ANY] * (blocks + len(w_parts) + len(after)),
+        in_specs=[SM] + [ANY] * (len(toks) + len(w_parts) + len(after)),
         out_specs=(VM, VM, VM),
         scratch_shapes=[
             pltpu.VMEM((blocks, slots + EXTRA, d), bf16),
@@ -298,8 +315,37 @@
     )(info, *toks, *w_parts, *after)
 
 
+def collect_kernel(info_ref, sums_ref, *refs):
+    w_refs, toks, (sums_out, w_out, u_out) = refs[0:4], refs[4:6], refs[6:]
+    sums_out[...] = sums_ref[...]
+    rows = w_refs[0].shape[0]
+    for i, ref in enumerate(w_refs):
+        w_out[i * rows : (i + 1) * rows, :] = ref[...]
+    core = info_ref[1]
+    for i, ref in enumerate(toks):
+        for z in range(ref.shape[0]):
+            u_out[2 * z + (1 - core if i else core)] = ref[z]
+
+
+def collect(info, sums, w_parts, toks):
+    rows, cols = w_parts[0].shape
+    n, slots, d = toks[0].shape
+    return pl.pallas_call(
+        collect_kernel,
+        out_shape=(
+            shape(sums.shape),
+            shape((SIDE * rows, cols), bf16),
+            shape((2 * n, slots, d), bf16),
+        ),
+        in_specs=[SM] + [VM] * (1 + len(w_parts) + len(toks)),
+        out_specs=(VM, VM, VM),
+        compiler_params=params(16),
+        name="collect",
+    )(info, sums, *w_parts, *toks)
+
+
 def row_kernel(*refs):
-    sums, (e, *_, out_ref, part, rows) = refs[0:SIDE], refs[SIDE:]
+    sums, e, (out_ref, part, rows) = refs[0:SIDE], refs[SIDE], refs[-3:]
     blocks, slots, cols = e.shape
     c = column_factor(sums)
     rows[...] = jnp.zeros_like(rows)
@@ -326,10 +372,7 @@
         out_shape=shape((peers, TALL, LANES), bf16),
         in_specs=[VM] * (SIDE + 1) + [ANY] * len(after),
         out_specs=VM,
-        scratch_shapes=[
-            pltpu.VMEM((slots, LANES), f32),
-            pltpu.VMEM((TALL, LANES), f32),
-        ],
+        scratch_shapes=[pltpu.VMEM((slots, LANES), f32), pltpu.VMEM((TALL, LANES), f32)],
         compiler_params=params(8),
         name="row_pass",
     )(*sums, pinned(energy), *after)
@@ -371,41 +414,72 @@
     )(rows, own, pinned(energy))
 
 
-def closing_kernel(info_ref, *refs):
-    toks, w_refs, sums = refs[0:8], refs[8:12], refs[12 : 12 + SIDE]
-    e, u, ut, w, out_ref, part, rows, crosses, t_sems, w_sems = refs[12 + SIDE :]
+def softmax_kernel(first, u, w, out_ref, part):
+    _, slots, _ = u.shape
+    cols = w.shape[1]
+    scale = inverse_norms(w) * (LOG2E / student_temp)
+
+    def step(b, _):
+        part[...] = jnp.zeros_like(part)
+        for n in chunks(cols, cols // 2):
+            raw = nn(u[first + b], w[:, n])
+            for r in chunks(slots, ROWS):
+                total = part[r, :]
+                for i in range(0, cols // 2, LANES):
+                    k = slice(n.start + i, n.start + i + LANES)
+                    total = total + jnp.exp2(raw[r, i : i + LANES] * scale[:, k])
+                part[r, :] = total
+        out_ref[pl.ds(PER * b, PER), :] = across(part)
+        return 0
+
+    lax.fori_loop(0, out_ref.shape[0] // PER, step, 0)
+
+
+def softmax_pass(u, w, first, count):
+    blocks, slots, d = u.shape
+    cols = w.shape[1]
+    return pl.pallas_call(
+        functools.partial(softmax_kernel, first),
+        out_shape=shape((PER * count, LANES)),
+        in_specs=[VM, VM],
+        out_specs=VM,
+        scratch_shapes=[pltpu.VMEM((slots, LANES), f32)],
+        compiler_params=params(16),
+        cost_estimate=pl.CostEstimate(
+            flops=2 * count * slots * cols * d,
+            transcendentals=count * slots * cols,
+            bytes_accessed=count * slots * d,
+        ),
+        name="softmax_pass",
+    )(u, w)
+
+
+def closing_kernel(*refs):
+    u, w, soft_a, soft_b, sums = refs[0], refs[1], refs[2], refs[3], refs[4 : 4 + SIDE]
+    e, ut, out_ref, part, rows, crosses = refs[4 + SIDE :]
     blocks, slots, cols = e.shape
-    t_copies = token_copies(info_ref, toks, u, t_sems)
-    w_copies = weight_copies(w_refs, w, w_sems)
-    for copy in w_copies + t_copies:
-        copy.start()
     c = column_factor(sums)
-    for copy in w_copies + t_copies:
-        copy.wait()
-    scale = inverse_norms(w) * (LOG2E / student_temp)
+    cs = c * (inverse_norms(w) * (1.0 / student_temp))
     rows[...] = jnp.zeros_like(rows)
+    half = PER * blocks // 2
+    rows[2 * half : 3 * half, :] = soft_a[...]
+    rows[3 * half : 4 * half, :] = soft_b[...]
 
     def step(b, _):
         ut[b] = jnp.transpose(u[b].astype(f32)).astype(bf16)
-        for tall in chunks(slots, LANES):
-            raw = nn(u[b, tall, :], w[...])
-            for at in chunks(LANES, ROWS):
-                r = slice(tall.start + at.start, tall.start + at.stop)
-                mass = jnp.zeros((ROWS, LANES), f32)
-                cross = jnp.zeros((ROWS, LANES), f32)
-                total = jnp.zeros((ROWS, LANES), f32)
-                for k in chunks(cols, LANES):
-                    power = raw[at, k] * scale[:, k]
-                    total = total + jnp.exp2(power)
-                    energy = e[b, r, k].astype(f32) * c[:, k]
-                    mass = mass + energy
-                    cross = cross + energy * power
-                part[0, r, :] = mass
-                part[1, r, :] = total
-                part[2, r, :] = cross
+        part[...] = jnp.zeros_like(part)
+        for n in chunks(cols, cols // 2):
+            raw = nn(u[b], w[:, n])
+            for r in chunks(slots, ROWS):
+                mass, cross = part[0, r, :], part[1, r, :]
+                for i in range(0, cols // 2, LANES):
+                    k = slice(n.start + i, n.start + i + LANES)
+                    energy = e[b, r, k].astype(f32)
+                    mass = mass + energy * c[:, k]
+                    cross = cross + energy * cs[:, k] * raw[r, i : i + LANES]
+                part[0, r, :], part[1, r, :] = mass, cross
         rows[pl.ds(PER * b, PER), :] = across(part.at[0])
-        rows[pl.ds(PER * (blocks + b), PER), :] = across(part.at[1])
-        crosses[b, 0:PER, :] = across(part.at[2]) * (1.0 / LOG2E)
+        crosses[b, 0:PER, :] = across(part.at[1])
         return 0
 
     lax.fori_loop(0, blocks, step, 0)
@@ -415,34 +489,30 @@
         out_ref[i] = rows[...].astype(bf16)
 
 
-def closing_pass(info, toks, w_parts, sums, energy, peers):
+def closing_pass(u, w, soft, sums, energy, peers):
     blocks, slots, cols = energy.shape
-    d = SIDE * w_parts[0].shape[0]
+    d = w.shape[0]
     return pl.pallas_call(
         closing_kernel,
         out_shape=(
-            pltpu.VMEM((blocks, slots, d), bf16),
             pltpu.VMEM((blocks, d, slots), bf16),
-            pltpu.VMEM((d, cols), bf16),
             shape((peers, 2 * TALL, LANES), bf16),
         ),
-        in_specs=[SM] + [ANY] * (blocks + len(w_parts)) + [VM] * (SIDE + 1),
-        out_specs=(VM, VM, VM, VM),
+        in_specs=[VM] * (SIDE + 5),
+        out_specs=(VM, VM),
         scratch_shapes=[
-            pltpu.VMEM((3, slots, LANES), f32),
+            pltpu.VMEM((2, slots, LANES), f32),
             pltpu.VMEM((2 * TALL, LANES), f32),
             pltpu.VMEM((blocks, 8, LANES), f32),
-            pltpu.SemaphoreType.DMA((blocks,)),
-            pltpu.SemaphoreType.DMA((len(w_parts),)),
         ],
         compiler_params=params(16),
         name="closing_pass",
-    )(info, *toks, *w_parts, *sums, pinned(energy))
+    )(u, w, *soft, *sums, pinned(energy))
 
 
 def grad_kernel(images, info_ref, rows_ref, own_ref, *refs):
     sums = refs[0:SIDE]
-    (u, ut, w, e, keep_ref, *sends, loss_ref, soft_w, mass_w, acc, totals, soft_all,
+    (u, ut, w, e, out_ref, loss_ref, soft_w, mass_w, acc, totals, soft_all,
      mass_all) = refs[SIDE:]
     blocks, slots, cols = e.shape
     totals[...] = added(rows_ref)
@@ -467,20 +537,20 @@
         units = jnp.concatenate([ut[2 * s], ut[2 * s + 1]], axis=1)
         for n in chunks(cols, WIDE):
             raws = [nn(u[2 * s + half], w[:, n]) for half in range(2)]
-            columns = []
-            for i in range(0, WIDE, LANES):
-                k = slice(n.start + i, n.start + i + LANES)
-                parts = []
-                for half in range(2):
-                    b = 2 * s + half
-                    for r in chunks(slots, ROWS):
-                        at = slice(half * slots + r.start, half * slots + r.stop)
+            parts = []
+            for half in range(2):
+                b = 2 * s + half
+                for r in chunks(slots, ROWS):
+                    at = slice(half * slots + r.start, half * slots + r.stop)
+                    soft_r, mass_r = soft_w[at, :], mass_w[at, :]
+                    line = []
+                    for i in range(0, WIDE, LANES):
+                        k = slice(n.start + i, n.start + i + LANES)
                         power = raws[half][r, i : i + LANES] * scale[:, k]
-                        soft = jnp.exp2(power) * soft_w[at, :]
-                        target = e[b, r, k].astype(f32) * c[:, k] * mass_w[at, :]
-                        parts.append((soft - target).astype(bf16))
-                columns.append(jnp.concatenate(parts, axis=0))
-            acc[:, n] += nn(units, jnp.concatenate(columns, axis=1))
+                        target = e[b, r, k].astype(f32) * c[:, k] * mass_r
+                        line.append((jnp.exp2(power) * soft_r - target).astype(bf16))
+                    parts.append(jnp.concatenate(line, axis=1))
+            acc[:, n] += nn(units, jnp.concatenate(parts, axis=0))
         return 0
 
     lax.fori_loop(0, blocks // 2, step, 0)
@@ -488,21 +558,22 @@
     unit = w[...].astype(f32) * inv
     dot = jnp.sum(grad * unit, axis=0, keepdims=True)
     acc[...] = inv * (grad - unit * dot)
-    rows = keep_ref.shape[0]
-    keep_ref[...] = acc[0:rows, :]
-    for i, ref in enumerate(sends):
-        ref[...] = acc[(i + 1) * rows : (i + 2) * rows, :].astype(bf16)
-
-
-def grad_pass(images, info, rows, own, sums, u, ut, w, energy):
+    rows = out_ref.shape[1]
+    for i, k in enumerate((0,) + SHIFTS):
+        y = (info_ref[2] + 4 - k) & 3
+        for q in range(8):
+            at = (8 * i + q) * rows
+            out_ref[(q // 2) * 8 + 2 * y + q % 2] = acc[at : at + rows, :].astype(bf16)
+
+
+def grad_pass(images, info, rows, own, sums, u, ut, w, energy, peers):
     blocks, slots, cols = energy.shape
     d = ut.shape[1]
-    part = (d // SIDE, cols)
     return pl.pallas_call(
         functools.partial(grad_kernel, float(images)),
-        out_shape=(shape(part), *[shape(part, bf16)] * len(SHIFTS), shape((PER, LANES))),
+        out_shape=(shape((peers, d // peers, cols), bf16), shape((PER, LANES))),
         in_specs=[SM] + [VM] * (SIDE + 6),
-        out_specs=(VM,) * 5,
+        out_specs=(VM, VM),
         scratch_shapes=[
             pltpu.VMEM((2 * slots, LANES), f32),
             pltpu.VMEM((2 * slots, LANES), f32),
@@ -516,6 +587,28 @@
     )(info, rows, own, *sums, u, ut, w, pinned(energy))
 
 
+def sum_kernel(parts_ref, out_ref):
+    peers, _, width = parts_ref.shape
+    for q in range(peers // SIDE):
+        first = (q // 2) * 2 * SIDE + q % 2
+        total = parts_ref[first].astype(f32)
+        for y in range(1, SIDE):
+            total = total + parts_ref[first + 2 * y].astype(f32)
+        out_ref[:, q * width : (q + 1) * width] = total
+
+
+def sum_pass(parts):
+    peers, rows, width = parts.shape
+    return pl.pallas_call(
+        sum_kernel,
+        out_shape=shape((rows, peers // SIDE * width)),
+        in_specs=[VM],
+        out_specs=VM,
+        compiler_params=params(16),
+        name="sum_pass",
+    )(parts)
+
+
 def shift(value, axis, k):
     n = lax.axis_size(axis)
     return lax.ppermute(value, axis, [(i, (i + k) % n) for i in range(n)])
@@ -529,48 +622,42 @@
     return [value] + [shift(value, axis, k) for k in SHIFTS]
 
 
-def both_cores(blocks):
-    return blocks + [shift(b, "c", 1) for b in blocks]
-
-
 def local(teacher_feat, student_feat, teacher_proto, student_proto, mask_index, mask_count):
     slots = mask_index.shape[0]
-    images = lax.axis_size(("z", "y", "c")) * (teacher_feat.shape[0] // PATCH)
+    images = lax.axis_size(DP) * (teacher_feat.shape[0] // PATCH)
     peers = lax.axis_size(GROUP)
-    me = lax.axis_index(("z", "y", "c")).reshape(1)
-    t_tok, s_tok, w, info = tokens(
+    me = lax.axis_index(DP).reshape(1)
+    tok, w, info = tokens(
         me, mask_count, mask_index, teacher_feat, student_feat, teacher_proto, student_proto
     )
     w = exchange(w, ("z", "c"))
-    s_toks = ring(s_tok, "z")
-    t_w, t_tok = split(0, w, t_tok, s_toks)
-    t_parts = ring(t_w, "y")
-    t_toks = both_cores(ring(t_tok, "z"))
-    s_toks = both_cores(s_toks)
-    s_w, _ = split(1, w, s_tok, t_parts)
-    s_parts = ring(s_w, "y")
-    energy, own, sums = energy_pass(info, t_toks, t_parts, slots, [s_w, *s_toks])
-    for i in range(SWEEPS - 1):
-        after = s_parts if i == 0 else []
-        rows = exchange(row_pass(ring(sums, "y"), energy, peers, after), GROUP)
-        sums = column_pass(rows, own, energy)
-    sums = ring(sums, "y")
-    s_u, s_ut, s_w, rows = closing_pass(info, s_toks, s_parts, sums, energy, peers)
+    t_parts = ring(split(0, w), "y")
+    t_mine, s_mine = stack(info, ring(tok, "z"), slots, t_parts[1:])
+    t_toks, s_toks = ([v, shift(v, "c", 1)] for v in (t_mine, s_mine))
+    s_parts = ring(split(1, w, t_parts[1:]), "y")
+    energy, own, sums = energy_pass(info, t_toks, t_parts, slots, s_parts[:1])
+    sums, s_w, s_u = collect(info, sums, s_parts, s_toks)
+    half = s_u.shape[0] // 2
+    soft = []
+    for _ in range(SWEEPS - 1):
+        rows = row_pass(ring(sums, "y"), energy, peers, soft)
+        soft.append(softmax_pass(s_u, s_w, half * len(soft), half))
+        sums = column_pass(exchange(rows, GROUP), own, energy)
+    ring_sums = ring(sums, "y")
+    s_ut, rows = closing_pass(s_u, s_w, soft, ring_sums, energy, peers)
     rows = exchange(rows, GROUP)
-    keep, *sends, loss = grad_pass(images, info, rows, own, sums, s_u, s_ut, s_w, energy)
-    for k, send in zip(SHIFTS, sends):
-        keep = keep + shift(send, "y", -k).astype(f32)
-    proto_grad = lax.all_to_all(keep, ("z", "c"), 0, 1, tiled=True)
-    return (loss.reshape(-1), proto_grad)
+    grad, loss = grad_pass(
+        images, info, rows, own, ring_sums, s_u, s_ut, s_w, energy, lax.axis_size(DP)
+    )
+    return (loss.reshape(-1), sum_pass(exchange(grad, DP)))
 
 
 def solution(mesh):
     parts = Mesh(mesh.devices.reshape(4, 4, 2, 4), ("z", "y", "c", "x"))
-    dp = ("z", "y", "c")
     return jax.shard_map(
         local,
         mesh=parts,
-        in_specs=(P(dp, None), P(dp, None), P(dp, "x"), P(dp, "x"), P(dp), P(dp)),
-        out_specs=(P(dp), P(dp, "x")),
+        in_specs=(P(DP, None), P(DP, None), P(DP, "x"), P(DP, "x"), P(DP), P(DP)),
+        out_specs=(P(DP), P(DP, "x")),
         check_vma=False,
     )

time: 205 us -> 181 us (0.88)
  waiting for transfers between devices: 40.8 us -> 23.5 us
  starting transfers between devices: 40 us -> 29.7 us
  blocking collectives: 63.5 us -> 70.8 us
  local copies, waits for them, and re-layouts: 2.66 us -> 0.01 us
    ppermute x32 -> x20, waiting for transfers between devices: 40.8 us -> 18.3 us  [shift(): return lax.ppermute(value, axis, [(i, (i + k) % n) for i in range(n)])]
    all_to_all x3 -> x4, blocking collectives: 49.7 us -> 70.8 us  [exchange(): return lax.all_to_all(value, axes, 0, 0, tiled=True)]
    all_to_all x1 -> x0, blocking collectives: 13.8 us -> none  [local(): proto_grad = lax.all_to_all(keep, ('z', 'c'), 0, 1, tiled=True)]
    ppermute x32 -> x20, starting transfers between devices: 33.2 us -> 22.8 us  [shift(): return lax.ppermute(value, axis, [(i, (i + k) % n) for i in range(n)])]
    all_to_all x1, waiting for transfers between devices: 0.01 us -> 5.17 us  [exchange(): return lax.all_to_all(value, axes, 0, 0, tiled=True)]
    unnamed x9 -> x4, local copies, waits for them, and re-layouts: 2.66 us -> 0.01 us
    pallas_call x4 -> x9, Pallas kernels: 21.3 us -> 21.4 us  [the longest x1 8.03 us: closing_pass(): pl.pallas_call(closing_kernel, out_shape=(pltpu.VMEM((blocks, d, slots),...]
  transfers between devices with their start and end apart: 33 -> 21, of which waited for: 16 -> 10; matrix products, arithmetic and copies ran while one was open for 0% -> 0% of each run, Pallas kernels for 5% -> 8%
where the time goes in v3:
time: 181 us
  blocking collectives  70.8 us (39%)
  Pallas kernels  55.4 us (31%)
  starting transfers between devices  29.7 us (16%)
  waiting for transfers between devices  23.5 us (13%)
    all_to_all x4, blocking collectives, exchange(): return lax.all_to_all(value, axes, 0, 0, tiled=True)  70.8 us
    ppermute x20, starting transfers between devices, shift(): return lax.ppermute(value, axis, [(i, (i + k) % n) for i in range(n)])  22.8 us
    ppermute x20, waiting for transfers between devices, shift(): return lax.ppermute(value, axis, [(i, (i + k) % n) for i in range(n)])  18.3 us
    pallas_call x1, Pallas kernels, grad_pass(): pl.pallas_call(functools.partial(grad_kernel, float(images)), out_shape=(...  11.6 us
    pallas_call x1, Pallas kernels, energy_pass(): pl.pallas_call(energy_kernel, out_shape=(pltpu.VMEM((blocks, slots, cols)...  9.47 us
    pallas_call x1, Pallas kernels, closing_pass(): pl.pallas_call(closing_kernel, out_shape=(pltpu.VMEM((blocks, d, slots),...  8.03 us
    all_to_all x1, starting transfers between devices, exchange(): return lax.all_to_all(value, axes, 0, 0, tiled=True)  6.96 us
    pallas_call x2, Pallas kernels, column_pass(): pl.pallas_call(column_kernel, out_shape=shape((1, cols)), in_specs=[VM, V...  6.68 us
  transfers between devices with their start and end apart: 21, of which 10 were waited for; matrix products, arithmetic and copies ran while one was open for 0% of the time, Pallas kernels for 8%

profile of v3, /device:TPU:1, one launch (start us, length us, event | category | flops | bytes accessed | tf_op | source)
XLA Modules:
  0.0 180.9 jit_solution(4766187877409427085)
XLA Ops:
  1.3 5.5 %token_rows.1 = (bf16[784,256]{1,0:T(8,128)(2,1)}, bf16[8,16,2048]{2,1,0:T(8,128)(2,1)}, s32[3]{0:T(128)}) custom-call(s32[1]{0:T(128)} %bitcast.me_ref, s32[1]{0:T(128)S(6)} %copy.8.count_ref, s32[384]{0:T(512)} %index_ref.1, bf16[2048,256]{1,0:T(8,128)(2,1)} %teacher_ref.1, bf16[2048,256]{1,0:T(8,128)(2,1)} %student_ref.1, bf16[8,16384]{1,0:T(8,128)(2,1)} %tp_ref.1, ...), custom_call_target="tpu_custom_call" | custom-call | tf_op jit(solution)/shard_map/token_rows/pallas_call | solution.py:120
  6.9 7.0 %all-to-all-start = ((bf16[8,16,2048]{2,1,0:T(8,128)(2,1)}), bf16[8,16,2048]{2,1,0:T(8,128)(2,1)S(1)}, u32[]{:S(2)}, u32[]{:S(2)}) async-start(bf16[8,16,2048]{2,1,0:T(8,128)(2,1)} %get-tuple-element.19), calls=%async_computation | async-start | bytes 1048576 | tf_op jit(solution)/shard_map/all_to_all | solution.py:618
  13.8 2.9 %collective-permute-start.2 = (bf16[784,256]{1,0:T(8,128)(2,1)}, bf16[784,256]{1,0:T(8,128)(2,1)S(1)}, u32[]{:S(2)}, u32[]{:S(2)}) collective-permute-start(bf16[784,256]{1,0:T(8,128)(2,1)} %get-tuple-element.18.refs_0_), channel_id=1, source_target_pairs={{0,64},{32,96},{64,0},{96,32},{1,65},{33,97},{65,1},{97,33},{2,66}... | collective-permute-start | bytes 1204232 | tf_op jit(solution)/shard_map/ppermute | solution.py:614
  16.7 0.9 collective-permute-start.1
  17.6 0.6 collective-permute-start
  18.2 5.2 %all-to-all-done.w_ref = bf16[8,16,2048]{2,1,0:T(8,128)(2,1)S(1)} async-done(((bf16[8,16,2048]{2,1,0:T(8,128)(2,1)}), bf16[8,16,2048]{2,1,0:T(8,128)(2,1)S(1)}, u32[]{:S(2)}, u32[]{:S(2)}) %all-to-all-start) | async-done | bytes 524320 | tf_op jit(solution)/shard_map/all_to_all | solution.py:618
  23.4 3.0 %collective-permute-start.5 = (bf16[64,2048]{1,0:T(8,128)(2,1)S(1)}, bf16[64,2048]{1,0:T(8,128)(2,1)S(1)}, u32[]{:S(2)}, u32[]{:S(2)}) collective-permute-start(bf16[64,2048]{1,0:T(8,128)(2,1)S(1)} %split_rows.2.refs_2_), channel_id=1, source_target_pairs={{0,16},{8,24},{16,0},{24,8},{1,17},{9,25},{17,1},{25,9},{2,18},{10... | collective-permute-start | bytes 786440 | tf_op jit(solution)/shard_map/ppermute | solution.py:614
  26.4 0.8 collective-permute-start.4
  27.1 4.8 %collective-permute-done.2.refs_3_ = bf16[784,256]{1,0:T(8,128)(2,1)S(1)} collective-permute-done((bf16[784,256]{1,0:T(8,128)(2,1)}, bf16[784,256]{1,0:T(8,128)(2,1)S(1)}, u32[]{:S(2)}, u32[]{:S(2)}) %collective-permute-start.2) | collective-permute-done | bytes 401440 | tf_op jit(solution)/shard_map/ppermute | solution.py:614
  31.9 1.3 collective-permute-start.3
  33.2 5.8 %collective-permute-done.1.refs_2_ = bf16[784,256]{1,0:T(8,128)(2,1)S(1)} collective-permute-done((bf16[784,256]{1,0:T(8,128)(2,1)}, bf16[784,256]{1,0:T(8,128)(2,1)S(1)}, u32[]{:S(2)}, u32[]{:S(2)}) %collective-permute-start.1) | collective-permute-done | bytes 401440 | tf_op jit(solution)/shard_map/ppermute | solution.py:614
  39.0 1.7 collective-permute-done.refs_1_
  40.7 0.0 collective-permute-done.5.refs_6_.refs_2_.refs_5_
  40.7 0.7 stack.1
  41.4 1.3 collective-permute-start.6
  42.7 0.1 collective-permute-start.10
  42.8 2.4 %collective-permute-start.9 = (bf16[64,2048]{1,0:T(8,128)(2,1)S(1)}, bf16[64,2048]{1,0:T(8,128)(2,1)S(1)}, u32[]{:S(2)}, u32[]{:S(2)}) collective-permute-start(bf16[64,2048]{1,0:T(8,128)(2,1)S(1)} %split_rows.3.refs_6_.refs_0_), channel_id=1, source_target_pairs={{0,16},{8,24},{16,0},{24,8},{1,17},{9,25},{17,1},{25,9},{2,18},{10... | collective-permute-start | bytes 786440 | tf_op jit(solution)/shard_map/ppermute | solution.py:614
  45.2 0.8 collective-permute-start.8
  45.9 0.7 collective-permute-start.7
  46.6 9.5 %energy_pass.1 = (bf16[8,384,2048]{2,1,0:T(8,128)(2,1)S(1)}, f32[32,128]{1,0:T(8,128)S(1)}, f32[1,2048]{1,0:T(1,128)S(1)}) custom-call(s32[3]{0:T(128)S(1)} %copy-done.1, bf16[4,400,256]{2,1,0:T(8,128)(2,1)S(1)} %get-tuple-element.20.refs_0_, bf16[4,400,256]{2,1,0:T(8,128)(2,1)S(1)} %collective-permute-done.6.refs_1_, ...), custom_call_target="tpu_custom_call" | custom-call | flops 3221225472 | bytes 12582912 | tf_op jit(solution)/shard_map/energy_pass/pallas_call | solution.py:291
  56.1 1.1 collective-permute-done.8.refs_2_
  57.2 1.0 collective-permute-done.7.refs_1_
  58.2 0.7 collect.1
  59.0 2.4 %collective-permute-start.13 = (f32[1,2048]{1,0:T(1,128)S(1)}, f32[1,2048]{1,0:T(1,128)S(1)}, u32[]{:S(2)}, u32[]{:S(2)}) collective-permute-start(f32[1,2048]{1,0:T(1,128)S(1)} %get-tuple-element.25.refs_0_), channel_id=1, source_target_pairs={{0,16},{8,24},{16,0},{24,8},{1,17},{9,25},{17,1},{25,9},{2,18},{10... | collective-permute-start | bytes 24584 | tf_op jit(solution)/shard_map/ppermute | solution.py:614
  61.3 0.8 collective-permute-start.12
  62.1 0.7 collective-permute-start.11
  62.8 0.2 collective-permute-done.13.refs_3_
  63.0 1.1 collective-permute-done.12.refs_2_
  64.1 1.7 collective-permute-done.11.refs_1_
  65.8 3.1 %row_pass.2 = bf16[32,32,128]{2,1,0:T(8,128)(2,1)S(1)} custom-call(f32[1,2048]{1,0:T(1,128)S(1)} %get-tuple-element.25.refs_0_, f32[1,2048]{1,0:T(1,128)S(1)} %collective-permute-done.11.refs_1_, f32[1,2048]{1,0:T(1,128)S(1)} %collective-permute-done.12.refs_2_, f32[1,2048]{1,0:T(1,128)S(1)} %collective-permute-done.13.refs_3_, ...), custom_call_target="tpu_custom_call" | custom-call | tf_op jit(solution)/shard_map/row_pass/pallas_call | solution.py:370
  68.9 17.8 %all_to_all.25.rows_ref = bf16[32,32,128]{2,1,0:T(8,128)(2,1)S(1)} all-to-all(bf16[32,32,128]{2,1,0:T(8,128)(2,1)S(1)} %row_pass.2), channel_id=1, replica_groups=mesh['z'=4,'y'=4,'c'=2,'x'=4] {'z','c','x'}, dimensions={0} | all-to-all | bytes 524288 | tf_op jit(solution)/shard_map/all_to_all | solution.py:618
  86.7 3.3 %column_pass.2.refs_0_ = f32[1,2048]{1,0:T(1,128)S(1)} custom-call(bf16[32,32,128]{2,1,0:T(8,128)(2,1)S(1)} %all_to_all.25.rows_ref, f32[32,128]{1,0:T(8,128)S(1)} %get-tuple-element.27.own_ref, bf16[8,384,2048]{2,1,0:T(8,128)(2,1)S(1)} %get-tuple-element.26.refs_4_.e.refs_8_.refs_7_), custom_call_target="tpu_custom_call" | custom-call | tf_op jit(solution)/shard_map/column_pass/pallas_call | solution.py:402
  90.1 0.1 collective-permute-start.16
  90.2 1.7 collective-permute-start.15
  91.9 2.8 %softmax_pass.2.refs_5_.refs_2_ = f32[12,128]{1,0:T(8,128)S(1)} custom-call(bf16[8,384,256]{2,1,0:T(8,128)(2,1)S(1)} %get-tuple-element.23.u.refs_0_.refs_4_, bf16[256,2048]{1,0:T(8,128)(2,1)S(1)} %get-tuple-element.24.w.refs_1_.refs_6_), custom_call_target="tpu_custom_call" | custom-call | flops 1610612736 | bytes 393216 | tf_op jit(solution)/shard_map/softmax_pass/pallas_call | solution.py:441
  94.7 0.9 collective-permute-done.14.refs_1_
  95.6 3.1 %row_pass.3 = bf16[32,32,128]{2,1,0:T(8,128)(2,1)S(1)} custom-call(f32[1,2048]{1,0:T(1,128)S(1)} %column_pass.2.refs_0_, f32[1,2048]{1,0:T(1,128)S(1)} %collective-permute-done.14.refs_1_, f32[1,2048]{1,0:T(1,128)S(1)} %collective-permute-done.15.refs_2_, f32[1,2048]{1,0:T(1,128)S(1)} %collective-permute-done.16.refs_3_, ...), custom_call_target="tpu_custom_call" | custom-call | tf_op jit(solution)/shard_map/row_pass/pallas_call | solution.py:370
  98.7 14.7 %all_to_all.26.rows_ref = bf16[32,32,128]{2,1,0:T(8,128)(2,1)S(1)} all-to-all(bf16[32,32,128]{2,1,0:T(8,128)(2,1)S(1)} %row_pass.3), channel_id=1, replica_groups=mesh['z'=4,'y'=4,'c'=2,'x'=4] {'z','c','x'}, dimensions={0} | all-to-all | bytes 524288 | tf_op jit(solution)/shard_map/all_to_all | solution.py:618
  113.4 3.3 %column_pass.3.refs_4_.refs_0_ = f32[1,2048]{1,0:T(1,128)S(1)} custom-call(bf16[32,32,128]{2,1,0:T(8,128)(2,1)S(1)} %all_to_all.26.rows_ref, f32[32,128]{1,0:T(8,128)S(1)} %get-tuple-element.27.own_ref, bf16[8,384,2048]{2,1,0:T(8,128)(2,1)S(1)} %get-tuple-element.26.refs_4_.e.refs_8_.refs_7_), custom_call_target="tpu_custom_call" | custom-call | tf_op jit(solution)/shard_map/column_pass/pallas_call | solution.py:402
  116.7 1.0 collective-permute-start.19
  117.8 0.3 collective-permute-start.18
  118.1 1.1 collective-permute-start.17
  119.2 2.8 %softmax_pass.3.refs_3_ = f32[12,128]{1,0:T(8,128)S(1)} custom-call(bf16[8,384,256]{2,1,0:T(8,128)(2,1)S(1)} %get-tuple-element.23.u.refs_0_.refs_4_, bf16[256,2048]{1,0:T(8,128)(2,1)S(1)} %get-tuple-element.24.w.refs_1_.refs_6_), custom_call_target="tpu_custom_call" | custom-call | flops 1610612736 | bytes 393216 | tf_op jit(solution)/shard_map/softmax_pass/pallas_call | solution.py:441
  122.0 8.0 %closing_pass.1 = (bf16[8,256,384]{2,1,0:T(8,128)(2,1)S(1)}, bf16[32,64,128]{2,1,0:T(8,128)(2,1)S(1)}) custom-call(bf16[8,384,256]{2,1,0:T(8,128)(2,1)S(1)} %get-tuple-element.23.u.refs_0_.refs_4_, bf16[256,2048]{1,0:T(8,128)(2,1)S(1)} %get-tuple-element.24.w.refs_1_.refs_6_, f32[12,128]{1,0:T(8,128)S(1)} %softmax_pass.2.refs_5_.refs_2_, ...), custom_call_target="tpu_custom_call" | custom-call | tf_op jit(solution)/shard_map/closing_pass/pallas_call | solution.py:495
  130.1 16.8 %all_to_all.27.rows_ref = bf16[32,64,128]{2,1,0:T(8,128)(2,1)S(1)} all-to-all(bf16[32,64,128]{2,1,0:T(8,128)(2,1)S(1)} %get-tuple-element.28), channel_id=1, replica_groups=mesh['z'=4,'y'=4,'c'=2,'x'=4] {'z','c','x'}, dimensions={0} | all-to-all | bytes 1048576 | tf_op jit(solution)/shard_map/all_to_all | solution.py:618
  146.9 11.6 %grad_pass.1 = (bf16[32,8,2048]{2,1,0:T(8,128)(2,1)S(1)}, f32[3,128]{1,0:T(4,128)}) custom-call(s32[3]{0:T(128)S(1)} %copy-done.1, bf16[32,64,128]{2,1,0:T(8,128)(2,1)S(1)} %all_to_all.27.rows_ref, f32[32,128]{1,0:T(8,128)S(1)} %get-tuple-element.27.own_ref, f32[1,2048]{1,0:T(1,128)S(1)} %column_pass.3.refs_4_.refs_0_, ...), custom_call_target="tpu_custom_call" | custom-call | tf_op jit(solution)/shard_map/grad_pass/pallas_call | solution.py:572
  158.4 21.5 %all_to_all.28.parts_ref = bf16[32,8,2048]{2,1,0:T(8,128)(2,1)S(1)} all-to-all(bf16[32,8,2048]{2,1,0:T(8,128)(2,1)S(1)} %get-tuple-element.31), channel_id=1, replica_groups=mesh['z'=4,'y'=4,'c'=2,'x'=4] {'z','y','c'}, dimensions={0} | all-to-all | bytes 2097152 | tf_op jit(solution)/shard_map/all_to_all | solution.py:618
  180.0 0.9 sum_pass.1
  (17 shorter events, 0.1 us)
Async XLA Ops:
  6.8 33.9 %copy-start = (bf16[784,256]{1,0:T(8,128)(2,1)S(1)}, bf16[784,256]{1,0:T(8,128)(2,1)}, u32[]{:S(2)}) copy-start(bf16[784,256]{1,0:T(8,128)(2,1)} %get-tuple-element.18.refs_0_) | copy-start | bytes 1204228
  6.9 33.9 %copy-start.1 = (s32[3]{0:T(128)S(1)}, s32[3]{0:T(128)}, u32[]{:S(2)}) copy-start(s32[3]{0:T(128)} %get-tuple-element.17.info_ref) | copy-start | bytes 40
  6.9 16.5 %all-to-all-start = ((bf16[8,16,2048]{2,1,0:T(8,128)(2,1)}), bf16[8,16,2048]{2,1,0:T(8,128)(2,1)S(1)}, u32[]{:S(2)}, u32[]{:S(2)}) async-start(bf16[8,16,2048]{2,1,0:T(8,128)(2,1)} %get-tuple-element.19), calls=%async_computation | async-start | bytes 1048576 | tf_op jit(solution)/shard_map/all_to_all | solution.py:618
  13.8 18.1 %collective-permute-start.2 = (bf16[784,256]{1,0:T(8,128)(2,1)}, bf16[784,256]{1,0:T(8,128)(2,1)S(1)}, u32[]{:S(2)}, u32[]{:S(2)}) collective-permute-start(bf16[784,256]{1,0:T(8,128)(2,1)} %get-tuple-element.18.refs_0_), channel_id=1, source_target_pairs={{0,64},{32,96},{64,0},{96,32},{1,65},{33,97},{65,1},{97,33},{2,66}... | collective-permute-start | bytes 1204232 | tf_op jit(solution)/shard_map/ppermute | solution.py:614
  16.7 22.3 %collective-permute-start.1 = (bf16[784,256]{1,0:T(8,128)(2,1)}, bf16[784,256]{1,0:T(8,128)(2,1)S(1)}, u32[]{:S(2)}, u32[]{:S(2)}) collective-permute-start(bf16[784,256]{1,0:T(8,128)(2,1)} %get-tuple-element.18.refs_0_), channel_id=1, source_target_pairs={{0,96},{32,0},{64,32},{96,64},{1,97},{33,1},{65,33},{97,65},{2,98}... | collective-permute-start | bytes 1204232 | tf_op jit(solution)/shard_map/ppermute | solution.py:614
  17.6 23.1 %collective-permute-start = (bf16[784,256]{1,0:T(8,128)(2,1)}, bf16[784,256]{1,0:T(8,128)(2,1)S(1)}, u32[]{:S(2)}, u32[]{:S(2)}) collective-permute-start(bf16[784,256]{1,0:T(8,128)(2,1)} %get-tuple-element.18.refs_0_), channel_id=1, source_target_pairs={{0,32},{32,64},{64,96},{96,0},{1,33},{33,65},{65,97},{97,1},{2,34}... | collective-permute-start | bytes 1204232 | tf_op jit(solution)/shard_map/ppermute | solution.py:614
  23.4 17.3 %collective-permute-start.5 = (bf16[64,2048]{1,0:T(8,128)(2,1)S(1)}, bf16[64,2048]{1,0:T(8,128)(2,1)S(1)}, u32[]{:S(2)}, u32[]{:S(2)}) collective-permute-start(bf16[64,2048]{1,0:T(8,128)(2,1)S(1)} %split_rows.2.refs_2_), channel_id=1, source_target_pairs={{0,16},{8,24},{16,0},{24,8},{1,17},{9,25},{17,1},{25,9},{2,18},{10... | collective-permute-start | bytes 786440 | tf_op jit(solution)/shard_map/ppermute | solution.py:614
  26.4 14.4 %collective-permute-start.4 = (bf16[64,2048]{1,0:T(8,128)(2,1)S(1)}, bf16[64,2048]{1,0:T(8,128)(2,1)S(1)}, u32[]{:S(2)}, u32[]{:S(2)}) collective-permute-start(bf16[64,2048]{1,0:T(8,128)(2,1)S(1)} %split_rows.2.refs_2_), channel_id=1, source_target_pairs={{0,24},{8,0},{16,8},{24,16},{1,25},{9,1},{17,9},{25,17},{2,26},{10... | collective-permute-start | bytes 786440 | tf_op jit(solution)/shard_map/ppermute | solution.py:614
  31.9 8.8 %collective-permute-start.3 = (bf16[64,2048]{1,0:T(8,128)(2,1)S(1)}, bf16[64,2048]{1,0:T(8,128)(2,1)S(1)}, u32[]{:S(2)}, u32[]{:S(2)}) collective-permute-start(bf16[64,2048]{1,0:T(8,128)(2,1)S(1)} %split_rows.2.refs_2_), channel_id=1, source_target_pairs={{0,8},{8,16},{16,24},{24,0},{1,9},{9,17},{17,25},{25,1},{2,10},{10... | collective-permute-start | bytes 786440 | tf_op jit(solution)/shard_map/ppermute | solution.py:614
  41.4 5.2 %collective-permute-start.6 = (bf16[4,400,256]{2,1,0:T(8,128)(2,1)S(1)}, bf16[4,400,256]{2,1,0:T(8,128)(2,1)S(1)}, u32[]{:S(2)}, u32[]{:S(2)}) collective-permute-start(bf16[4,400,256]{2,1,0:T(8,128)(2,1)S(1)} %get-tuple-element.20.refs_0_), channel_id=1, source_target_pairs={{0,4},{4,0},{1,5},{5,1},{2,6},{6,2},{3,7},{7,3},{8,12},{12,8},{9,1... | collective-permute-start | bytes 2457608 | tf_op jit(solution)/shard_map/ppermute | solution.py:614
  42.7 15.5 %collective-permute-start.10 = (bf16[4,384,256]{2,1,0:T(8,128)(2,1)S(1)}, bf16[4,384,256]{2,1,0:T(8,128)(2,1)S(1)}, u32[]{:S(2)}, u32[]{:S(2)}) collective-permute-start(bf16[4,384,256]{2,1,0:T(8,128)(2,1)S(1)} %get-tuple-element.22.refs_4_), channel_id=1, source_target_pairs={{0,4},{4,0},{1,5},{5,1},{2,6},{6,2},{3,7},{7,3},{8,12},{12,8},{9,1... | collective-permute-start | bytes 2359304 | tf_op jit(solution)/shard_map/ppermute | solution.py:614
  42.8 13.3 %collective-permute-start.9 = (bf16[64,2048]{1,0:T(8,128)(2,1)S(1)}, bf16[64,2048]{1,0:T(8,128)(2,1)S(1)}, u32[]{:S(2)}, u32[]{:S(2)}) collective-permute-start(bf16[64,2048]{1,0:T(8,128)(2,1)S(1)} %split_rows.3.refs_6_.refs_0_), channel_id=1, source_target_pairs={{0,16},{8,24},{16,0},{24,8},{1,17},{9,25},{17,1},{25,9},{2,18},{10... | collective-permute-start | bytes 786440 | tf_op jit(solution)/shard_map/ppermute | solution.py:614
  45.2 12.1 %collective-permute-start.8 = (bf16[64,2048]{1,0:T(8,128)(2,1)S(1)}, bf16[64,2048]{1,0:T(8,128)(2,1)S(1)}, u32[]{:S(2)}, u32[]{:S(2)}) collective-permute-start(bf16[64,2048]{1,0:T(8,128)(2,1)S(1)} %split_rows.3.refs_6_.refs_0_), channel_id=1, source_target_pairs={{0,24},{8,0},{16,8},{24,16},{1,25},{9,1},{17,9},{25,17},{2,26},{10... | collective-permute-start | bytes 786440 | tf_op jit(solution)/shard_map/ppermute | solution.py:614
  45.9 12.3 %collective-permute-start.7 = (bf16[64,2048]{1,0:T(8,128)(2,1)S(1)}, bf16[64,2048]{1,0:T(8,128)(2,1)S(1)}, u32[]{:S(2)}, u32[]{:S(2)}) collective-permute-start(bf16[64,2048]{1,0:T(8,128)(2,1)S(1)} %split_rows.3.refs_6_.refs_0_), channel_id=1, source_target_pairs={{0,8},{8,16},{16,24},{24,0},{1,9},{9,17},{17,25},{25,1},{2,10},{10... | collective-permute-start | bytes 786440 | tf_op jit(solution)/shard_map/ppermute | solution.py:614
  59.0 4.1 %collective-permute-start.13 = (f32[1,2048]{1,0:T(1,128)S(1)}, f32[1,2048]{1,0:T(1,128)S(1)}, u32[]{:S(2)}, u32[]{:S(2)}) collective-permute-start(f32[1,2048]{1,0:T(1,128)S(1)} %get-tuple-element.25.refs_0_), channel_id=1, source_target_pairs={{0,16},{8,24},{16,0},{24,8},{1,17},{9,25},{17,1},{25,9},{2,18},{10... | collective-permute-start | bytes 24584 | tf_op jit(solution)/shard_map/ppermute | solution.py:614
  61.3 2.8 %collective-permute-start.12 = (f32[1,2048]{1,0:T(1,128)S(1)}, f32[1,2048]{1,0:T(1,128)S(1)}, u32[]{:S(2)}, u32[]{:S(2)}) collective-permute-start(f32[1,2048]{1,0:T(1,128)S(1)} %get-tuple-element.25.refs_0_), channel_id=1, source_target_pairs={{0,24},{8,0},{16,8},{24,16},{1,25},{9,1},{17,9},{25,17},{2,26},{10... | collective-permute-start | bytes 24584 | tf_op jit(solution)/shard_map/ppermute | solution.py:614
  62.1 3.7 %collective-permute-start.11 = (f32[1,2048]{1,0:T(1,128)S(1)}, f32[1,2048]{1,0:T(1,128)S(1)}, u32[]{:S(2)}, u32[]{:S(2)}) collective-permute-start(f32[1,2048]{1,0:T(1,128)S(1)} %get-tuple-element.25.refs_0_), channel_id=1, source_target_pairs={{0,8},{8,16},{16,24},{24,0},{1,9},{9,17},{17,25},{25,1},{2,10},{10... | collective-permute-start | bytes 24584 | tf_op jit(solution)/shard_map/ppermute | solution.py:614
  90.1 4.6 %collective-permute-start.16 = (f32[1,2048]{1,0:T(1,128)S(1)}, f32[1,2048]{1,0:T(1,128)S(1)}, u32[]{:S(2)}, u32[]{:S(2)}) collective-permute-start(f32[1,2048]{1,0:T(1,128)S(1)} %column_pass.2.refs_0_), channel_id=1, source_target_pairs={{0,16},{8,24},{16,0},{24,8},{1,17},{9,25},{17,1},{25,9},{2,18},{10... | collective-permute-start | bytes 24584 | tf_op jit(solution)/shard_map/ppermute | solution.py:614
  90.2 4.5 %collective-permute-start.15 = (f32[1,2048]{1,0:T(1,128)S(1)}, f32[1,2048]{1,0:T(1,128)S(1)}, u32[]{:S(2)}, u32[]{:S(2)}) collective-permute-start(f32[1,2048]{1,0:T(1,128)S(1)} %column_pass.2.refs_0_), channel_id=1, source_target_pairs={{0,24},{8,0},{16,8},{24,16},{1,25},{9,1},{17,9},{25,17},{2,26},{10... | collective-permute-start | bytes 24584 | tf_op jit(solution)/shard_map/ppermute | solution.py:614
  91.9 3.7 %collective-permute-start.14 = (f32[1,2048]{1,0:T(1,128)S(1)}, f32[1,2048]{1,0:T(1,128)S(1)}, u32[]{:S(2)}, u32[]{:S(2)}) collective-permute-start(f32[1,2048]{1,0:T(1,128)S(1)} %column_pass.2.refs_0_), channel_id=1, source_target_pairs={{0,8},{8,16},{16,24},{24,0},{1,9},{9,17},{17,25},{25,1},{2,10},{10... | collective-permute-start | bytes 24584 | tf_op jit(solution)/shard_map/ppermute | solution.py:614
  116.7 5.3 %collective-permute-start.19 = (f32[1,2048]{1,0:T(1,128)S(1)}, f32[1,2048]{1,0:T(1,128)S(1)}, u32[]{:S(2)}, u32[]{:S(2)}) collective-permute-start(f32[1,2048]{1,0:T(1,128)S(1)} %column_pass.3.refs_4_.refs_0_), channel_id=1, source_target_pairs={{0,16},{8,24},{16,0},{24,8},{1,17},{9,25},{17,1},{25,9},{2,18},{10... | collective-permute-start | bytes 24584 | tf_op jit(solution)/shard_map/ppermute | solution.py:614
  117.8 4.3 %collective-permute-start.18 = (f32[1,2048]{1,0:T(1,128)S(1)}, f32[1,2048]{1,0:T(1,128)S(1)}, u32[]{:S(2)}, u32[]{:S(2)}) collective-permute-start(f32[1,2048]{1,0:T(1,128)S(1)} %column_pass.3.refs_4_.refs_0_), channel_id=1, source_target_pairs={{0,24},{8,0},{16,8},{24,16},{1,25},{9,1},{17,9},{25,17},{2,26},{10... | collective-permute-start | bytes 24584 | tf_op jit(solution)/shard_map/ppermute | solution.py:614
  118.1 3.9 %collective-permute-start.17 = (f32[1,2048]{1,0:T(1,128)S(1)}, f32[1,2048]{1,0:T(1,128)S(1)}, u32[]{:S(2)}, u32[]{:S(2)}) collective-permute-start(f32[1,2048]{1,0:T(1,128)S(1)} %column_pass.3.refs_4_.refs_0_), channel_id=1, source_target_pairs={{0,8},{8,16},{16,24},{24,0},{1,9},{9,17},{17,25},{25,1},{2,10},{10... | collective-permute-start | bytes 24584 | tf_op jit(solution)/shard_map/ppermute | solution.py:614

commit v4 on v3

--- a/solution.py
+++ b/solution.py
@@ -16,6 +16,7 @@
 SURE = 192
 WIDE = 256
 PER = 3
+HALF = 16
 TALL = 32
 LANES = 128
 SHIFTS = (1, 3, 2)
@@ -177,23 +178,17 @@
     )(w, *after)
 
 
-def token_copies(info_ref, refs, dst, sems):
+def place(info_ref, refs, dst):
     core = info_ref[1]
-    return [
-        pltpu.make_async_copy(
-            ref.at[z], dst.at[2 * z + (1 - core if i else core)], sems.at[4 * i + z]
-        )
-        for i, ref in enumerate(refs)
-        for z in range(4)
-    ]
-
-
-def weight_copies(refs, dst, sems):
+    for i, ref in enumerate(refs):
+        for z in range(ref.shape[0]):
+            dst[2 * z + (1 - core if i else core)] = ref[z]
+
+
+def lay(refs, dst):
     rows = refs[0].shape[0]
-    return [
-        pltpu.make_async_copy(ref, dst.at[pl.ds(i * rows, rows)], sems.at[i])
-        for i, ref in enumerate(refs)
-    ]
+    for i, ref in enumerate(refs):
+        dst[i * rows : (i + 1) * rows, :] = ref[...]
 
 
 def inverse_norms(w_ref):
@@ -249,19 +244,13 @@
 
 def energy_kernel(info_ref, *refs):
     toks, w_refs = refs[0:2], refs[2:6]
-    e_ref, own_ref, sum_ref, u, w, live, acc, t_sems, w_sems = refs[-9:]
+    e_ref, own_ref, sum_ref, u, w, live, acc = refs[-7:]
     blocks, slots, cols = e_ref.shape
-    t_copies = token_copies(info_ref, toks, u, t_sems)
-    w_copies = weight_copies(w_refs, w, w_sems)
-    for c in t_copies + w_copies:
-        c.start()
-    for c in w_copies:
-        c.wait()
+    place(info_ref, toks, u)
+    lay(w_refs, w)
     scale = inverse_norms(w) * (LOG2E / teacher_temp)
     acc[...] = jnp.zeros_like(acc)
     own_ref[...] = jnp.zeros_like(own_ref)
-    for c in t_copies:
-        c.wait()
 
     def step(b, _):
         counts = u[b, slots : slots + EXTRA, :].astype(f32)
@@ -295,15 +284,13 @@
             shape((TALL, LANES)),
             shape((1, cols)),
         ),
-        in_specs=[SM] + [ANY] * (len(toks) + len(w_parts) + len(after)),
+        in_specs=[SM] + [VM] * (len(toks) + len(w_parts)) + [ANY] * len(after),
         out_specs=(VM, VM, VM),
         scratch_shapes=[
             pltpu.VMEM((blocks, slots + EXTRA, d), bf16),
             pltpu.VMEM((d, cols), bf16),
             pltpu.VMEM((slots, LANES), f32),
             pltpu.VMEM((ROWS, cols), f32),
-            pltpu.SemaphoreType.DMA((blocks,)),
-            pltpu.SemaphoreType.DMA((len(w_parts),)),
         ],
         compiler_params=params(16),
         cost_estimate=pl.CostEstimate(
@@ -318,13 +305,8 @@
 def collect_kernel(info_ref, sums_ref, *refs):
     w_refs, toks, (sums_out, w_out, u_out) = refs[0:4], refs[4:6], refs[6:]
     sums_out[...] = sums_ref[...]
-    rows = w_refs[0].shape[0]
-    for i, ref in enumerate(w_refs):
-        w_out[i * rows : (i + 1) * rows, :] = ref[...]
-    core = info_ref[1]
-    for i, ref in enumerate(toks):
-        for z in range(ref.shape[0]):
-            u_out[2 * z + (1 - core if i else core)] = ref[z]
+    lay(w_refs, w_out)
+    place(info_ref, toks, u_out)
 
 
 def collect(info, sums, w_parts, toks):
@@ -345,7 +327,8 @@
 
 
 def row_kernel(*refs):
-    sums, e, (out_ref, part, rows) = refs[0:SIDE], refs[SIDE], refs[-3:]
+    sums, e, extra = refs[0:SIDE], refs[SIDE], refs[SIDE + 1 : -3]
+    out_ref, part, rows = refs[-3:]
     blocks, slots, cols = e.shape
     c = column_factor(sums)
     rows[...] = jnp.zeros_like(rows)
@@ -360,29 +343,36 @@
         return 0
 
     lax.fori_loop(0, blocks, step, 0)
+    at = PER * blocks
+    for ref in extra:
+        end = at + ref.shape[0]
+        if end <= rows.shape[0]:
+            rows[at:end, :] = ref[...]
+        at = end
     low = rows[...].astype(bf16)
     for i in range(out_ref.shape[0]):
         out_ref[i] = low
 
 
-def row_pass(sums, energy, peers, after=()):
+def row_pass(sums, energy, peers, tall, extra):
     blocks, slots, cols = energy.shape
     return pl.pallas_call(
         row_kernel,
-        out_shape=shape((peers, TALL, LANES), bf16),
-        in_specs=[VM] * (SIDE + 1) + [ANY] * len(after),
+        out_shape=shape((peers, tall, LANES), bf16),
+        in_specs=[VM] * (SIDE + 1 + len(extra)),
         out_specs=VM,
-        scratch_shapes=[pltpu.VMEM((slots, LANES), f32), pltpu.VMEM((TALL, LANES), f32)],
+        scratch_shapes=[pltpu.VMEM((slots, LANES), f32), pltpu.VMEM((tall, LANES), f32)],
         compiler_params=params(8),
         name="row_pass",
-    )(*sums, pinned(energy), *after)
+    )(*sums, pinned(energy), *extra)
 
 
 def column_kernel(rows_ref, own_ref, e, out_ref, weight, ratio, acc):
     blocks, slots, cols = e.shape
     acc[...] = jnp.zeros_like(acc)
     own = own_ref[...]
-    ratio[...] = live_of(own) / jnp.where(own > 0.0, added(rows_ref), 1.0)
+    total = added(rows_ref)[0 : own.shape[0]]
+    ratio[...] = live_of(own) / jnp.where(own > 0.0, total, 1.0)
 
     def step(b, _):
         weight[...] = down(vector(ratio, b))
@@ -454,16 +444,12 @@
     )(u, w)
 
 
-def closing_kernel(*refs):
-    u, w, soft_a, soft_b, sums = refs[0], refs[1], refs[2], refs[3], refs[4 : 4 + SIDE]
-    e, ut, out_ref, part, rows, crosses = refs[4 + SIDE :]
+def closing_kernel(u, w, *refs):
+    sums, (e, ut, out_ref, part, rows, crosses) = refs[0:SIDE], refs[SIDE:]
     blocks, slots, cols = e.shape
     c = column_factor(sums)
     cs = c * (inverse_norms(w) * (1.0 / student_temp))
     rows[...] = jnp.zeros_like(rows)
-    half = PER * blocks // 2
-    rows[2 * half : 3 * half, :] = soft_a[...]
-    rows[3 * half : 4 * half, :] = soft_b[...]
 
     def step(b, _):
         ut[b] = jnp.transpose(u[b].astype(f32)).astype(bf16)
@@ -483,34 +469,34 @@
         return 0
 
     lax.fori_loop(0, blocks, step, 0)
-    at = 2 * PER * blocks
+    at = PER * blocks
     for i in range(out_ref.shape[0]):
         rows[at : at + PER, :] = crosses[i // 4, 0:PER, :]
         out_ref[i] = rows[...].astype(bf16)
 
 
-def closing_pass(u, w, soft, sums, energy, peers):
+def closing_pass(u, w, sums, energy, peers):
     blocks, slots, cols = energy.shape
     d = w.shape[0]
     return pl.pallas_call(
         closing_kernel,
         out_shape=(
             pltpu.VMEM((blocks, d, slots), bf16),
-            shape((peers, 2 * TALL, LANES), bf16),
+            shape((peers, TALL, LANES), bf16),
         ),
-        in_specs=[VM] * (SIDE + 5),
+        in_specs=[VM] * (SIDE + 3),
         out_specs=(VM, VM),
         scratch_shapes=[
             pltpu.VMEM((2, slots, LANES), f32),
-            pltpu.VMEM((2 * TALL, LANES), f32),
+            pltpu.VMEM((TALL, LANES), f32),
             pltpu.VMEM((blocks, 8, LANES), f32),
         ],
         compiler_params=params(16),
         name="closing_pass",
-    )(u, w, *soft, *sums, pinned(energy))
-
-
-def grad_kernel(images, info_ref, rows_ref, own_ref, *refs):
+    )(u, w, *sums, pinned(energy))
+
+
+def grad_kernel(images, info_ref, rows_ref, softs_ref, own_ref, *refs):
     sums = refs[0:SIDE]
     (u, ut, w, e, out_ref, loss_ref, soft_w, mass_w, acc, totals, soft_all,
      mass_all) = refs[SIDE:]
@@ -519,10 +505,11 @@
     own = own_ref[...]
     n = PER * blocks
     me = info_ref[0] * 2 + info_ref[1]
-    mine = jnp.log(vector(totals, me, n)) - vector(totals, 0, 2 * n) / vector(totals, me)
+    soft_all[0:n, :] = added(softs_ref)[n : 2 * n]
+    mine = jnp.log(vector(soft_all, me)) - vector(totals, 0, n) / vector(totals, me)
     loss_ref[...] = jnp.where(vector(own_ref, me) > 0.0, mine, 0.0)
     weight = live_of(own) / (jnp.maximum(own, 1.0) * images) * (loss_scale / student_temp)
-    soft_all[0:n, :] = weight[0:n] / totals[n : 2 * n, :]
+    soft_all[0:n, :] = weight[0:n] / soft_all[0:n, :]
     mass_all[0:n, :] = weight[0:n] / totals[0:n, :]
     c = column_factor(sums)
     inv = inverse_norms(w)
@@ -566,25 +553,25 @@
             out_ref[(q // 2) * 8 + 2 * y + q % 2] = acc[at : at + rows, :].astype(bf16)
 
 
-def grad_pass(images, info, rows, own, sums, u, ut, w, energy, peers):
+def grad_pass(images, info, rows, softs, own, sums, u, ut, w, energy, peers):
     blocks, slots, cols = energy.shape
     d = ut.shape[1]
     return pl.pallas_call(
         functools.partial(grad_kernel, float(images)),
         out_shape=(shape((peers, d // peers, cols), bf16), shape((PER, LANES))),
-        in_specs=[SM] + [VM] * (SIDE + 6),
+        in_specs=[SM] + [VM] * (SIDE + 7),
         out_specs=(VM, VM),
         scratch_shapes=[
             pltpu.VMEM((2 * slots, LANES), f32),
             pltpu.VMEM((2 * slots, LANES), f32),
             pltpu.VMEM((d, cols), f32),
-            pltpu.VMEM(rows.shape[1:], f32),
+            pltpu.VMEM((TALL, LANES), f32),
             pltpu.VMEM((TALL, LANES), f32),
             pltpu.VMEM((TALL, LANES), f32),
         ],
         compiler_params=params(16),
         name="grad_pass",
-    )(info, rows, own, *sums, u, ut, w, pinned(energy))
+    )(info, rows, softs, own, *sums, u, ut, w, pinned(energy))
 
 
 def sum_kernel(parts_ref, out_ref):
@@ -639,15 +626,16 @@
     sums, s_w, s_u = collect(info, sums, s_parts, s_toks)
     half = s_u.shape[0] // 2
     soft = []
-    for _ in range(SWEEPS - 1):
-        rows = row_pass(ring(sums, "y"), energy, peers, soft)
-        soft.append(softmax_pass(s_u, s_w, half * len(soft), half))
-        sums = column_pass(exchange(rows, GROUP), own, energy)
+    for i in range(SWEEPS - 1):
+        soft.append(softmax_pass(s_u, s_w, half * i, half))
+        tall = TALL if i < SWEEPS - 2 else TALL + HALF
+        rows = exchange(row_pass(ring(sums, "y"), energy, peers, tall, soft), GROUP)
+        sums = column_pass(rows, own, energy)
     ring_sums = ring(sums, "y")
-    s_ut, rows = closing_pass(s_u, s_w, soft, ring_sums, energy, peers)
-    rows = exchange(rows, GROUP)
+    s_ut, closing = closing_pass(s_u, s_w, ring_sums, energy, peers)
+    closing = exchange(closing, GROUP)
     grad, loss = grad_pass(
-        images, info, rows, own, ring_sums, s_u, s_ut, s_w, energy, lax.axis_size(DP)
+        images, info, closing, rows, own, ring_sums, s_u, s_ut, s_w, energy, lax.axis_size(DP)
     )
     return (loss.reshape(-1), sum_pass(exchange(grad, DP)))
 

time: 181 us -> 179 us (0.989)
  blocking collectives: 70.8 us -> 68.3 us
  Pallas kernels: 55.4 us -> 53 us
  waiting for transfers between devices: 23.5 us -> 25.5 us
    all_to_all x4, blocking collectives: 70.8 us -> 68.3 us  [exchange(): return lax.all_to_all(value, axes, 0, 0, tiled=True)]
    pallas_call x1, Pallas kernels: 9.47 us -> 7.38 us  [energy_pass(): pl.pallas_call(energy_kernel, out_shape=(pltpu.VMEM((blocks, slots, cols)...]
    ppermute x20, waiting for transfers between devices: 18.3 us -> 20.3 us  [shift(): return lax.ppermute(value, axis, [(i, (i + k) % n) for i in range(n)])]
  transfers between devices with their start and end apart: 21 -> 21, of which waited for: 10 -> 10; matrix products, arithmetic and copies ran while one was open for 0% -> 0% of each run, Pallas kernels for 8% -> 7%
where the time goes in v4:
time: 179 us; the launch traced here: 178 us
  blocking collectives  68.3 us (38%)
  Pallas kernels  53 us (30%)
  starting transfers between devices  30.2 us (17%)
  waiting for transfers between devices  25.5 us (14%)
    all_to_all x4, blocking collectives, exchange(): return lax.all_to_all(value, axes, 0, 0, tiled=True)  68.3 us
    ppermute x20, starting transfers between devices, shift(): return lax.ppermute(value, axis, [(i, (i + k) % n) for i in range(n)])  23.3 us
    ppermute x20, waiting for transfers between devices, shift(): return lax.ppermute(value, axis, [(i, (i + k) % n) for i in range(n)])  20.3 us
    pallas_call x1, Pallas kernels, grad_pass(): pl.pallas_call(functools.partial(grad_kernel, float(images)), out_shape=(...  11.3 us
    pallas_call x1, Pallas kernels, closing_pass(): pl.pallas_call(closing_kernel, out_shape=(pltpu.VMEM((blocks, d, slots),...  8.02 us
    pallas_call x1, Pallas kernels, energy_pass(): pl.pallas_call(energy_kernel, out_shape=(pltpu.VMEM((blocks, slots, cols)...  7.38 us
    all_to_all x1, starting transfers between devices, exchange(): return lax.all_to_all(value, axes, 0, 0, tiled=True)  6.96 us
    pallas_call x2, Pallas kernels, column_pass(): pl.pallas_call(column_kernel, out_shape=shape((1, cols)), in_specs=[VM, V...  6.68 us
  transfers between devices with their start and end apart: 21, of which 10 were waited for; matrix products, arithmetic and copies ran while one was open for 0% of the time, Pallas kernels for 7%

profile of v4, /device:TPU:1, one launch (start us, length us, event | category | flops | bytes accessed | tf_op | source)
XLA Modules:
  0.0 178.5 jit_solution(7730025481673775380)
XLA Ops:
  1.3 5.5 %token_rows.1 = (bf16[784,256]{1,0:T(8,128)(2,1)}, bf16[8,16,2048]{2,1,0:T(8,128)(2,1)}, s32[3]{0:T(128)}) custom-call(s32[1]{0:T(128)} %bitcast.me_ref, s32[1]{0:T(128)S(6)} %copy.8.count_ref, s32[384]{0:T(512)} %index_ref.1, bf16[2048,256]{1,0:T(8,128)(2,1)} %teacher_ref.1, bf16[2048,256]{1,0:T(8,128)(2,1)} %student_ref.1, bf16[8,16384]{1,0:T(8,128)(2,1)} %tp_ref.1, ...), custom_call_target="tpu_custom_call" | custom-call | tf_op jit(solution)/shard_map/token_rows/pallas_call | solution.py:121
  6.9 7.0 %all-to-all-start = ((bf16[8,16,2048]{2,1,0:T(8,128)(2,1)}), bf16[8,16,2048]{2,1,0:T(8,128)(2,1)S(1)}, u32[]{:S(2)}, u32[]{:S(2)}) async-start(bf16[8,16,2048]{2,1,0:T(8,128)(2,1)} %get-tuple-element.19), calls=%async_computation | async-start | bytes 1048576 | tf_op jit(solution)/shard_map/all_to_all | solution.py:605
  13.8 2.9 %collective-permute-start.2 = (bf16[784,256]{1,0:T(8,128)(2,1)}, bf16[784,256]{1,0:T(8,128)(2,1)S(1)}, u32[]{:S(2)}, u32[]{:S(2)}) collective-permute-start(bf16[784,256]{1,0:T(8,128)(2,1)} %get-tuple-element.18.refs_0_), channel_id=1, source_target_pairs={{0,64},{32,96},{64,0},{96,32},{1,65},{33,97},{65,1},{97,33},{2,66}... | collective-permute-start | bytes 1204232 | tf_op jit(solution)/shard_map/ppermute | solution.py:601
  16.7 0.9 collective-permute-start.1
  17.6 0.6 collective-permute-start
  18.2 5.2 %all-to-all-done.w_ref = bf16[8,16,2048]{2,1,0:T(8,128)(2,1)S(1)} async-done(((bf16[8,16,2048]{2,1,0:T(8,128)(2,1)}), bf16[8,16,2048]{2,1,0:T(8,128)(2,1)S(1)}, u32[]{:S(2)}, u32[]{:S(2)}) %all-to-all-start) | async-done | bytes 524320 | tf_op jit(solution)/shard_map/all_to_all | solution.py:605
  23.4 3.0 %collective-permute-start.5 = (bf16[64,2048]{1,0:T(8,128)(2,1)S(1)}, bf16[64,2048]{1,0:T(8,128)(2,1)S(1)}, u32[]{:S(2)}, u32[]{:S(2)}) collective-permute-start(bf16[64,2048]{1,0:T(8,128)(2,1)S(1)} %split_rows.2.refs_2_), channel_id=1, source_target_pairs={{0,16},{8,24},{16,0},{24,8},{1,17},{9,25},{17,1},{25,9},{2,18},{10... | collective-permute-start | bytes 786440 | tf_op jit(solution)/shard_map/ppermute | solution.py:601
  26.4 0.8 collective-permute-start.4
  27.1 4.8 %collective-permute-done.2.refs_3_ = bf16[784,256]{1,0:T(8,128)(2,1)S(1)} collective-permute-done((bf16[784,256]{1,0:T(8,128)(2,1)}, bf16[784,256]{1,0:T(8,128)(2,1)S(1)}, u32[]{:S(2)}, u32[]{:S(2)}) %collective-permute-start.2) | collective-permute-done | bytes 401440 | tf_op jit(solution)/shard_map/ppermute | solution.py:601
  31.9 1.3 collective-permute-start.3
  33.2 5.8 %collective-permute-done.1.refs_2_ = bf16[784,256]{1,0:T(8,128)(2,1)S(1)} collective-permute-done((bf16[784,256]{1,0:T(8,128)(2,1)}, bf16[784,256]{1,0:T(8,128)(2,1)S(1)}, u32[]{:S(2)}, u32[]{:S(2)}) %collective-permute-start.1) | collective-permute-done | bytes 401440 | tf_op jit(solution)/shard_map/ppermute | solution.py:601
  39.0 1.7 collective-permute-done.refs_1_
  40.7 0.7 stack.1
  41.4 1.3 collective-permute-start.6
  42.7 0.1 collective-permute-start.10
  42.8 2.4 %collective-permute-start.9 = (bf16[64,2048]{1,0:T(8,128)(2,1)S(1)}, bf16[64,2048]{1,0:T(8,128)(2,1)S(1)}, u32[]{:S(2)}, u32[]{:S(2)}) collective-permute-start(bf16[64,2048]{1,0:T(8,128)(2,1)S(1)} %split_rows.3.refs_6_.refs_0_), channel_id=1, source_target_pairs={{0,16},{8,24},{16,0},{24,8},{1,17},{9,25},{17,1},{25,9},{2,18},{10... | collective-permute-start | bytes 786440 | tf_op jit(solution)/shard_map/ppermute | solution.py:601
  45.2 0.8 collective-permute-start.8
  45.9 0.7 collective-permute-start.7
  46.6 7.4 %energy_pass.1 = (bf16[8,384,2048]{2,1,0:T(8,128)(2,1)S(1)}, f32[32,128]{1,0:T(8,128)S(1)}, f32[1,2048]{1,0:T(1,128)S(1)}) custom-call(s32[3]{0:T(128)S(1)} %copy-done.1, bf16[4,400,256]{2,1,0:T(8,128)(2,1)S(1)} %get-tuple-element.20.refs_0_, bf16[4,400,256]{2,1,0:T(8,128)(2,1)S(1)} %collective-permute-done.6.refs_1_, ...), custom_call_target="tpu_custom_call" | custom-call | flops 3221225472 | bytes 12582912 | tf_op jit(solution)/shard_map/energy_pass/pallas_call | solution.py:280
  54.0 3.2 %collective-permute-done.8.refs_2_ = bf16[64,2048]{1,0:T(8,128)(2,1)S(1)} collective-permute-done((bf16[64,2048]{1,0:T(8,128)(2,1)S(1)}, bf16[64,2048]{1,0:T(8,128)(2,1)S(1)}, u32[]{:S(2)}, u32[]{:S(2)}) %collective-permute-start.8) | collective-permute-done | bytes 262176 | tf_op jit(solution)/shard_map/ppermute | solution.py:601
  57.2 1.0 collective-permute-done.7.refs_1_
  58.2 0.7 collect.1
  59.0 2.4 %collective-permute-start.13 = (f32[1,2048]{1,0:T(1,128)S(1)}, f32[1,2048]{1,0:T(1,128)S(1)}, u32[]{:S(2)}, u32[]{:S(2)}) collective-permute-start(f32[1,2048]{1,0:T(1,128)S(1)} %get-tuple-element.25.refs_0_), channel_id=1, source_target_pairs={{0,16},{8,24},{16,0},{24,8},{1,17},{9,25},{17,1},{25,9},{2,18},{10... | collective-permute-start | bytes 24584 | tf_op jit(solution)/shard_map/ppermute | solution.py:601
  61.3 0.8 collective-permute-start.12
  62.1 0.7 collective-permute-start.11
  62.8 2.8 %softmax_pass.2.refs_5_ = f32[12,128]{1,0:T(8,128)S(1)} custom-call(bf16[8,384,256]{2,1,0:T(8,128)(2,1)S(1)} %get-tuple-element.23.u.refs_4_, bf16[256,2048]{1,0:T(8,128)(2,1)S(1)} %get-tuple-element.24.w.refs_6_), custom_call_target="tpu_custom_call" | custom-call | flops 1610612736 | bytes 393216 | tf_op jit(solution)/shard_map/softmax_pass/pallas_call | solution.py:431
  65.6 0.2 collective-permute-done.11.refs_1_
  65.8 3.1 %row_pass.2 = bf16[32,32,128]{2,1,0:T(8,128)(2,1)S(1)} custom-call(f32[1,2048]{1,0:T(1,128)S(1)} %get-tuple-element.25.refs_0_, f32[1,2048]{1,0:T(1,128)S(1)} %collective-permute-done.11.refs_1_, f32[1,2048]{1,0:T(1,128)S(1)} %collective-permute-done.12.refs_2_, f32[1,2048]{1,0:T(1,128)S(1)} %collective-permute-done.13.refs_3_, ...), custom_call_target="tpu_custom_call" | custom-call | tf_op jit(solution)/shard_map/row_pass/pallas_call | solution.py:359
  68.9 17.8 %all_to_all.25.rows_ref = bf16[32,32,128]{2,1,0:T(8,128)(2,1)S(1)} all-to-all(bf16[32,32,128]{2,1,0:T(8,128)(2,1)S(1)} %row_pass.2), channel_id=1, replica_groups=mesh['z'=4,'y'=4,'c'=2,'x'=4] {'z','c','x'}, dimensions={0} | all-to-all | bytes 524288 | tf_op jit(solution)/shard_map/all_to_all | solution.py:605
  86.7 3.3 %column_pass.2.refs_0_ = f32[1,2048]{1,0:T(1,128)S(1)} custom-call(bf16[32,32,128]{2,1,0:T(8,128)(2,1)S(1)} %all_to_all.25.rows_ref, f32[32,128]{1,0:T(8,128)S(1)} %get-tuple-element.27.own_ref, bf16[8,384,2048]{2,1,0:T(8,128)(2,1)S(1)} %get-tuple-element.26.refs_4_.e.refs_7_), custom_call_target="tpu_custom_call" | custom-call | tf_op jit(solution)/shard_map/column_pass/pallas_call | solution.py:392
  90.1 0.8 collective-permute-start.16
  90.9 1.0 collective-permute-start.15
  91.9 0.5 collective-permute-start.14
  92.4 2.8 %softmax_pass.3.refs_6_ = f32[12,128]{1,0:T(8,128)S(1)} custom-call(bf16[8,384,256]{2,1,0:T(8,128)(2,1)S(1)} %get-tuple-element.23.u.refs_4_, bf16[256,2048]{1,0:T(8,128)(2,1)S(1)} %get-tuple-element.24.w.refs_6_), custom_call_target="tpu_custom_call" | custom-call | flops 1610612736 | bytes 393216 | tf_op jit(solution)/shard_map/softmax_pass/pallas_call | solution.py:431
  95.2 0.4 collective-permute-done.14.refs_1_
  95.6 3.1 %row_pass.3 = bf16[32,48,128]{2,1,0:T(8,128)(2,1)S(1)} custom-call(f32[1,2048]{1,0:T(1,128)S(1)} %column_pass.2.refs_0_, f32[1,2048]{1,0:T(1,128)S(1)} %collective-permute-done.14.refs_1_, f32[1,2048]{1,0:T(1,128)S(1)} %collective-permute-done.15.refs_2_, f32[1,2048]{1,0:T(1,128)S(1)} %collective-permute-done.16.refs_3_, ...), custom_call_target="tpu_custom_call" | custom-call | tf_op jit(solution)/shard_map/row_pass/pallas_call | solution.py:359
  98.7 15.8 %all_to_all.26.rows_ref.softs_ref = bf16[32,48,128]{2,1,0:T(8,128)(2,1)S(1)} all-to-all(bf16[32,48,128]{2,1,0:T(8,128)(2,1)S(1)} %row_pass.3), channel_id=1, replica_groups=mesh['z'=4,'y'=4,'c'=2,'x'=4] {'z','c','x'}, dimensions={0} | all-to-all | bytes 786432 | tf_op jit(solution)/shard_map/all_to_all | solution.py:605
  114.5 3.3 %column_pass.3.refs_0_ = f32[1,2048]{1,0:T(1,128)S(1)} custom-call(bf16[32,48,128]{2,1,0:T(8,128)(2,1)S(1)} %all_to_all.26.rows_ref.softs_ref, f32[32,128]{1,0:T(8,128)S(1)} %get-tuple-element.27.own_ref, bf16[8,384,2048]{2,1,0:T(8,128)(2,1)S(1)} %get-tuple-element.26.refs_4_.e.refs_7_), custom_call_target="tpu_custom_call" | custom-call | tf_op jit(solution)/shard_map/column_pass/pallas_call | solution.py:392
  117.8 1.0 collective-permute-start.19
  118.9 0.9 collective-permute-start.18
  119.8 0.6 collective-permute-start.17
  120.3 1.6 collective-permute-done.19.refs_3_
  121.9 1.6 collective-permute-done.17.refs_1_
  123.5 8.0 %closing_pass.1 = (bf16[8,256,384]{2,1,0:T(8,128)(2,1)S(1)}, bf16[32,32,128]{2,1,0:T(8,128)(2,1)S(1)}) custom-call(bf16[8,384,256]{2,1,0:T(8,128)(2,1)S(1)} %get-tuple-element.23.u.refs_4_, bf16[256,2048]{1,0:T(8,128)(2,1)S(1)} %get-tuple-element.24.w.refs_6_, f32[1,2048]{1,0:T(1,128)S(1)} %column_pass.3.refs_0_, ...), custom_call_target="tpu_custom_call" | custom-call | tf_op jit(solution)/shard_map/closing_pass/pallas_call | solution.py:481
  131.5 14.6 %all_to_all.27.rows_ref = bf16[32,32,128]{2,1,0:T(8,128)(2,1)S(1)} all-to-all(bf16[32,32,128]{2,1,0:T(8,128)(2,1)S(1)} %get-tuple-element.28), channel_id=1, replica_groups=mesh['z'=4,'y'=4,'c'=2,'x'=4] {'z','c','x'}, dimensions={0} | all-to-all | bytes 524288 | tf_op jit(solution)/shard_map/all_to_all | solution.py:605
  146.1 11.3 %grad_pass.1 = (bf16[32,8,2048]{2,1,0:T(8,128)(2,1)S(1)}, f32[3,128]{1,0:T(4,128)}) custom-call(s32[3]{0:T(128)S(1)} %copy-done.1, bf16[32,32,128]{2,1,0:T(8,128)(2,1)S(1)} %all_to_all.27.rows_ref, bf16[32,48,128]{2,1,0:T(8,128)(2,1)S(1)} %all_to_all.26.rows_ref.softs_ref, f32[32,128]{1,0:T(8,128)S(1)} %get-tuple-element.27.own_ref, ...), custom_call_target="tpu_custom_call" | custom-call | tf_op jit(solution)/shard_map/grad_pass/pallas_call | solution.py:559
  157.4 20.1 %all_to_all.28.parts_ref = bf16[32,8,2048]{2,1,0:T(8,128)(2,1)S(1)} all-to-all(bf16[32,8,2048]{2,1,0:T(8,128)(2,1)S(1)} %get-tuple-element.31), channel_id=1, replica_groups=mesh['z'=4,'y'=4,'c'=2,'x'=4] {'z','y','c'}, dimensions={0} | all-to-all | bytes 2097152 | tf_op jit(solution)/shard_map/all_to_all | solution.py:605
  177.5 0.9 sum_pass.1
  (17 shorter events, 0.1 us)
Async XLA Ops:
  6.8 33.9 %copy-start = (bf16[784,256]{1,0:T(8,128)(2,1)S(1)}, bf16[784,256]{1,0:T(8,128)(2,1)}, u32[]{:S(2)}) copy-start(bf16[784,256]{1,0:T(8,128)(2,1)} %get-tuple-element.18.refs_0_) | copy-start | bytes 1204228
  6.9 33.9 %copy-start.1 = (s32[3]{0:T(128)S(1)}, s32[3]{0:T(128)}, u32[]{:S(2)}) copy-start(s32[3]{0:T(128)} %get-tuple-element.17.info_ref) | copy-start | bytes 40
  6.9 16.5 %all-to-all-start = ((bf16[8,16,2048]{2,1,0:T(8,128)(2,1)}), bf16[8,16,2048]{2,1,0:T(8,128)(2,1)S(1)}, u32[]{:S(2)}, u32[]{:S(2)}) async-start(bf16[8,16,2048]{2,1,0:T(8,128)(2,1)} %get-tuple-element.19), calls=%async_computation | async-start | bytes 1048576 | tf_op jit(solution)/shard_map/all_to_all | solution.py:605
  13.8 18.1 %collective-permute-start.2 = (bf16[784,256]{1,0:T(8,128)(2,1)}, bf16[784,256]{1,0:T(8,128)(2,1)S(1)}, u32[]{:S(2)}, u32[]{:S(2)}) collective-permute-start(bf16[784,256]{1,0:T(8,128)(2,1)} %get-tuple-element.18.refs_0_), channel_id=1, source_target_pairs={{0,64},{32,96},{64,0},{96,32},{1,65},{33,97},{65,1},{97,33},{2,66}... | collective-permute-start | bytes 1204232 | tf_op jit(solution)/shard_map/ppermute | solution.py:601
  16.7 22.3 %collective-permute-start.1 = (bf16[784,256]{1,0:T(8,128)(2,1)}, bf16[784,256]{1,0:T(8,128)(2,1)S(1)}, u32[]{:S(2)}, u32[]{:S(2)}) collective-permute-start(bf16[784,256]{1,0:T(8,128)(2,1)} %get-tuple-element.18.refs_0_), channel_id=1, source_target_pairs={{0,96},{32,0},{64,32},{96,64},{1,97},{33,1},{65,33},{97,65},{2,98}... | collective-permute-start | bytes 1204232 | tf_op jit(solution)/shard_map/ppermute | solution.py:601
  17.6 23.1 %collective-permute-start = (bf16[784,256]{1,0:T(8,128)(2,1)}, bf16[784,256]{1,0:T(8,128)(2,1)S(1)}, u32[]{:S(2)}, u32[]{:S(2)}) collective-permute-start(bf16[784,256]{1,0:T(8,128)(2,1)} %get-tuple-element.18.refs_0_), channel_id=1, source_target_pairs={{0,32},{32,64},{64,96},{96,0},{1,33},{33,65},{65,97},{97,1},{2,34}... | collective-permute-start | bytes 1204232 | tf_op jit(solution)/shard_map/ppermute | solution.py:601
  23.4 17.3 %collective-permute-start.5 = (bf16[64,2048]{1,0:T(8,128)(2,1)S(1)}, bf16[64,2048]{1,0:T(8,128)(2,1)S(1)}, u32[]{:S(2)}, u32[]{:S(2)}) collective-permute-start(bf16[64,2048]{1,0:T(8,128)(2,1)S(1)} %split_rows.2.refs_2_), channel_id=1, source_target_pairs={{0,16},{8,24},{16,0},{24,8},{1,17},{9,25},{17,1},{25,9},{2,18},{10... | collective-permute-start | bytes 786440 | tf_op jit(solution)/shard_map/ppermute | solution.py:601
  26.4 14.4 %collective-permute-start.4 = (bf16[64,2048]{1,0:T(8,128)(2,1)S(1)}, bf16[64,2048]{1,0:T(8,128)(2,1)S(1)}, u32[]{:S(2)}, u32[]{:S(2)}) collective-permute-start(bf16[64,2048]{1,0:T(8,128)(2,1)S(1)} %split_rows.2.refs_2_), channel_id=1, source_target_pairs={{0,24},{8,0},{16,8},{24,16},{1,25},{9,1},{17,9},{25,17},{2,26},{10... | collective-permute-start | bytes 786440 | tf_op jit(solution)/shard_map/ppermute | solution.py:601
  31.9 8.8 %collective-permute-start.3 = (bf16[64,2048]{1,0:T(8,128)(2,1)S(1)}, bf16[64,2048]{1,0:T(8,128)(2,1)S(1)}, u32[]{:S(2)}, u32[]{:S(2)}) collective-permute-start(bf16[64,2048]{1,0:T(8,128)(2,1)S(1)} %split_rows.2.refs_2_), channel_id=1, source_target_pairs={{0,8},{8,16},{16,24},{24,0},{1,9},{9,17},{17,25},{25,1},{2,10},{10... | collective-permute-start | bytes 786440 | tf_op jit(solution)/shard_map/ppermute | solution.py:601
  41.4 5.2 %collective-permute-start.6 = (bf16[4,400,256]{2,1,0:T(8,128)(2,1)S(1)}, bf16[4,400,256]{2,1,0:T(8,128)(2,1)S(1)}, u32[]{:S(2)}, u32[]{:S(2)}) collective-permute-start(bf16[4,400,256]{2,1,0:T(8,128)(2,1)S(1)} %get-tuple-element.20.refs_0_), channel_id=1, source_target_pairs={{0,4},{4,0},{1,5},{5,1},{2,6},{6,2},{3,7},{7,3},{8,12},{12,8},{9,1... | collective-permute-start | bytes 2457608 | tf_op jit(solution)/shard_map/ppermute | solution.py:601
  42.7 15.5 %collective-permute-start.10 = (bf16[4,384,256]{2,1,0:T(8,128)(2,1)S(1)}, bf16[4,384,256]{2,1,0:T(8,128)(2,1)S(1)}, u32[]{:S(2)}, u32[]{:S(2)}) collective-permute-start(bf16[4,384,256]{2,1,0:T(8,128)(2,1)S(1)} %get-tuple-element.22.refs_4_), channel_id=1, source_target_pairs={{0,4},{4,0},{1,5},{5,1},{2,6},{6,2},{3,7},{7,3},{8,12},{12,8},{9,1... | collective-permute-start | bytes 2359304 | tf_op jit(solution)/shard_map/ppermute | solution.py:601
  42.8 11.2 %collective-permute-start.9 = (bf16[64,2048]{1,0:T(8,128)(2,1)S(1)}, bf16[64,2048]{1,0:T(8,128)(2,1)S(1)}, u32[]{:S(2)}, u32[]{:S(2)}) collective-permute-start(bf16[64,2048]{1,0:T(8,128)(2,1)S(1)} %split_rows.3.refs_6_.refs_0_), channel_id=1, source_target_pairs={{0,16},{8,24},{16,0},{24,8},{1,17},{9,25},{17,1},{25,9},{2,18},{10... | collective-permute-start | bytes 786440 | tf_op jit(solution)/shard_map/ppermute | solution.py:601
  45.2 12.1 %collective-permute-start.8 = (bf16[64,2048]{1,0:T(8,128)(2,1)S(1)}, bf16[64,2048]{1,0:T(8,128)(2,1)S(1)}, u32[]{:S(2)}, u32[]{:S(2)}) collective-permute-start(bf16[64,2048]{1,0:T(8,128)(2,1)S(1)} %split_rows.3.refs_6_.refs_0_), channel_id=1, source_target_pairs={{0,24},{8,0},{16,8},{24,16},{1,25},{9,1},{17,9},{25,17},{2,26},{10... | collective-permute-start | bytes 786440 | tf_op jit(solution)/shard_map/ppermute | solution.py:601
  45.9 12.3 %collective-permute-start.7 = (bf16[64,2048]{1,0:T(8,128)(2,1)S(1)}, bf16[64,2048]{1,0:T(8,128)(2,1)S(1)}, u32[]{:S(2)}, u32[]{:S(2)}) collective-permute-start(bf16[64,2048]{1,0:T(8,128)(2,1)S(1)} %split_rows.3.refs_6_.refs_0_), channel_id=1, source_target_pairs={{0,8},{8,16},{16,24},{24,0},{1,9},{9,17},{17,25},{25,1},{2,10},{10... | collective-permute-start | bytes 786440 | tf_op jit(solution)/shard_map/ppermute | solution.py:601
  59.0 6.6 %collective-permute-start.13 = (f32[1,2048]{1,0:T(1,128)S(1)}, f32[1,2048]{1,0:T(1,128)S(1)}, u32[]{:S(2)}, u32[]{:S(2)}) collective-permute-start(f32[1,2048]{1,0:T(1,128)S(1)} %get-tuple-element.25.refs_0_), channel_id=1, source_target_pairs={{0,16},{8,24},{16,0},{24,8},{1,17},{9,25},{17,1},{25,9},{2,18},{10... | collective-permute-start | bytes 24584 | tf_op jit(solution)/shard_map/ppermute | solution.py:601
  61.3 4.3 %collective-permute-start.12 = (f32[1,2048]{1,0:T(1,128)S(1)}, f32[1,2048]{1,0:T(1,128)S(1)}, u32[]{:S(2)}, u32[]{:S(2)}) collective-permute-start(f32[1,2048]{1,0:T(1,128)S(1)} %get-tuple-element.25.refs_0_), channel_id=1, source_target_pairs={{0,24},{8,0},{16,8},{24,16},{1,25},{9,1},{17,9},{25,17},{2,26},{10... | collective-permute-start | bytes 24584 | tf_op jit(solution)/shard_map/ppermute | solution.py:601
  62.1 3.7 %collective-permute-start.11 = (f32[1,2048]{1,0:T(1,128)S(1)}, f32[1,2048]{1,0:T(1,128)S(1)}, u32[]{:S(2)}, u32[]{:S(2)}) collective-permute-start(f32[1,2048]{1,0:T(1,128)S(1)} %get-tuple-element.25.refs_0_), channel_id=1, source_target_pairs={{0,8},{8,16},{16,24},{24,0},{1,9},{9,17},{17,25},{25,1},{2,10},{10... | collective-permute-start | bytes 24584 | tf_op jit(solution)/shard_map/ppermute | solution.py:601
  90.1 5.1 %collective-permute-start.16 = (f32[1,2048]{1,0:T(1,128)S(1)}, f32[1,2048]{1,0:T(1,128)S(1)}, u32[]{:S(2)}, u32[]{:S(2)}) collective-permute-start(f32[1,2048]{1,0:T(1,128)S(1)} %column_pass.2.refs_0_), channel_id=1, source_target_pairs={{0,16},{8,24},{16,0},{24,8},{1,17},{9,25},{17,1},{25,9},{2,18},{10... | collective-permute-start | bytes 24584 | tf_op jit(solution)/shard_map/ppermute | solution.py:601
  90.9 4.3 %collective-permute-start.15 = (f32[1,2048]{1,0:T(1,128)S(1)}, f32[1,2048]{1,0:T(1,128)S(1)}, u32[]{:S(2)}, u32[]{:S(2)}) collective-permute-start(f32[1,2048]{1,0:T(1,128)S(1)} %column_pass.2.refs_0_), channel_id=1, source_target_pairs={{0,24},{8,0},{16,8},{24,16},{1,25},{9,1},{17,9},{25,17},{2,26},{10... | collective-permute-start | bytes 24584 | tf_op jit(solution)/shard_map/ppermute | solution.py:601
  91.9 3.7 %collective-permute-start.14 = (f32[1,2048]{1,0:T(1,128)S(1)}, f32[1,2048]{1,0:T(1,128)S(1)}, u32[]{:S(2)}, u32[]{:S(2)}) collective-permute-start(f32[1,2048]{1,0:T(1,128)S(1)} %column_pass.2.refs_0_), channel_id=1, source_target_pairs={{0,8},{8,16},{16,24},{24,0},{1,9},{9,17},{17,25},{25,1},{2,10},{10... | collective-permute-start | bytes 24584 | tf_op jit(solution)/shard_map/ppermute | solution.py:601
  117.8 4.1 %collective-permute-start.19 = (f32[1,2048]{1,0:T(1,128)S(1)}, f32[1,2048]{1,0:T(1,128)S(1)}, u32[]{:S(2)}, u32[]{:S(2)}) collective-permute-start(f32[1,2048]{1,0:T(1,128)S(1)} %column_pass.3.refs_0_), channel_id=1, source_target_pairs={{0,16},{8,24},{16,0},{24,8},{1,17},{9,25},{17,1},{25,9},{2,18},{10... | collective-permute-start | bytes 24584 | tf_op jit(solution)/shard_map/ppermute | solution.py:601
  118.9 3.1 %collective-permute-start.18 = (f32[1,2048]{1,0:T(1,128)S(1)}, f32[1,2048]{1,0:T(1,128)S(1)}, u32[]{:S(2)}, u32[]{:S(2)}) collective-permute-start(f32[1,2048]{1,0:T(1,128)S(1)} %column_pass.3.refs_0_), channel_id=1, source_target_pairs={{0,24},{8,0},{16,8},{24,16},{1,25},{9,1},{17,9},{25,17},{2,26},{10... | collective-permute-start | bytes 24584 | tf_op jit(solution)/shard_map/ppermute | solution.py:601
  119.8 3.7 %collective-permute-start.17 = (f32[1,2048]{1,0:T(1,128)S(1)}, f32[1,2048]{1,0:T(1,128)S(1)}, u32[]{:S(2)}, u32[]{:S(2)}) collective-permute-start(f32[1,2048]{1,0:T(1,128)S(1)} %column_pass.3.refs_0_), channel_id=1, source_target_pairs={{0,8},{8,16},{16,24},{24,0},{1,9},{9,17},{17,25},{25,1},{2,10},{10... | collective-permute-start | bytes 24584 | tf_op jit(solution)/shard_map/ppermute | solution.py:601

commit v5 on v4

--- a/solution.py
+++ b/solution.py
@@ -56,17 +56,13 @@
     return lax.dot_general(a, b, (((0,), (0,)), ((), ())), preferred_element_type=f32)
 
 
-def tokens_kernel(me_ref, count_ref, index_ref, teacher_ref, student_ref, tp_ref, sp_ref,
-                  tok_out, w_out, info_out, feats, protos, sems, p_sems):
-    proto_copies = [
-        pltpu.make_async_copy(ref, protos.at[i], p_sems.at[i])
-        for i, ref in enumerate((tp_ref, sp_ref))
-    ]
+def tokens_kernel(me_ref, count_ref, index_ref, teacher_ref, student_ref, *refs):
+    tok_out, info_out, feats, sems = refs[-4:]
     copies = [
         pltpu.make_async_copy(ref, feats.at[i], sems.at[i])
         for i, ref in enumerate((teacher_ref, student_ref))
     ]
-    for c in proto_copies + copies:
+    for c in copies:
         c.start()
     me = me_ref[0]
     y = (me >> 1) & 3
@@ -99,7 +95,37 @@
     order = jnp.where(
         lax.broadcasted_iota(jnp.int32, (d, d), 0) == origin, 1.0, 0.0
     ).astype(bf16)
-    for c in proto_copies:
+    for i, at in enumerate((0, slots + EXTRA)):
+        copies[i].wait()
+        rows = nn(pick, feats[i])
+        unit = rows * lax.rsqrt(jnp.sum(rows * rows, axis=1, keepdims=True) + 1e-06)
+        tok_out[at : at + slots, :] = nn(unit.astype(bf16), order).astype(bf16)
+
+
+def tokens(me, count, index, teacher_feat, student_feat, after=()):
+    slots, (source, d) = index.shape[0], teacher_feat.shape
+    return pl.pallas_call(
+        tokens_kernel,
+        out_shape=(shape((2 * slots + EXTRA, d), bf16), shape((3,), jnp.int32)),
+        in_specs=[SM, SM, VM, ANY, ANY] + [ANY] * len(after),
+        out_specs=(VM, SM),
+        scratch_shapes=[
+            pltpu.VMEM((2, source, d), bf16),
+            pltpu.SemaphoreType.DMA((2,)),
+        ],
+        compiler_params=params(56),
+        name="token_rows",
+    )(me, count, index, teacher_feat, student_feat, *after)
+
+
+def weave_kernel(tp_ref, sp_ref, w_out, protos, sems):
+    copies = [
+        pltpu.make_async_copy(ref, protos.at[i], sems.at[i])
+        for i, ref in enumerate((tp_ref, sp_ref))
+    ]
+    for c in copies:
+        c.start()
+    for c in copies:
         c.wait()
     parts, _, width = w_out.shape
     for q in range(parts):
@@ -107,35 +133,23 @@
         w_out[q] = jnp.concatenate(
             [protos[0, :, lanes].astype(f32), protos[1, :, lanes].astype(f32)], axis=0
         ).astype(bf16)
-    for i, at in enumerate((0, slots + EXTRA)):
-        copies[i].wait()
-        rows = nn(pick, feats[i])
-        unit = rows * lax.rsqrt(jnp.sum(rows * rows, axis=1, keepdims=True) + 1e-06)
-        tok_out[at : at + slots, :] = nn(unit.astype(bf16), order).astype(bf16)
-
-
-def tokens(me, count, index, teacher_feat, student_feat, teacher_proto, student_proto):
-    slots, (source, d) = index.shape[0], teacher_feat.shape
+
+
+def weave(teacher_proto, student_proto):
     rows, cols = teacher_proto.shape
     parts = 8
     return pl.pallas_call(
-        tokens_kernel,
-        out_shape=(
-            shape((2 * slots + EXTRA, d), bf16),
-            shape((parts, 2 * rows, cols // parts), bf16),
-            shape((3,), jnp.int32),
-        ),
-        in_specs=[SM, SM, VM, ANY, ANY, ANY, ANY],
-        out_specs=(VM, VM, SM),
+        weave_kernel,
+        out_shape=shape((parts, 2 * rows, cols // parts), bf16),
+        in_specs=[ANY, ANY],
+        out_specs=VM,
         scratch_shapes=[
-            pltpu.VMEM((2, source, d), bf16),
             pltpu.VMEM((2, rows, cols), bf16),
             pltpu.SemaphoreType.DMA((2,)),
-            pltpu.SemaphoreType.DMA((2,)),
         ],
         compiler_params=params(56),
-        name="token_rows",
-    )(me, count, index, teacher_feat, student_feat, teacher_proto, student_proto)
+        name="weave",
+    )(teacher_proto, student_proto)
 
 
 def stack_kernel(info_ref, *refs):
@@ -614,9 +628,8 @@
     images = lax.axis_size(DP) * (teacher_feat.shape[0] // PATCH)
     peers = lax.axis_size(GROUP)
     me = lax.axis_index(DP).reshape(1)
-    tok, w, info = tokens(
-        me, mask_count, mask_index, teacher_feat, student_feat, teacher_proto, student_proto
-    )
+    w = weave(teacher_proto, student_proto)
+    tok, info = tokens(me, mask_count, mask_index, teacher_feat, student_feat)
     w = exchange(w, ("z", "c"))
     t_parts = ring(split(0, w), "y")
     t_mine, s_mine = stack(info, ring(tok, "z"), slots, t_parts[1:])

time: 179 us -> 177 us (0.989)
  waiting for transfers between devices: 25.5 us -> 20.3 us
    all_to_all x1, waiting for transfers between devices: 5.17 us -> 0.01 us  [exchange(): return lax.all_to_all(value, axes, 0, 0, tiled=True)]
    pallas_call x0 -> x1, Pallas kernels: none -> 1.87 us  [weave(): pl.pallas_call(weave_kernel, out_shape=shape((parts, 2 * rows, cols // pa...]
  transfers between devices with their start and end apart: 21 -> 21, of which waited for: 10 -> 9; matrix products, arithmetic and copies ran while one was open for 0% -> 0% of each run, Pallas kernels for 7% -> 10%
where the time goes in v5:
time: 177 us; the launch traced here: 176 us
  blocking collectives  68.3 us (39%)
  Pallas kernels  54.5 us (31%)
  starting transfers between devices  30.1 us (17%)
  waiting for transfers between devices  20.3 us (11%)
    all_to_all x4, blocking collectives, exchange(): return lax.all_to_all(value, axes, 0, 0, tiled=True)  68.3 us
    ppermute x20, starting transfers between devices, shift(): return lax.ppermute(value, axis, [(i, (i + k) % n) for i in range(n)])  23.3 us
    ppermute x20, waiting for transfers between devices, shift(): return lax.ppermute(value, axis, [(i, (i + k) % n) for i in range(n)])  20.3 us
    pallas_call x1, Pallas kernels, grad_pass(): pl.pallas_call(functools.partial(grad_kernel, float(images)), out_shape=(...  11.3 us
    pallas_call x1, Pallas kernels, closing_pass(): pl.pallas_call(closing_kernel, out_shape=(pltpu.VMEM((blocks, d, slots),...  8.02 us
    pallas_call x1, Pallas kernels, energy_pass(): pl.pallas_call(energy_kernel, out_shape=(pltpu.VMEM((blocks, slots, cols)...  7.38 us
    all_to_all x1, starting transfers between devices, exchange(): return lax.all_to_all(value, axes, 0, 0, tiled=True)  6.83 us
    pallas_call x2, Pallas kernels, column_pass(): pl.pallas_call(column_kernel, out_shape=shape((1, cols)), in_specs=[VM, V...  6.68 us
  transfers between devices with their start and end apart: 21, of which 9 were waited for; matrix products, arithmetic and copies ran while one was open for 0% of the time, Pallas kernels for 10%

profile of v5, /device:TPU:1, one launch (start us, length us, event | category | flops | bytes accessed | tf_op | source)
XLA Modules:
  0.0 176.4 jit_solution(15122154703070934802)
XLA Ops:
  0.6 1.9 %weave.1 = bf16[8,16,2048]{2,1,0:T(8,128)(2,1)} custom-call(bf16[8,16384]{1,0:T(8,128)(2,1)} %tp_ref.1, bf16[8,16384]{1,0:T(8,128)(2,1)} %sp_ref.1), custom_call_target="tpu_custom_call" | custom-call | tf_op jit(solution)/shard_map/weave/pallas_call | solution.py:141
  2.5 6.8 %all-to-all-start = ((bf16[8,16,2048]{2,1,0:T(8,128)(2,1)}), bf16[8,16,2048]{2,1,0:T(8,128)(2,1)S(1)}, u32[]{:S(2)}, u32[]{:S(2)}) async-start(bf16[8,16,2048]{2,1,0:T(8,128)(2,1)} %weave.1), calls=%async_computation | async-start | bytes 1048576 | tf_op jit(solution)/shard_map/all_to_all | solution.py:619
  10.0 5.2 %token_rows.1 = (bf16[784,256]{1,0:T(8,128)(2,1)}, s32[3]{0:T(128)}) custom-call(s32[1]{0:T(128)} %bitcast.me_ref, s32[1]{0:T(128)S(6)} %copy.8.count_ref, s32[384]{0:T(512)} %index_ref.1, bf16[2048,256]{1,0:T(8,128)(2,1)} %teacher_ref.1, bf16[2048,256]{1,0:T(8,128)(2,1)} %student_ref.1), custom_call_target="tpu_custom_call" | custom-call | tf_op jit(solution)/shard_map/token_rows/pallas_call | solution.py:107
  15.2 3.0 %collective-permute-start.2 = (bf16[784,256]{1,0:T(8,128)(2,1)}, bf16[784,256]{1,0:T(8,128)(2,1)S(1)}, u32[]{:S(2)}, u32[]{:S(2)}) collective-permute-start(bf16[784,256]{1,0:T(8,128)(2,1)} %get-tuple-element.17.refs_0_), channel_id=1, source_target_pairs={{0,64},{32,96},{64,0},{96,32},{1,65},{33,97},{65,1},{97,33},{2,66}... | collective-permute-start | bytes 1204232 | tf_op jit(solution)/shard_map/ppermute | solution.py:615
  18.2 0.9 collective-permute-start.1
  19.0 0.6 collective-permute-start
  19.7 3.0 %collective-permute-start.5 = (bf16[64,2048]{1,0:T(8,128)(2,1)S(1)}, bf16[64,2048]{1,0:T(8,128)(2,1)S(1)}, u32[]{:S(2)}, u32[]{:S(2)}) collective-permute-start(bf16[64,2048]{1,0:T(8,128)(2,1)S(1)} %split_rows.2.refs_2_), channel_id=1, source_target_pairs={{0,16},{8,24},{16,0},{24,8},{1,17},{9,25},{17,1},{25,9},{2,18},{10... | collective-permute-start | bytes 786440 | tf_op jit(solution)/shard_map/ppermute | solution.py:615
  22.6 0.8 collective-permute-start.4
  23.4 4.5 %collective-permute-done.2.refs_3_ = bf16[784,256]{1,0:T(8,128)(2,1)S(1)} collective-permute-done((bf16[784,256]{1,0:T(8,128)(2,1)}, bf16[784,256]{1,0:T(8,128)(2,1)S(1)}, u32[]{:S(2)}, u32[]{:S(2)}) %collective-permute-start.2) | collective-permute-done | bytes 401440 | tf_op jit(solution)/shard_map/ppermute | solution.py:615
  27.9 1.3 collective-permute-start.3
  29.2 7.1 %collective-permute-done.1.refs_2_ = bf16[784,256]{1,0:T(8,128)(2,1)S(1)} collective-permute-done((bf16[784,256]{1,0:T(8,128)(2,1)}, bf16[784,256]{1,0:T(8,128)(2,1)S(1)}, u32[]{:S(2)}, u32[]{:S(2)}) %collective-permute-start.1) | collective-permute-done | bytes 401440 | tf_op jit(solution)/shard_map/ppermute | solution.py:615
  36.3 0.4 collective-permute-done.refs_1_
  36.8 1.0 copy-done
  37.8 0.6 copy-done.1
  38.4 0.6 stack.1
  39.1 1.2 collective-permute-start.6
  40.4 2.6 %collective-permute-start.9 = (bf16[64,2048]{1,0:T(8,128)(2,1)S(1)}, bf16[64,2048]{1,0:T(8,128)(2,1)S(1)}, u32[]{:S(2)}, u32[]{:S(2)}) collective-permute-start(bf16[64,2048]{1,0:T(8,128)(2,1)S(1)} %split_rows.3.refs_6_.refs_0_), channel_id=1, source_target_pairs={{0,16},{8,24},{16,0},{24,8},{1,17},{9,25},{17,1},{25,9},{2,18},{10... | collective-permute-start | bytes 786440 | tf_op jit(solution)/shard_map/ppermute | solution.py:615
  43.0 0.8 collective-permute-start.8
  43.8 0.7 collective-permute-start.7
  44.5 7.4 %energy_pass.1 = (bf16[8,384,2048]{2,1,0:T(8,128)(2,1)S(1)}, f32[32,128]{1,0:T(8,128)S(1)}, f32[1,2048]{1,0:T(1,128)S(1)}) custom-call(s32[3]{0:T(128)S(1)} %copy-done.2, bf16[4,400,256]{2,1,0:T(8,128)(2,1)S(1)} %get-tuple-element.18.refs_0_, bf16[4,400,256]{2,1,0:T(8,128)(2,1)S(1)} %collective-permute-done.6.refs_1_, ...), custom_call_target="tpu_custom_call" | custom-call | flops 3221225472 | bytes 12582912 | tf_op jit(solution)/shard_map/energy_pass/pallas_call | solution.py:294
  51.9 3.2 %collective-permute-done.8.refs_2_ = bf16[64,2048]{1,0:T(8,128)(2,1)S(1)} collective-permute-done((bf16[64,2048]{1,0:T(8,128)(2,1)S(1)}, bf16[64,2048]{1,0:T(8,128)(2,1)S(1)}, u32[]{:S(2)}, u32[]{:S(2)}) %collective-permute-start.8) | collective-permute-done | bytes 262176 | tf_op jit(solution)/shard_map/ppermute | solution.py:615
  55.1 0.8 collective-permute-done.7.refs_1_
  55.9 0.7 collect.1
  56.6 2.6 %collective-permute-start.13 = (f32[1,2048]{1,0:T(1,128)S(1)}, f32[1,2048]{1,0:T(1,128)S(1)}, u32[]{:S(2)}, u32[]{:S(2)}) collective-permute-start(f32[1,2048]{1,0:T(1,128)S(1)} %get-tuple-element.23.refs_0_), channel_id=1, source_target_pairs={{0,16},{8,24},{16,0},{24,8},{1,17},{9,25},{17,1},{25,9},{2,18},{10... | collective-permute-start | bytes 24584 | tf_op jit(solution)/shard_map/ppermute | solution.py:615
  59.2 0.8 collective-permute-start.12
  60.0 0.7 collective-permute-start.11
  60.7 2.8 %softmax_pass.2.refs_5_ = f32[12,128]{1,0:T(8,128)S(1)} custom-call(bf16[8,384,256]{2,1,0:T(8,128)(2,1)S(1)} %get-tuple-element.21.u.refs_4_, bf16[256,2048]{1,0:T(8,128)(2,1)S(1)} %get-tuple-element.22.w.refs_6_), custom_call_target="tpu_custom_call" | custom-call | flops 1610612736 | bytes 393216 | tf_op jit(solution)/shard_map/softmax_pass/pallas_call | solution.py:445
  63.5 0.2 collective-permute-done.11.refs_1_
  63.7 3.1 %row_pass.2 = bf16[32,32,128]{2,1,0:T(8,128)(2,1)S(1)} custom-call(f32[1,2048]{1,0:T(1,128)S(1)} %get-tuple-element.23.refs_0_, f32[1,2048]{1,0:T(1,128)S(1)} %collective-permute-done.11.refs_1_, f32[1,2048]{1,0:T(1,128)S(1)} %collective-permute-done.12.refs_2_, f32[1,2048]{1,0:T(1,128)S(1)} %collective-permute-done.13.refs_3_, ...), custom_call_target="tpu_custom_call" | custom-call | tf_op jit(solution)/shard_map/row_pass/pallas_call | solution.py:373
  66.8 17.9 %all_to_all.25.rows_ref = bf16[32,32,128]{2,1,0:T(8,128)(2,1)S(1)} all-to-all(bf16[32,32,128]{2,1,0:T(8,128)(2,1)S(1)} %row_pass.2), channel_id=1, replica_groups=mesh['z'=4,'y'=4,'c'=2,'x'=4] {'z','c','x'}, dimensions={0} | all-to-all | bytes 524288 | tf_op jit(solution)/shard_map/all_to_all | solution.py:619
  84.6 3.3 %column_pass.2.refs_0_ = f32[1,2048]{1,0:T(1,128)S(1)} custom-call(bf16[32,32,128]{2,1,0:T(8,128)(2,1)S(1)} %all_to_all.25.rows_ref, f32[32,128]{1,0:T(8,128)S(1)} %get-tuple-element.25.own_ref, bf16[8,384,2048]{2,1,0:T(8,128)(2,1)S(1)} %get-tuple-element.24.refs_4_.e.refs_7_), custom_call_target="tpu_custom_call" | custom-call | tf_op jit(solution)/shard_map/column_pass/pallas_call | solution.py:406
  88.0 0.1 collective-permute-start.16
  88.1 1.7 collective-permute-start.15
  89.8 2.8 %softmax_pass.3.refs_6_ = f32[12,128]{1,0:T(8,128)S(1)} custom-call(bf16[8,384,256]{2,1,0:T(8,128)(2,1)S(1)} %get-tuple-element.21.u.refs_4_, bf16[256,2048]{1,0:T(8,128)(2,1)S(1)} %get-tuple-element.22.w.refs_6_), custom_call_target="tpu_custom_call" | custom-call | flops 1610612736 | bytes 393216 | tf_op jit(solution)/shard_map/softmax_pass/pallas_call | solution.py:445
  92.6 0.9 collective-permute-done.14.refs_1_
  93.5 3.1 %row_pass.3 = bf16[32,48,128]{2,1,0:T(8,128)(2,1)S(1)} custom-call(f32[1,2048]{1,0:T(1,128)S(1)} %column_pass.2.refs_0_, f32[1,2048]{1,0:T(1,128)S(1)} %collective-permute-done.14.refs_1_, f32[1,2048]{1,0:T(1,128)S(1)} %collective-permute-done.15.refs_2_, f32[1,2048]{1,0:T(1,128)S(1)} %collective-permute-done.16.refs_3_, ...), custom_call_target="tpu_custom_call" | custom-call | tf_op jit(solution)/shard_map/row_pass/pallas_call | solution.py:373
  96.6 15.8 %all_to_all.26.rows_ref.softs_ref = bf16[32,48,128]{2,1,0:T(8,128)(2,1)S(1)} all-to-all(bf16[32,48,128]{2,1,0:T(8,128)(2,1)S(1)} %row_pass.3), channel_id=1, replica_groups=mesh['z'=4,'y'=4,'c'=2,'x'=4] {'z','c','x'}, dimensions={0} | all-to-all | bytes 786432 | tf_op jit(solution)/shard_map/all_to_all | solution.py:619
  112.4 3.3 %column_pass.3.refs_0_ = f32[1,2048]{1,0:T(1,128)S(1)} custom-call(bf16[32,48,128]{2,1,0:T(8,128)(2,1)S(1)} %all_to_all.26.rows_ref.softs_ref, f32[32,128]{1,0:T(8,128)S(1)} %get-tuple-element.25.own_ref, bf16[8,384,2048]{2,1,0:T(8,128)(2,1)S(1)} %get-tuple-element.24.refs_4_.e.refs_7_), custom_call_target="tpu_custom_call" | custom-call | tf_op jit(solution)/shard_map/column_pass/pallas_call | solution.py:406
  115.8 1.0 collective-permute-start.19
  116.8 0.9 collective-permute-start.18
  117.7 0.6 collective-permute-start.17
  118.2 1.6 collective-permute-done.19.refs_3_
  119.8 1.5 collective-permute-done.17.refs_1_
  121.4 8.0 %closing_pass.1 = (bf16[8,256,384]{2,1,0:T(8,128)(2,1)S(1)}, bf16[32,32,128]{2,1,0:T(8,128)(2,1)S(1)}) custom-call(bf16[8,384,256]{2,1,0:T(8,128)(2,1)S(1)} %get-tuple-element.21.u.refs_4_, bf16[256,2048]{1,0:T(8,128)(2,1)S(1)} %get-tuple-element.22.w.refs_6_, f32[1,2048]{1,0:T(1,128)S(1)} %column_pass.3.refs_0_, ...), custom_call_target="tpu_custom_call" | custom-call | tf_op jit(solution)/shard_map/closing_pass/pallas_call | solution.py:495
  129.4 14.6 %all_to_all.27.rows_ref = bf16[32,32,128]{2,1,0:T(8,128)(2,1)S(1)} all-to-all(bf16[32,32,128]{2,1,0:T(8,128)(2,1)S(1)} %get-tuple-element.26), channel_id=1, replica_groups=mesh['z'=4,'y'=4,'c'=2,'x'=4] {'z','c','x'}, dimensions={0} | all-to-all | bytes 524288 | tf_op jit(solution)/shard_map/all_to_all | solution.py:619
  144.0 11.3 %grad_pass.1 = (bf16[32,8,2048]{2,1,0:T(8,128)(2,1)S(1)}, f32[3,128]{1,0:T(4,128)}) custom-call(s32[3]{0:T(128)S(1)} %copy-done.2, bf16[32,32,128]{2,1,0:T(8,128)(2,1)S(1)} %all_to_all.27.rows_ref, bf16[32,48,128]{2,1,0:T(8,128)(2,1)S(1)} %all_to_all.26.rows_ref.softs_ref, f32[32,128]{1,0:T(8,128)S(1)} %get-tuple-element.25.own_ref, ...), custom_call_target="tpu_custom_call" | custom-call | tf_op jit(solution)/shard_map/grad_pass/pallas_call | solution.py:573
  155.3 20.1 %all_to_all.28.parts_ref = bf16[32,8,2048]{2,1,0:T(8,128)(2,1)S(1)} all-to-all(bf16[32,8,2048]{2,1,0:T(8,128)(2,1)S(1)} %get-tuple-element.29), channel_id=1, replica_groups=mesh['z'=4,'y'=4,'c'=2,'x'=4] {'z','y','c'}, dimensions={0} | all-to-all | bytes 2097152 | tf_op jit(solution)/shard_map/all_to_all | solution.py:619
  175.4 0.9 sum_pass.1
  (20 shorter events, 0.2 us)
Async XLA Ops:
  2.5 17.1 %all-to-all-start = ((bf16[8,16,2048]{2,1,0:T(8,128)(2,1)}), bf16[8,16,2048]{2,1,0:T(8,128)(2,1)S(1)}, u32[]{:S(2)}, u32[]{:S(2)}) async-start(bf16[8,16,2048]{2,1,0:T(8,128)(2,1)} %weave.1), calls=%async_computation | async-start | bytes 1048576 | tf_op jit(solution)/shard_map/all_to_all | solution.py:619
  15.2 12.8 %collective-permute-start.2 = (bf16[784,256]{1,0:T(8,128)(2,1)}, bf16[784,256]{1,0:T(8,128)(2,1)S(1)}, u32[]{:S(2)}, u32[]{:S(2)}) collective-permute-start(bf16[784,256]{1,0:T(8,128)(2,1)} %get-tuple-element.17.refs_0_), channel_id=1, source_target_pairs={{0,64},{32,96},{64,0},{96,32},{1,65},{33,97},{65,1},{97,33},{2,66}... | collective-permute-start | bytes 1204232 | tf_op jit(solution)/shard_map/ppermute | solution.py:615
  18.2 18.2 %collective-permute-start.1 = (bf16[784,256]{1,0:T(8,128)(2,1)}, bf16[784,256]{1,0:T(8,128)(2,1)S(1)}, u32[]{:S(2)}, u32[]{:S(2)}) collective-permute-start(bf16[784,256]{1,0:T(8,128)(2,1)} %get-tuple-element.17.refs_0_), channel_id=1, source_target_pairs={{0,96},{32,0},{64,32},{96,64},{1,97},{33,1},{65,33},{97,65},{2,98}... | collective-permute-start | bytes 1204232 | tf_op jit(solution)/shard_map/ppermute | solution.py:615
  19.0 17.8 %collective-permute-start = (bf16[784,256]{1,0:T(8,128)(2,1)}, bf16[784,256]{1,0:T(8,128)(2,1)S(1)}, u32[]{:S(2)}, u32[]{:S(2)}) collective-permute-start(bf16[784,256]{1,0:T(8,128)(2,1)} %get-tuple-element.17.refs_0_), channel_id=1, source_target_pairs={{0,32},{32,64},{64,96},{96,0},{1,33},{33,65},{65,97},{97,1},{2,34}... | collective-permute-start | bytes 1204232 | tf_op jit(solution)/shard_map/ppermute | solution.py:615
  19.7 17.1 %collective-permute-start.5 = (bf16[64,2048]{1,0:T(8,128)(2,1)S(1)}, bf16[64,2048]{1,0:T(8,128)(2,1)S(1)}, u32[]{:S(2)}, u32[]{:S(2)}) collective-permute-start(bf16[64,2048]{1,0:T(8,128)(2,1)S(1)} %split_rows.2.refs_2_), channel_id=1, source_target_pairs={{0,16},{8,24},{16,0},{24,8},{1,17},{9,25},{17,1},{25,9},{2,18},{10... | collective-permute-start | bytes 786440 | tf_op jit(solution)/shard_map/ppermute | solution.py:615
  22.6 14.2 %collective-permute-start.4 = (bf16[64,2048]{1,0:T(8,128)(2,1)S(1)}, bf16[64,2048]{1,0:T(8,128)(2,1)S(1)}, u32[]{:S(2)}, u32[]{:S(2)}) collective-permute-start(bf16[64,2048]{1,0:T(8,128)(2,1)S(1)} %split_rows.2.refs_2_), channel_id=1, source_target_pairs={{0,24},{8,0},{16,8},{24,16},{1,25},{9,1},{17,9},{25,17},{2,26},{10... | collective-permute-start | bytes 786440 | tf_op jit(solution)/shard_map/ppermute | solution.py:615
  27.9 8.9 %collective-permute-start.3 = (bf16[64,2048]{1,0:T(8,128)(2,1)S(1)}, bf16[64,2048]{1,0:T(8,128)(2,1)S(1)}, u32[]{:S(2)}, u32[]{:S(2)}) collective-permute-start(bf16[64,2048]{1,0:T(8,128)(2,1)S(1)} %split_rows.2.refs_2_), channel_id=1, source_target_pairs={{0,8},{8,16},{16,24},{24,0},{1,9},{9,17},{17,25},{25,1},{2,10},{10... | collective-permute-start | bytes 786440 | tf_op jit(solution)/shard_map/ppermute | solution.py:615
  36.8 1.0 copy-start
  37.8 0.6 copy-start.1
  38.4 6.1 %copy-start.2 = (s32[3]{0:T(128)S(1)}, s32[3]{0:T(128)}, u32[]{:S(2)}) copy-start(s32[3]{0:T(128)} %get-tuple-element.16.info_ref) | copy-start | bytes 40
  39.1 5.4 %collective-permute-start.6 = (bf16[4,400,256]{2,1,0:T(8,128)(2,1)S(1)}, bf16[4,400,256]{2,1,0:T(8,128)(2,1)S(1)}, u32[]{:S(2)}, u32[]{:S(2)}) collective-permute-start(bf16[4,400,256]{2,1,0:T(8,128)(2,1)S(1)} %get-tuple-element.18.refs_0_), channel_id=1, source_target_pairs={{0,4},{4,0},{1,5},{5,1},{2,6},{6,2},{3,7},{7,3},{8,12},{12,8},{9,1... | collective-permute-start | bytes 2457608 | tf_op jit(solution)/shard_map/ppermute | solution.py:615
  40.3 15.5 %collective-permute-start.10 = (bf16[4,384,256]{2,1,0:T(8,128)(2,1)S(1)}, bf16[4,384,256]{2,1,0:T(8,128)(2,1)S(1)}, u32[]{:S(2)}, u32[]{:S(2)}) collective-permute-start(bf16[4,384,256]{2,1,0:T(8,128)(2,1)S(1)} %get-tuple-element.20.refs_4_), channel_id=1, source_target_pairs={{0,4},{4,0},{1,5},{5,1},{2,6},{6,2},{3,7},{7,3},{8,12},{12,8},{9,1... | collective-permute-start | bytes 2359304 | tf_op jit(solution)/shard_map/ppermute | solution.py:615
  40.4 11.5 %collective-permute-start.9 = (bf16[64,2048]{1,0:T(8,128)(2,1)S(1)}, bf16[64,2048]{1,0:T(8,128)(2,1)S(1)}, u32[]{:S(2)}, u32[]{:S(2)}) collective-permute-start(bf16[64,2048]{1,0:T(8,128)(2,1)S(1)} %split_rows.3.refs_6_.refs_0_), channel_id=1, source_target_pairs={{0,16},{8,24},{16,0},{24,8},{1,17},{9,25},{17,1},{25,9},{2,18},{10... | collective-permute-start | bytes 786440 | tf_op jit(solution)/shard_map/ppermute | solution.py:615
  43.0 12.1 %collective-permute-start.8 = (bf16[64,2048]{1,0:T(8,128)(2,1)S(1)}, bf16[64,2048]{1,0:T(8,128)(2,1)S(1)}, u32[]{:S(2)}, u32[]{:S(2)}) collective-permute-start(bf16[64,2048]{1,0:T(8,128)(2,1)S(1)} %split_rows.3.refs_6_.refs_0_), channel_id=1, source_target_pairs={{0,24},{8,0},{16,8},{24,16},{1,25},{9,1},{17,9},{25,17},{2,26},{10... | collective-permute-start | bytes 786440 | tf_op jit(solution)/shard_map/ppermute | solution.py:615
  43.8 12.0 %collective-permute-start.7 = (bf16[64,2048]{1,0:T(8,128)(2,1)S(1)}, bf16[64,2048]{1,0:T(8,128)(2,1)S(1)}, u32[]{:S(2)}, u32[]{:S(2)}) collective-permute-start(bf16[64,2048]{1,0:T(8,128)(2,1)S(1)} %split_rows.3.refs_6_.refs_0_), channel_id=1, source_target_pairs={{0,8},{8,16},{16,24},{24,0},{1,9},{9,17},{17,25},{25,1},{2,10},{10... | collective-permute-start | bytes 786440 | tf_op jit(solution)/shard_map/ppermute | solution.py:615
  56.6 6.9 %collective-permute-start.13 = (f32[1,2048]{1,0:T(1,128)S(1)}, f32[1,2048]{1,0:T(1,128)S(1)}, u32[]{:S(2)}, u32[]{:S(2)}) collective-permute-start(f32[1,2048]{1,0:T(1,128)S(1)} %get-tuple-element.23.refs_0_), channel_id=1, source_target_pairs={{0,16},{8,24},{16,0},{24,8},{1,17},{9,25},{17,1},{25,9},{2,18},{10... | collective-permute-start | bytes 24584 | tf_op jit(solution)/shard_map/ppermute | solution.py:615
  59.2 4.3 %collective-permute-start.12 = (f32[1,2048]{1,0:T(1,128)S(1)}, f32[1,2048]{1,0:T(1,128)S(1)}, u32[]{:S(2)}, u32[]{:S(2)}) collective-permute-start(f32[1,2048]{1,0:T(1,128)S(1)} %get-tuple-element.23.refs_0_), channel_id=1, source_target_pairs={{0,24},{8,0},{16,8},{24,16},{1,25},{9,1},{17,9},{25,17},{2,26},{10... | collective-permute-start | bytes 24584 | tf_op jit(solution)/shard_map/ppermute | solution.py:615
  60.0 3.7 %collective-permute-start.11 = (f32[1,2048]{1,0:T(1,128)S(1)}, f32[1,2048]{1,0:T(1,128)S(1)}, u32[]{:S(2)}, u32[]{:S(2)}) collective-permute-start(f32[1,2048]{1,0:T(1,128)S(1)} %get-tuple-element.23.refs_0_), channel_id=1, source_target_pairs={{0,8},{8,16},{16,24},{24,0},{1,9},{9,17},{17,25},{25,1},{2,10},{10... | collective-permute-start | bytes 24584 | tf_op jit(solution)/shard_map/ppermute | solution.py:615
  88.0 4.6 %collective-permute-start.16 = (f32[1,2048]{1,0:T(1,128)S(1)}, f32[1,2048]{1,0:T(1,128)S(1)}, u32[]{:S(2)}, u32[]{:S(2)}) collective-permute-start(f32[1,2048]{1,0:T(1,128)S(1)} %column_pass.2.refs_0_), channel_id=1, source_target_pairs={{0,16},{8,24},{16,0},{24,8},{1,17},{9,25},{17,1},{25,9},{2,18},{10... | collective-permute-start | bytes 24584 | tf_op jit(solution)/shard_map/ppermute | solution.py:615
  88.1 4.5 %collective-permute-start.15 = (f32[1,2048]{1,0:T(1,128)S(1)}, f32[1,2048]{1,0:T(1,128)S(1)}, u32[]{:S(2)}, u32[]{:S(2)}) collective-permute-start(f32[1,2048]{1,0:T(1,128)S(1)} %column_pass.2.refs_0_), channel_id=1, source_target_pairs={{0,24},{8,0},{16,8},{24,16},{1,25},{9,1},{17,9},{25,17},{2,26},{10... | collective-permute-start | bytes 24584 | tf_op jit(solution)/shard_map/ppermute | solution.py:615
  89.8 3.7 %collective-permute-start.14 = (f32[1,2048]{1,0:T(1,128)S(1)}, f32[1,2048]{1,0:T(1,128)S(1)}, u32[]{:S(2)}, u32[]{:S(2)}) collective-permute-start(f32[1,2048]{1,0:T(1,128)S(1)} %column_pass.2.refs_0_), channel_id=1, source_target_pairs={{0,8},{8,16},{16,24},{24,0},{1,9},{9,17},{17,25},{25,1},{2,10},{10... | collective-permute-start | bytes 24584 | tf_op jit(solution)/shard_map/ppermute | solution.py:615
  115.8 4.1 %collective-permute-start.19 = (f32[1,2048]{1,0:T(1,128)S(1)}, f32[1,2048]{1,0:T(1,128)S(1)}, u32[]{:S(2)}, u32[]{:S(2)}) collective-permute-start(f32[1,2048]{1,0:T(1,128)S(1)} %column_pass.3.refs_0_), channel_id=1, source_target_pairs={{0,16},{8,24},{16,0},{24,8},{1,17},{9,25},{17,1},{25,9},{2,18},{10... | collective-permute-start | bytes 24584 | tf_op jit(solution)/shard_map/ppermute | solution.py:615
  116.8 3.1 %collective-permute-start.18 = (f32[1,2048]{1,0:T(1,128)S(1)}, f32[1,2048]{1,0:T(1,128)S(1)}, u32[]{:S(2)}, u32[]{:S(2)}) collective-permute-start(f32[1,2048]{1,0:T(1,128)S(1)} %column_pass.3.refs_0_), channel_id=1, source_target_pairs={{0,24},{8,0},{16,8},{24,16},{1,25},{9,1},{17,9},{25,17},{2,26},{10... | collective-permute-start | bytes 24584 | tf_op jit(solution)/shard_map/ppermute | solution.py:615
  117.7 3.7 %collective-permute-start.17 = (f32[1,2048]{1,0:T(1,128)S(1)}, f32[1,2048]{1,0:T(1,128)S(1)}, u32[]{:S(2)}, u32[]{:S(2)}) collective-permute-start(f32[1,2048]{1,0:T(1,128)S(1)} %column_pass.3.refs_0_), channel_id=1, source_target_pairs={{0,8},{8,16},{16,24},{24,0},{1,9},{9,17},{17,25},{25,1},{2,10},{10... | collective-permute-start | bytes 24584 | tf_op jit(solution)/shard_map/ppermute | solution.py:615

commit v6 on v5

--- a/solution.py
+++ b/solution.py
@@ -22,7 +22,7 @@
 SHIFTS = (1, 3, 2)
 SIDE = 4
 DP = ("z", "y", "c")
-GROUP = ("z", "c", "x")
+GROUP = ("x", "z", "c")
 
 teacher_temp = 0.07
 student_temp = 0.1
@@ -485,7 +485,7 @@
     lax.fori_loop(0, blocks, step, 0)
     at = PER * blocks
     for i in range(out_ref.shape[0]):
-        rows[at : at + PER, :] = crosses[i // 4, 0:PER, :]
+        rows[at : at + PER, :] = crosses[i % 8, 0:PER, :]
         out_ref[i] = rows[...].astype(bf16)
 
 

time: 177 us -> 176 us (level)
  no operation moved by 1% of the time
where the time goes in v6:
time: 176 us
  blocking collectives  67.6 us (38%)
  Pallas kernels  54.5 us (31%)
  starting transfers between devices  30.1 us (17%)
  waiting for transfers between devices  20.3 us (12%)
    all_to_all x4, blocking collectives, exchange(): return lax.all_to_all(value, axes, 0, 0, tiled=True)  67.6 us
    ppermute x20, starting transfers between devices, shift(): return lax.ppermute(value, axis, [(i, (i + k) % n) for i in range(n)])  23.3 us
    ppermute x20, waiting for transfers between devices, shift(): return lax.ppermute(value, axis, [(i, (i + k) % n) for i in range(n)])  20.3 us
    pallas_call x1, Pallas kernels, grad_pass(): pl.pallas_call(functools.partial(grad_kernel, float(images)), out_shape=(...  11.3 us
    pallas_call x1, Pallas kernels, closing_pass(): pl.pallas_call(closing_kernel, out_shape=(pltpu.VMEM((blocks, d, slots),...  8.02 us
    pallas_call x1, Pallas kernels, energy_pass(): pl.pallas_call(energy_kernel, out_shape=(pltpu.VMEM((blocks, slots, cols)...  7.38 us
    all_to_all x1, starting transfers between devices, exchange(): return lax.all_to_all(value, axes, 0, 0, tiled=True)  6.83 us
    pallas_call x2, Pallas kernels, column_pass(): pl.pallas_call(column_kernel, out_shape=shape((1, cols)), in_specs=[VM, V...  6.68 us
  transfers between devices with their start and end apart: 21, of which 9 were waited for; matrix products, arithmetic and copies ran while one was open for 0% of the time, Pallas kernels for 10%

profile of v6, /device:TPU:1, one launch (start us, length us, event | category | flops | bytes accessed | tf_op | source)
XLA Modules:
  0.0 175.6 jit_solution(8665016592663860247)
XLA Ops:
  0.6 1.9 %weave.1 = bf16[8,16,2048]{2,1,0:T(8,128)(2,1)} custom-call(bf16[8,16384]{1,0:T(8,128)(2,1)} %tp_ref.1, bf16[8,16384]{1,0:T(8,128)(2,1)} %sp_ref.1), custom_call_target="tpu_custom_call" | custom-call | tf_op jit(solution)/shard_map/weave/pallas_call | solution.py:141
  2.5 6.8 %all-to-all-start = ((bf16[8,16,2048]{2,1,0:T(8,128)(2,1)}), bf16[8,16,2048]{2,1,0:T(8,128)(2,1)S(1)}, u32[]{:S(2)}, u32[]{:S(2)}) async-start(bf16[8,16,2048]{2,1,0:T(8,128)(2,1)} %weave.1), calls=%async_computation | async-start | bytes 1048576 | tf_op jit(solution)/shard_map/all_to_all | solution.py:619
  10.0 5.2 %token_rows.1 = (bf16[784,256]{1,0:T(8,128)(2,1)}, s32[3]{0:T(128)}) custom-call(s32[1]{0:T(128)} %bitcast.me_ref, s32[1]{0:T(128)S(6)} %copy.8.count_ref, s32[384]{0:T(512)} %index_ref.1, bf16[2048,256]{1,0:T(8,128)(2,1)} %teacher_ref.1, bf16[2048,256]{1,0:T(8,128)(2,1)} %student_ref.1), custom_call_target="tpu_custom_call" | custom-call | tf_op jit(solution)/shard_map/token_rows/pallas_call | solution.py:107
  15.2 3.0 %collective-permute-start.2 = (bf16[784,256]{1,0:T(8,128)(2,1)}, bf16[784,256]{1,0:T(8,128)(2,1)S(1)}, u32[]{:S(2)}, u32[]{:S(2)}) collective-permute-start(bf16[784,256]{1,0:T(8,128)(2,1)} %get-tuple-element.17.refs_0_), channel_id=1, source_target_pairs={{0,64},{32,96},{64,0},{96,32},{1,65},{33,97},{65,1},{97,33},{2,66}... | collective-permute-start | bytes 1204232 | tf_op jit(solution)/shard_map/ppermute | solution.py:615
  18.2 0.9 collective-permute-start.1
  19.0 0.6 collective-permute-start
  19.7 3.0 %collective-permute-start.5 = (bf16[64,2048]{1,0:T(8,128)(2,1)S(1)}, bf16[64,2048]{1,0:T(8,128)(2,1)S(1)}, u32[]{:S(2)}, u32[]{:S(2)}) collective-permute-start(bf16[64,2048]{1,0:T(8,128)(2,1)S(1)} %split_rows.2.refs_2_), channel_id=1, source_target_pairs={{0,16},{8,24},{16,0},{24,8},{1,17},{9,25},{17,1},{25,9},{2,18},{10... | collective-permute-start | bytes 786440 | tf_op jit(solution)/shard_map/ppermute | solution.py:615
  22.6 0.8 collective-permute-start.4
  23.4 4.5 %collective-permute-done.2.refs_3_ = bf16[784,256]{1,0:T(8,128)(2,1)S(1)} collective-permute-done((bf16[784,256]{1,0:T(8,128)(2,1)}, bf16[784,256]{1,0:T(8,128)(2,1)S(1)}, u32[]{:S(2)}, u32[]{:S(2)}) %collective-permute-start.2) | collective-permute-done | bytes 401440 | tf_op jit(solution)/shard_map/ppermute | solution.py:615
  27.9 1.3 collective-permute-start.3
  29.2 7.1 %collective-permute-done.1.refs_2_ = bf16[784,256]{1,0:T(8,128)(2,1)S(1)} collective-permute-done((bf16[784,256]{1,0:T(8,128)(2,1)}, bf16[784,256]{1,0:T(8,128)(2,1)S(1)}, u32[]{:S(2)}, u32[]{:S(2)}) %collective-permute-start.1) | collective-permute-done | bytes 401440 | tf_op jit(solution)/shard_map/ppermute | solution.py:615
  36.3 0.4 collective-permute-done.refs_1_
  36.8 1.0 copy-done
  37.8 0.6 copy-done.1
  38.4 0.6 stack.1
  39.1 1.2 collective-permute-start.6
  40.4 2.6 %collective-permute-start.9 = (bf16[64,2048]{1,0:T(8,128)(2,1)S(1)}, bf16[64,2048]{1,0:T(8,128)(2,1)S(1)}, u32[]{:S(2)}, u32[]{:S(2)}) collective-permute-start(bf16[64,2048]{1,0:T(8,128)(2,1)S(1)} %split_rows.3.refs_6_.refs_0_), channel_id=1, source_target_pairs={{0,16},{8,24},{16,0},{24,8},{1,17},{9,25},{17,1},{25,9},{2,18},{10... | collective-permute-start | bytes 786440 | tf_op jit(solution)/shard_map/ppermute | solution.py:615
  43.0 0.8 collective-permute-start.8
  43.8 0.7 collective-permute-start.7
  44.5 7.4 %energy_pass.1 = (bf16[8,384,2048]{2,1,0:T(8,128)(2,1)S(1)}, f32[32,128]{1,0:T(8,128)S(1)}, f32[1,2048]{1,0:T(1,128)S(1)}) custom-call(s32[3]{0:T(128)S(1)} %copy-done.2, bf16[4,400,256]{2,1,0:T(8,128)(2,1)S(1)} %get-tuple-element.18.refs_0_, bf16[4,400,256]{2,1,0:T(8,128)(2,1)S(1)} %collective-permute-done.6.refs_1_, ...), custom_call_target="tpu_custom_call" | custom-call | flops 3221225472 | bytes 12582912 | tf_op jit(solution)/shard_map/energy_pass/pallas_call | solution.py:294
  51.9 3.2 %collective-permute-done.8.refs_2_ = bf16[64,2048]{1,0:T(8,128)(2,1)S(1)} collective-permute-done((bf16[64,2048]{1,0:T(8,128)(2,1)S(1)}, bf16[64,2048]{1,0:T(8,128)(2,1)S(1)}, u32[]{:S(2)}, u32[]{:S(2)}) %collective-permute-start.8) | collective-permute-done | bytes 262176 | tf_op jit(solution)/shard_map/ppermute | solution.py:615
  55.1 0.8 collective-permute-done.7.refs_1_
  55.9 0.7 collect.1
  56.6 2.6 %collective-permute-start.13 = (f32[1,2048]{1,0:T(1,128)S(1)}, f32[1,2048]{1,0:T(1,128)S(1)}, u32[]{:S(2)}, u32[]{:S(2)}) collective-permute-start(f32[1,2048]{1,0:T(1,128)S(1)} %get-tuple-element.23.refs_0_), channel_id=1, source_target_pairs={{0,16},{8,24},{16,0},{24,8},{1,17},{9,25},{17,1},{25,9},{2,18},{10... | collective-permute-start | bytes 24584 | tf_op jit(solution)/shard_map/ppermute | solution.py:615
  59.2 0.8 collective-permute-start.12
  60.0 0.7 collective-permute-start.11
  60.7 2.8 %softmax_pass.2.refs_5_ = f32[12,128]{1,0:T(8,128)S(1)} custom-call(bf16[8,384,256]{2,1,0:T(8,128)(2,1)S(1)} %get-tuple-element.21.u.refs_4_, bf16[256,2048]{1,0:T(8,128)(2,1)S(1)} %get-tuple-element.22.w.refs_6_), custom_call_target="tpu_custom_call" | custom-call | flops 1610612736 | bytes 393216 | tf_op jit(solution)/shard_map/softmax_pass/pallas_call | solution.py:445
  63.5 0.2 collective-permute-done.11.refs_1_
  63.7 3.1 %row_pass.2 = bf16[32,32,128]{2,1,0:T(8,128)(2,1)S(1)} custom-call(f32[1,2048]{1,0:T(1,128)S(1)} %get-tuple-element.23.refs_0_, f32[1,2048]{1,0:T(1,128)S(1)} %collective-permute-done.11.refs_1_, f32[1,2048]{1,0:T(1,128)S(1)} %collective-permute-done.12.refs_2_, f32[1,2048]{1,0:T(1,128)S(1)} %collective-permute-done.13.refs_3_, ...), custom_call_target="tpu_custom_call" | custom-call | tf_op jit(solution)/shard_map/row_pass/pallas_call | solution.py:373
  66.8 17.9 %all_to_all.25.rows_ref = bf16[32,32,128]{2,1,0:T(8,128)(2,1)S(1)} all-to-all(bf16[32,32,128]{2,1,0:T(8,128)(2,1)S(1)} %row_pass.2), channel_id=1, replica_groups=mesh['z'=4,'y'=4,'c'=2,'x'=4] {'x','z','c'}, dimensions={0} | all-to-all | bytes 524288 | tf_op jit(solution)/shard_map/all_to_all | solution.py:619
  84.7 3.3 %column_pass.2.refs_0_ = f32[1,2048]{1,0:T(1,128)S(1)} custom-call(bf16[32,32,128]{2,1,0:T(8,128)(2,1)S(1)} %all_to_all.25.rows_ref, f32[32,128]{1,0:T(8,128)S(1)} %get-tuple-element.25.own_ref, bf16[8,384,2048]{2,1,0:T(8,128)(2,1)S(1)} %get-tuple-element.24.refs_4_.e.refs_7_), custom_call_target="tpu_custom_call" | custom-call | tf_op jit(solution)/shard_map/column_pass/pallas_call | solution.py:406
  88.1 0.1 collective-permute-start.16
  88.2 1.7 collective-permute-start.15
  89.9 2.8 %softmax_pass.3.refs_6_ = f32[12,128]{1,0:T(8,128)S(1)} custom-call(bf16[8,384,256]{2,1,0:T(8,128)(2,1)S(1)} %get-tuple-element.21.u.refs_4_, bf16[256,2048]{1,0:T(8,128)(2,1)S(1)} %get-tuple-element.22.w.refs_6_), custom_call_target="tpu_custom_call" | custom-call | flops 1610612736 | bytes 393216 | tf_op jit(solution)/shard_map/softmax_pass/pallas_call | solution.py:445
  92.7 0.9 collective-permute-done.14.refs_1_
  93.6 3.1 %row_pass.3 = bf16[32,48,128]{2,1,0:T(8,128)(2,1)S(1)} custom-call(f32[1,2048]{1,0:T(1,128)S(1)} %column_pass.2.refs_0_, f32[1,2048]{1,0:T(1,128)S(1)} %collective-permute-done.14.refs_1_, f32[1,2048]{1,0:T(1,128)S(1)} %collective-permute-done.15.refs_2_, f32[1,2048]{1,0:T(1,128)S(1)} %collective-permute-done.16.refs_3_, ...), custom_call_target="tpu_custom_call" | custom-call | tf_op jit(solution)/shard_map/row_pass/pallas_call | solution.py:373
  96.7 15.5 %all_to_all.26.rows_ref.softs_ref = bf16[32,48,128]{2,1,0:T(8,128)(2,1)S(1)} all-to-all(bf16[32,48,128]{2,1,0:T(8,128)(2,1)S(1)} %row_pass.3), channel_id=1, replica_groups=mesh['z'=4,'y'=4,'c'=2,'x'=4] {'x','z','c'}, dimensions={0} | all-to-all | bytes 786432 | tf_op jit(solution)/shard_map/all_to_all | solution.py:619
  112.2 3.3 %column_pass.3.refs_0_ = f32[1,2048]{1,0:T(1,128)S(1)} custom-call(bf16[32,48,128]{2,1,0:T(8,128)(2,1)S(1)} %all_to_all.26.rows_ref.softs_ref, f32[32,128]{1,0:T(8,128)S(1)} %get-tuple-element.25.own_ref, bf16[8,384,2048]{2,1,0:T(8,128)(2,1)S(1)} %get-tuple-element.24.refs_4_.e.refs_7_), custom_call_target="tpu_custom_call" | custom-call | tf_op jit(solution)/shard_map/column_pass/pallas_call | solution.py:406
  115.5 1.0 collective-permute-start.19
  116.6 0.9 collective-permute-start.18
  117.5 0.6 collective-permute-start.17
  118.0 1.6 collective-permute-done.19.refs_3_
  119.6 1.5 collective-permute-done.17.refs_1_
  121.2 8.0 %closing_pass.1 = (bf16[8,256,384]{2,1,0:T(8,128)(2,1)S(1)}, bf16[32,32,128]{2,1,0:T(8,128)(2,1)S(1)}) custom-call(bf16[8,384,256]{2,1,0:T(8,128)(2,1)S(1)} %get-tuple-element.21.u.refs_4_, bf16[256,2048]{1,0:T(8,128)(2,1)S(1)} %get-tuple-element.22.w.refs_6_, f32[1,2048]{1,0:T(1,128)S(1)} %column_pass.3.refs_0_, ...), custom_call_target="tpu_custom_call" | custom-call | tf_op jit(solution)/shard_map/closing_pass/pallas_call | solution.py:495
  129.2 14.0 %all_to_all.27.rows_ref = bf16[32,32,128]{2,1,0:T(8,128)(2,1)S(1)} all-to-all(bf16[32,32,128]{2,1,0:T(8,128)(2,1)S(1)} %get-tuple-element.26), channel_id=1, replica_groups=mesh['z'=4,'y'=4,'c'=2,'x'=4] {'x','z','c'}, dimensions={0} | all-to-all | bytes 524288 | tf_op jit(solution)/shard_map/all_to_all | solution.py:619
  143.2 11.3 %grad_pass.1 = (bf16[32,8,2048]{2,1,0:T(8,128)(2,1)S(1)}, f32[3,128]{1,0:T(4,128)}) custom-call(s32[3]{0:T(128)S(1)} %copy-done.2, bf16[32,32,128]{2,1,0:T(8,128)(2,1)S(1)} %all_to_all.27.rows_ref, bf16[32,48,128]{2,1,0:T(8,128)(2,1)S(1)} %all_to_all.26.rows_ref.softs_ref, f32[32,128]{1,0:T(8,128)S(1)} %get-tuple-element.25.own_ref, ...), custom_call_target="tpu_custom_call" | custom-call | tf_op jit(solution)/shard_map/grad_pass/pallas_call | solution.py:573
  154.6 20.1 %all_to_all.28.parts_ref = bf16[32,8,2048]{2,1,0:T(8,128)(2,1)S(1)} all-to-all(bf16[32,8,2048]{2,1,0:T(8,128)(2,1)S(1)} %get-tuple-element.29), channel_id=1, replica_groups=mesh['z'=4,'y'=4,'c'=2,'x'=4] {'z','y','c'}, dimensions={0} | all-to-all | bytes 2097152 | tf_op jit(solution)/shard_map/all_to_all | solution.py:619
  174.7 0.9 sum_pass.1
  (20 shorter events, 0.2 us)
Async XLA Ops:
  2.5 17.1 %all-to-all-start = ((bf16[8,16,2048]{2,1,0:T(8,128)(2,1)}), bf16[8,16,2048]{2,1,0:T(8,128)(2,1)S(1)}, u32[]{:S(2)}, u32[]{:S(2)}) async-start(bf16[8,16,2048]{2,1,0:T(8,128)(2,1)} %weave.1), calls=%async_computation | async-start | bytes 1048576 | tf_op jit(solution)/shard_map/all_to_all | solution.py:619
  15.2 12.8 %collective-permute-start.2 = (bf16[784,256]{1,0:T(8,128)(2,1)}, bf16[784,256]{1,0:T(8,128)(2,1)S(1)}, u32[]{:S(2)}, u32[]{:S(2)}) collective-permute-start(bf16[784,256]{1,0:T(8,128)(2,1)} %get-tuple-element.17.refs_0_), channel_id=1, source_target_pairs={{0,64},{32,96},{64,0},{96,32},{1,65},{33,97},{65,1},{97,33},{2,66}... | collective-permute-start | bytes 1204232 | tf_op jit(solution)/shard_map/ppermute | solution.py:615
  18.2 18.2 %collective-permute-start.1 = (bf16[784,256]{1,0:T(8,128)(2,1)}, bf16[784,256]{1,0:T(8,128)(2,1)S(1)}, u32[]{:S(2)}, u32[]{:S(2)}) collective-permute-start(bf16[784,256]{1,0:T(8,128)(2,1)} %get-tuple-element.17.refs_0_), channel_id=1, source_target_pairs={{0,96},{32,0},{64,32},{96,64},{1,97},{33,1},{65,33},{97,65},{2,98}... | collective-permute-start | bytes 1204232 | tf_op jit(solution)/shard_map/ppermute | solution.py:615
  19.0 17.8 %collective-permute-start = (bf16[784,256]{1,0:T(8,128)(2,1)}, bf16[784,256]{1,0:T(8,128)(2,1)S(1)}, u32[]{:S(2)}, u32[]{:S(2)}) collective-permute-start(bf16[784,256]{1,0:T(8,128)(2,1)} %get-tuple-element.17.refs_0_), channel_id=1, source_target_pairs={{0,32},{32,64},{64,96},{96,0},{1,33},{33,65},{65,97},{97,1},{2,34}... | collective-permute-start | bytes 1204232 | tf_op jit(solution)/shard_map/ppermute | solution.py:615
  19.7 17.1 %collective-permute-start.5 = (bf16[64,2048]{1,0:T(8,128)(2,1)S(1)}, bf16[64,2048]{1,0:T(8,128)(2,1)S(1)}, u32[]{:S(2)}, u32[]{:S(2)}) collective-permute-start(bf16[64,2048]{1,0:T(8,128)(2,1)S(1)} %split_rows.2.refs_2_), channel_id=1, source_target_pairs={{0,16},{8,24},{16,0},{24,8},{1,17},{9,25},{17,1},{25,9},{2,18},{10... | collective-permute-start | bytes 786440 | tf_op jit(solution)/shard_map/ppermute | solution.py:615
  22.6 14.2 %collective-permute-start.4 = (bf16[64,2048]{1,0:T(8,128)(2,1)S(1)}, bf16[64,2048]{1,0:T(8,128)(2,1)S(1)}, u32[]{:S(2)}, u32[]{:S(2)}) collective-permute-start(bf16[64,2048]{1,0:T(8,128)(2,1)S(1)} %split_rows.2.refs_2_), channel_id=1, source_target_pairs={{0,24},{8,0},{16,8},{24,16},{1,25},{9,1},{17,9},{25,17},{2,26},{10... | collective-permute-start | bytes 786440 | tf_op jit(solution)/shard_map/ppermute | solution.py:615
  27.9 8.9 %collective-permute-start.3 = (bf16[64,2048]{1,0:T(8,128)(2,1)S(1)}, bf16[64,2048]{1,0:T(8,128)(2,1)S(1)}, u32[]{:S(2)}, u32[]{:S(2)}) collective-permute-start(bf16[64,2048]{1,0:T(8,128)(2,1)S(1)} %split_rows.2.refs_2_), channel_id=1, source_target_pairs={{0,8},{8,16},{16,24},{24,0},{1,9},{9,17},{17,25},{25,1},{2,10},{10... | collective-permute-start | bytes 786440 | tf_op jit(solution)/shard_map/ppermute | solution.py:615
  36.8 1.0 copy-start
  37.8 0.6 copy-start.1
  38.4 6.1 %copy-start.2 = (s32[3]{0:T(128)S(1)}, s32[3]{0:T(128)}, u32[]{:S(2)}) copy-start(s32[3]{0:T(128)} %get-tuple-element.16.info_ref) | copy-start | bytes 40
  39.1 5.4 %collective-permute-start.6 = (bf16[4,400,256]{2,1,0:T(8,128)(2,1)S(1)}, bf16[4,400,256]{2,1,0:T(8,128)(2,1)S(1)}, u32[]{:S(2)}, u32[]{:S(2)}) collective-permute-start(bf16[4,400,256]{2,1,0:T(8,128)(2,1)S(1)} %get-tuple-element.18.refs_0_), channel_id=1, source_target_pairs={{0,4},{4,0},{1,5},{5,1},{2,6},{6,2},{3,7},{7,3},{8,12},{12,8},{9,1... | collective-permute-start | bytes 2457608 | tf_op jit(solution)/shard_map/ppermute | solution.py:615
  40.3 15.5 %collective-permute-start.10 = (bf16[4,384,256]{2,1,0:T(8,128)(2,1)S(1)}, bf16[4,384,256]{2,1,0:T(8,128)(2,1)S(1)}, u32[]{:S(2)}, u32[]{:S(2)}) collective-permute-start(bf16[4,384,256]{2,1,0:T(8,128)(2,1)S(1)} %get-tuple-element.20.refs_4_), channel_id=1, source_target_pairs={{0,4},{4,0},{1,5},{5,1},{2,6},{6,2},{3,7},{7,3},{8,12},{12,8},{9,1... | collective-permute-start | bytes 2359304 | tf_op jit(solution)/shard_map/ppermute | solution.py:615
  40.4 11.5 %collective-permute-start.9 = (bf16[64,2048]{1,0:T(8,128)(2,1)S(1)}, bf16[64,2048]{1,0:T(8,128)(2,1)S(1)}, u32[]{:S(2)}, u32[]{:S(2)}) collective-permute-start(bf16[64,2048]{1,0:T(8,128)(2,1)S(1)} %split_rows.3.refs_6_.refs_0_), channel_id=1, source_target_pairs={{0,16},{8,24},{16,0},{24,8},{1,17},{9,25},{17,1},{25,9},{2,18},{10... | collective-permute-start | bytes 786440 | tf_op jit(solution)/shard_map/ppermute | solution.py:615
  43.0 12.1 %collective-permute-start.8 = (bf16[64,2048]{1,0:T(8,128)(2,1)S(1)}, bf16[64,2048]{1,0:T(8,128)(2,1)S(1)}, u32[]{:S(2)}, u32[]{:S(2)}) collective-permute-start(bf16[64,2048]{1,0:T(8,128)(2,1)S(1)} %split_rows.3.refs_6_.refs_0_), channel_id=1, source_target_pairs={{0,24},{8,0},{16,8},{24,16},{1,25},{9,1},{17,9},{25,17},{2,26},{10... | collective-permute-start | bytes 786440 | tf_op jit(solution)/shard_map/ppermute | solution.py:615
  43.8 12.0 %collective-permute-start.7 = (bf16[64,2048]{1,0:T(8,128)(2,1)S(1)}, bf16[64,2048]{1,0:T(8,128)(2,1)S(1)}, u32[]{:S(2)}, u32[]{:S(2)}) collective-permute-start(bf16[64,2048]{1,0:T(8,128)(2,1)S(1)} %split_rows.3.refs_6_.refs_0_), channel_id=1, source_target_pairs={{0,8},{8,16},{16,24},{24,0},{1,9},{9,17},{17,25},{25,1},{2,10},{10... | collective-permute-start | bytes 786440 | tf_op jit(solution)/shard_map/ppermute | solution.py:615
  56.6 6.9 %collective-permute-start.13 = (f32[1,2048]{1,0:T(1,128)S(1)}, f32[1,2048]{1,0:T(1,128)S(1)}, u32[]{:S(2)}, u32[]{:S(2)}) collective-permute-start(f32[1,2048]{1,0:T(1,128)S(1)} %get-tuple-element.23.refs_0_), channel_id=1, source_target_pairs={{0,16},{8,24},{16,0},{24,8},{1,17},{9,25},{17,1},{25,9},{2,18},{10... | collective-permute-start | bytes 24584 | tf_op jit(solution)/shard_map/ppermute | solution.py:615
  59.2 4.3 %collective-permute-start.12 = (f32[1,2048]{1,0:T(1,128)S(1)}, f32[1,2048]{1,0:T(1,128)S(1)}, u32[]{:S(2)}, u32[]{:S(2)}) collective-permute-start(f32[1,2048]{1,0:T(1,128)S(1)} %get-tuple-element.23.refs_0_), channel_id=1, source_target_pairs={{0,24},{8,0},{16,8},{24,16},{1,25},{9,1},{17,9},{25,17},{2,26},{10... | collective-permute-start | bytes 24584 | tf_op jit(solution)/shard_map/ppermute | solution.py:615
  60.0 3.7 %collective-permute-start.11 = (f32[1,2048]{1,0:T(1,128)S(1)}, f32[1,2048]{1,0:T(1,128)S(1)}, u32[]{:S(2)}, u32[]{:S(2)}) collective-permute-start(f32[1,2048]{1,0:T(1,128)S(1)} %get-tuple-element.23.refs_0_), channel_id=1, source_target_pairs={{0,8},{8,16},{16,24},{24,0},{1,9},{9,17},{17,25},{25,1},{2,10},{10... | collective-permute-start | bytes 24584 | tf_op jit(solution)/shard_map/ppermute | solution.py:615
  88.1 4.6 %collective-permute-start.16 = (f32[1,2048]{1,0:T(1,128)S(1)}, f32[1,2048]{1,0:T(1,128)S(1)}, u32[]{:S(2)}, u32[]{:S(2)}) collective-permute-start(f32[1,2048]{1,0:T(1,128)S(1)} %column_pass.2.refs_0_), channel_id=1, source_target_pairs={{0,16},{8,24},{16,0},{24,8},{1,17},{9,25},{17,1},{25,9},{2,18},{10... | collective-permute-start | bytes 24584 | tf_op jit(solution)/shard_map/ppermute | solution.py:615
  88.2 4.5 %collective-permute-start.15 = (f32[1,2048]{1,0:T(1,128)S(1)}, f32[1,2048]{1,0:T(1,128)S(1)}, u32[]{:S(2)}, u32[]{:S(2)}) collective-permute-start(f32[1,2048]{1,0:T(1,128)S(1)} %column_pass.2.refs_0_), channel_id=1, source_target_pairs={{0,24},{8,0},{16,8},{24,16},{1,25},{9,1},{17,9},{25,17},{2,26},{10... | collective-permute-start | bytes 24584 | tf_op jit(solution)/shard_map/ppermute | solution.py:615
  89.9 3.7 %collective-permute-start.14 = (f32[1,2048]{1,0:T(1,128)S(1)}, f32[1,2048]{1,0:T(1,128)S(1)}, u32[]{:S(2)}, u32[]{:S(2)}) collective-permute-start(f32[1,2048]{1,0:T(1,128)S(1)} %column_pass.2.refs_0_), channel_id=1, source_target_pairs={{0,8},{8,16},{16,24},{24,0},{1,9},{9,17},{17,25},{25,1},{2,10},{10... | collective-permute-start | bytes 24584 | tf_op jit(solution)/shard_map/ppermute | solution.py:615
  115.5 4.1 %collective-permute-start.19 = (f32[1,2048]{1,0:T(1,128)S(1)}, f32[1,2048]{1,0:T(1,128)S(1)}, u32[]{:S(2)}, u32[]{:S(2)}) collective-permute-start(f32[1,2048]{1,0:T(1,128)S(1)} %column_pass.3.refs_0_), channel_id=1, source_target_pairs={{0,16},{8,24},{16,0},{24,8},{1,17},{9,25},{17,1},{25,9},{2,18},{10... | collective-permute-start | bytes 24584 | tf_op jit(solution)/shard_map/ppermute | solution.py:615
  116.6 3.1 %collective-permute-start.18 = (f32[1,2048]{1,0:T(1,128)S(1)}, f32[1,2048]{1,0:T(1,128)S(1)}, u32[]{:S(2)}, u32[]{:S(2)}) collective-permute-start(f32[1,2048]{1,0:T(1,128)S(1)} %column_pass.3.refs_0_), channel_id=1, source_target_pairs={{0,24},{8,0},{16,8},{24,16},{1,25},{9,1},{17,9},{25,17},{2,26},{10... | collective-permute-start | bytes 24584 | tf_op jit(solution)/shard_map/ppermute | solution.py:615
  117.5 3.7 %collective-permute-start.17 = (f32[1,2048]{1,0:T(1,128)S(1)}, f32[1,2048]{1,0:T(1,128)S(1)}, u32[]{:S(2)}, u32[]{:S(2)}) collective-permute-start(f32[1,2048]{1,0:T(1,128)S(1)} %column_pass.3.refs_0_), channel_id=1, source_target_pairs={{0,8},{8,16},{16,24},{24,0},{1,9},{9,17},{17,25},{25,1},{2,10},{10... | collective-permute-start | bytes 24584 | tf_op jit(solution)/shard_map/ppermute | solution.py:615
